TPU v7x, 32 devices: a whole 2x2x4 slice. The times are simulated.
32 devices in a mesh: gx: 2 (over y), gz: 4 (over z), gy: 4 (over x, core).
Axes of the slice: x: 2, y: 2, z: 4, core: 2. Of those that a mesh axis runs over, the one named last changes fastest.
Arguments:
- spectral: float32 [2, 128, 32, 2048], P(None, 'gz', 'gy', 'gx'), may hold values from -6 to 6
- shifts: int32 [128, 32], P('gz', 'gy'), may hold values from 0 to 2047
- colour: int32 [32, 2048], P('gy', 'gx'), may hold values 0 or 1
- pressure: float32 [128, 32, 2048], P('gz', 'gy', 'gx'), may hold values from -5 to 7
- source: float32 [128, 32, 2048], P('gz', 'gy', 'gx'), may hold values from -4.5 to 7
Outputs:
- log_perm: float32 [128, 32, 2048], P('gz', 'gy', 'gx')
- smoothed: float32 [128, 32, 2048], P('gz', 'gy', 'gx')
All inputs are finite; a program needn't handle non-finite values. No bound on the sum of `colour` on one device may be relied on, other than what follows from the above.
Results may differ from a plain program's by a relative error of at most 0.0038.
Values sent between devices are 32-bit elements; how exact they have to be, the bound alone decides.
No kernel may reach another device: no remote copies, remote signals or barrier semaphores. Data moves between devices by JAX's collectives and lax.ppermute only.
A program may use at most 128 MiB of HBM per device.

v0:
```python
import functools
import math

import jax
import jax.numpy as jnp


from jax import lax
from jax.experimental import pallas as pl
from jax.experimental.pallas import tpu as pltpu
from jax.sharding import PartitionSpec as P

NX = 2048


STORE = 1.0


def padded_2(block, sides, width):
    for axis, dim in sides:
        count = lax.axis_size(axis)
        forward = [(i, i + 1) for i in range(count - 1)]
        backward = [(target, source) for source, target in forward]
        low = lax.ppermute(
            lax.slice_in_dim(block, block.shape[dim] - width, None, axis=dim), axis, forward
        )
        high = lax.ppermute(lax.slice_in_dim(block, 0, width, axis=dim), axis, backward)
        block = jnp.concatenate([low, block, high], axis=dim)
    return block


def twisted_coeffs(spectral, shifts, first_wave):
    count = spectral.shape[3]
    wave_index = first_wave + jnp.arange(count, dtype=jnp.int32)
    wave_turns = shifts[:, :, None] * wave_index[None, None, :] % NX
    phase_angle = wave_turns.astype(jnp.float32) * (2.0 * math.pi / NX)
    cosine = jnp.cos(phase_angle)
    sine_part = jnp.sin(phase_angle)
    real_part = spectral[0] * cosine - spectral[1] * sine_part
    imag_part = spectral[0] * sine_part + spectral[1] * cosine
    return jnp.stack([real_part, imag_part])


def basis(count, first_cell, width_cells):
    wave_index = jnp.arange(count, dtype=jnp.int32)
    cell_index = first_cell + jnp.arange(width_cells, dtype=jnp.int32)
    wave_turns = wave_index[:, None] * cell_index[None, :] % NX
    phase_angle = wave_turns.astype(jnp.float32) * (2.0 * math.pi / NX)
    offsets = jnp.concatenate(
        [jnp.zeros((count, 1), jnp.float32), jnp.full((count, 1), 0.5 * math.pi, jnp.float32)],
        axis=0,
    )
    stacked = jnp.concatenate([phase_angle, phase_angle], axis=0) + offsets
    return jnp.cos(stacked) * (1.0 / math.sqrt(NX))


def flatten_pair(piece):
    depth, items, count = (piece.shape[1], piece.shape[2], piece.shape[3])
    return jnp.concatenate(
        [piece[0].reshape(depth * items, count), piece[1].reshape(depth * items, count)], axis=1
    )


def harmonic(center, beside):
    return 2.0 * center * beside / (center + beside)


def thomas(lower_diagonal, main_diagonal, upper_diagonal, right_hand_side):

    def thomas_forward_scan(carried_state, row_entries):
        previous_ratio, previous_eliminated = carried_state
        column_lower, main_c, sup_c, column_right_hand = row_entries
        present_denominator = main_c - column_lower * previous_ratio
        present_ratio = sup_c / present_denominator
        present_eliminated = (
            column_right_hand - column_lower * previous_eliminated
        ) / present_denominator
        return ((present_ratio, present_eliminated), (present_ratio, present_eliminated))

    zeroed_layer = jnp.zeros(right_hand_side.shape[1:], right_hand_side.dtype)
    unused_output, (ratio_rows, eliminated_rows) = lax.scan(
        thomas_forward_scan,
        (zeroed_layer, zeroed_layer),
        (lower_diagonal, main_diagonal, upper_diagonal, right_hand_side),
    )

    def thomas_backward_scan(following_value, row_entries):
        column_ratio, column_eliminated = row_entries
        present_value = column_eliminated - column_ratio * following_value
        return (present_value, present_value)

    unused_output, solved_values = lax.scan(
        thomas_backward_scan, zeroed_layer, (ratio_rows, eliminated_rows), reverse=True
    )
    return solved_values


def factor(lower_diagonal, main_diagonal, upper_diagonal):

    def factor_forward_scan(previous_ratio, row_entries):
        column_lower, main_c, sup_c = row_entries
        present_denominator = main_c - column_lower * previous_ratio
        present_ratio = sup_c / present_denominator
        return (present_ratio, (present_denominator, present_ratio))

    unused_output, (denominator_rows, ratio_rows) = lax.scan(
        factor_forward_scan,
        jnp.zeros_like(main_diagonal[0]),
        (lower_diagonal, main_diagonal, upper_diagonal),
    )
    return (denominator_rows, ratio_rows)


def solve_factored(lower_diagonal, denominator_rows, ratio_rows, right_hand_side):

    def solve_forward_scan(previous_eliminated, row_entries):
        column_lower, column_denominator, column_right_hand = row_entries
        present_eliminated = (
            column_right_hand - column_lower[None] * previous_eliminated
        ) / column_denominator[None]
        return (present_eliminated, present_eliminated)

    unused_output, eliminated_rows = lax.scan(
        solve_forward_scan,
        jnp.zeros_like(right_hand_side[0]),
        (lower_diagonal, denominator_rows, right_hand_side),
    )

    def solve_backward_scan(following_value, row_entries):
        column_ratio, column_eliminated = row_entries
        present_value = column_eliminated - column_ratio[None] * following_value
        return (present_value, present_value)

    unused_output, solved_values = lax.scan(
        solve_backward_scan,
        jnp.zeros_like(right_hand_side[0]),
        (ratio_rows, eliminated_rows),
        reverse=True,
    )
    return solved_values


def generic_body(spectral, shifts, colour, pressure, source):
    total_depth = pressure.shape[0] * lax.axis_size("gz")
    vert_factor = float(total_depth * total_depth // 4)
    width_cells = spectral.shape[3]
    first_cell = lax.axis_index("gx") * width_cells
    twisted = twisted_coeffs(spectral, shifts, first_cell)
    piece = lax.all_to_all(twisted, "gx", split_axis=1, concat_axis=3, tiled=True)
    depth = piece.shape[1]
    items = piece.shape[2]
    length = piece.shape[3]
    flat = flatten_pair(piece)
    block_width = min(512, length)
    blocks = [
        jnp.dot(
            flat,
            basis(length, block * block_width, block_width),
            precision=lax.Precision.HIGHEST,
            preferred_element_type=jnp.float32,
        )
        for block in range(length // block_width)
    ]
    field_rows = jnp.concatenate(blocks, axis=1).reshape(depth, items, length)
    log_perm = lax.all_to_all(field_rows, "gx", split_axis=2, concat_axis=0, tiled=True)
    perm = jnp.exp(log_perm)
    padded = padded_2(perm, (("gx", 2), ("gz", 0), ("gy", 1)), 1)
    w_zm = vert_factor * harmonic(perm, padded[:-2, 1:-1, 1:-1])
    w_zp = vert_factor * harmonic(perm, padded[2:, 1:-1, 1:-1])
    w_ym = harmonic(perm, padded[1:-1, :-2, 1:-1])
    w_yp = harmonic(perm, padded[1:-1, 2:, 1:-1])
    w_xm = harmonic(perm, padded[1:-1, 1:-1, :-2])
    w_xp = harmonic(perm, padded[1:-1, 1:-1, 2:])
    main_diagonal = STORE + w_xm + w_xp + w_ym + w_yp + w_zm + w_zp
    lower_diagonal = -w_zm
    upper_diagonal = -w_zp
    zeroed_layer = jnp.zeros_like(main_diagonal[0])
    inner_sub = jnp.concatenate([zeroed_layer[None], lower_diagonal[2:-1]], axis=0)
    inner_sup = jnp.concatenate([upper_diagonal[1:-2], zeroed_layer[None]], axis=0)
    inner_main = main_diagonal[1:-1]
    denominator_rows, ratio_rows = factor(inner_sub, inner_main, inner_sup)
    unit_rhs = jnp.zeros((inner_main.shape[0], 2) + zeroed_layer.shape, jnp.float32)
    unit_rhs = unit_rhs.at[0, 0].set(-lower_diagonal[1])
    unit_rhs = unit_rhs.at[-1, 1].set(-upper_diagonal[-2])
    coupled = solve_factored(inner_sub, denominator_rows, ratio_rows, unit_rhs)
    left_part = coupled[:, 0]
    right_part = coupled[:, 1]
    sub_first = lower_diagonal[0]
    main_first = main_diagonal[0] + upper_diagonal[0] * left_part[0]
    sup_first = upper_diagonal[0] * right_part[0]
    sub_last = lower_diagonal[-1] * left_part[-1]
    main_last = main_diagonal[-1] + lower_diagonal[-1] * right_part[-1]
    sup_last = upper_diagonal[-1]

    def line_solve(current):
        cycle = padded_2(current, (("gx", 2), ("gy", 1)), 1)
        right_hand_side = source + w_xm * cycle[:, 1:-1, :-2] + w_xp * cycle[:, 1:-1, 2:]
        right_hand_side = right_hand_side + w_ym * cycle[:, :-2, 1:-1] + w_yp * cycle[:, 2:, 1:-1]
        particular = solve_factored(
            inner_sub, denominator_rows, ratio_rows, right_hand_side[1:-1][:, None]
        )[:, 0]
        rhs_first = right_hand_side[0] - upper_diagonal[0] * particular[0]
        rhs_last = right_hand_side[-1] - lower_diagonal[-1] * particular[-1]
        reduced_rows = jnp.stack(
            [sub_first, main_first, sup_first, rhs_first, sub_last, main_last, sup_last, rhs_last]
        )
        gathered = lax.all_gather(reduced_rows, "gz", axis=0, tiled=True)
        segments = gathered.shape[0] // 8
        system = gathered.reshape((2 * segments, 4) + zeroed_layer.shape)
        reduced_sol = thomas(system[:, 0], system[:, 1], system[:, 2], system[:, 3])
        own_pair = lax.dynamic_slice_in_dim(reduced_sol, 2 * lax.axis_index("gz"), 2, 0)
        face_first = own_pair[0]
        face_last = own_pair[1]
        inner = particular + face_first[None] * left_part + face_last[None] * right_part
        return jnp.concatenate([face_first[None], inner, face_last[None]], axis=0)

    half = jnp.where((colour == 0)[None], line_solve(pressure), pressure)
    smoothed = jnp.where((colour == 1)[None], line_solve(half), half)
    return (log_perm, smoothed)


LANES = 128
ROWS = 8
F32 = jnp.float32
MIB = 1 << 20
SUMS_GRANT = 60


def suits(mesh):
    sizes = dict(mesh.shape)
    return sizes["gx"] == 2 and sizes["gz"] == 4 and sizes["gy"] == 4


def params(mib):
    return pltpu.CompilerParams(vmem_limit_bytes=mib * MIB)


def cos_sin(turns):
    quarter = (turns + NX // 8) >> 9
    angle = (turns - (quarter << 9)).astype(F32) * (2.0 * math.pi / NX)
    square = angle * angle
    sine = angle * (
        1.0
        + square * (-1.0 / 6 + square * (1.0 / 120 + square * (-1.0 / 5040 + square / 362880)))
    )
    cosine = 1.0 + square * (
        -0.5 + square * (1.0 / 24 + square * (-1.0 / 720 + square * (1.0 / 40320)))
    )
    odd = (quarter & 1) == 1
    first = jnp.where(odd, sine, cosine)
    second = jnp.where(odd, cosine, sine)
    cos_sign = jnp.where(((quarter + 1) & 2) == 2, -1.0, 1.0)
    sin_sign = jnp.where((quarter & 2) == 2, -1.0, 1.0)
    return first * cos_sign, second * sin_sign


def split(values):
    high = values.astype(jnp.bfloat16)
    return high, (values - high.astype(F32)).astype(jnp.bfloat16)


def times(first, second):
    return (
        first[0] * second[0] - first[1] * second[1],
        first[0] * second[1] + first[1] * second[0],
    )


def plus(first, second):
    return (first[0] + second[0], first[1] + second[1])


def minus(first, second):
    return (first[0] - second[0], first[1] - second[1])


def quarter_turn(value):
    return (-value[1], value[0])


def four_point(first, second, third, fourth):
    even, gap = plus(first, third), minus(first, third)
    odd, turned = plus(second, fourth), quarter_turn(minus(second, fourth))
    return [plus(even, odd), plus(gap, turned), minus(even, odd), minus(gap, turned)]


def eight_point(values):
    even = four_point(*values[0::2])
    odd = four_point(*values[1::2])
    root = math.sqrt(0.5)
    real, imag = odd[1]
    odd[1] = (root * (real - imag), root * (real + imag))
    odd[2] = quarter_turn(odd[2])
    real, imag = odd[3]
    odd[3] = (-root * (real + imag), root * (real - imag))
    return [plus(*pair) for pair in zip(even, odd)] + [minus(*pair) for pair in zip(even, odd)]


def fill_tables(basis, turns):
    groups = NX // LANES
    shape = (LANES, LANES)
    lane = lane_of(shape)
    cells = (lane % groups) * (LANES // groups) + lane // groups
    cosine, sine = cos_sin((row_of(shape) * cells) % LANES * groups)
    for at, value in enumerate((cosine, -sine)):
        rows = slice(at * LANES, (at + 1) * LANES)
        high, low = split(value * (1.0 / math.sqrt(NX)))
        basis[0, rows], basis[1, rows], basis[2, rows] = high, high, low
    shape = (groups, LANES)
    turns[0], turns[1] = cos_sin(row_of(shape) * lane_of(shape))


def diagonal_of(depth):
    square = (depth, depth)
    return row_of(square) == lane_of(square)


def shift_columns(shifts, rows_of, columns):
    depth = shifts.shape[1]
    diagonal = diagonal_of(depth)
    for at, y in enumerate(rows_of):
        spread = jnp.where(diagonal, shifts[y : y + 1, :].astype(F32), 0.0)
        shift = jnp.broadcast_to(jnp.sum(spread, axis=1, keepdims=True), (depth, LANES))
        columns[at * depth : (at + 1) * depth, :] = shift.astype(jnp.int32)


def edge_columns(ys, depth, edges, kept):
    kept[...] = jnp.zeros_like(kept)
    diagonal = diagonal_of(depth)
    for at in range(len(ys)):
        rows = slice(at * depth, (at + 1) * depth)
        for side, lane in enumerate((LANES - 1, 0)):
            column = jnp.broadcast_to(edges[side, rows, lane : lane + 1], (depth, depth))
            row = jnp.sum(jnp.where(diagonal, column, 0.0), axis=0, keepdims=True)
            kept[side, at : at + 1, :depth] = row


def twisted(first_wave, shift, coefficients, rows):
    lane = lane_of(shift.shape)
    phase = cos_sin((shift * (lane + first_wave)) & (NX - 1))
    turn = cos_sin((shift * LANES) & (NX - 1))
    values = []
    for part in range(coefficients.shape[0]):
        values.append(times((coefficients[part, 0, rows], coefficients[part, 1, rows]), phase))
        phase = times(phase, turn)
    return values


def interleave(tiles):
    count = len(tiles)
    lane = lane_of(tiles[0].shape)
    bit = count // 2
    while bit:
        low = (lane & bit) == 0
        moved = list(tiles)
        for at in range(count):
            if not at & bit:
                first, second = tiles[at], tiles[at | bit]
                crossed = jnp.take_along_axis(
                    jnp.where(low, second, first), lane ^ bit, axis=1
                )
                moved[at] = jnp.where(low, first, crossed)
                moved[at | bit] = jnp.where(low, crossed, second)
        tiles = moved
        bit //= 2
    return tiles


def row_sums(g, at, y, depth, items, columns, coefficients, basis, turns, left, right, emit):
    groups = NX // LANES
    sign = 1.0 - 2.0 * g.astype(F32)
    first_wave = g * (coefficients.shape[0] * LANES)
    step = 16
    for part in range(depth // step):
        rows = pl.ds(part * step * items + y, step, stride=items)
        shift = columns[pl.ds(at * depth + part * step, step), :]
        values = twisted(first_wave, shift, coefficients, rows)
        turned = [
            times(value, (sign * math.cos(2 * math.pi * p / groups), sign * math.sin(2 * math.pi * p / groups)))
            if p
            else (sign * value[0], sign * value[1])
            for p, value in enumerate(values)
        ]
        even, odd = eight_point(values), eight_point(turned)
        for group in range(groups):
            value = odd[group // 2] if group % 2 else even[group // 2]
            if group:
                value = times(value, (turns[0, group : group + 1], turns[1, group : group + 1]))
            first = group * depth + part * step
            for place_of, piece in enumerate(value):
                for half, bits in enumerate(split(piece)):
                    target = (2 * half + place_of) * LANES
                    left[first : first + step, target : target + LANES] = bits
    spread = jnp.concatenate([left[...], left[:, : 2 * LANES]], axis=1)
    bases = basis[...].reshape(-1, LANES)
    right[...] = jnp.dot(spread, bases, preferred_element_type=F32)
    for part in range(depth // ROWS):
        tiles = [
            right[group * depth + part * ROWS : group * depth + (part + 1) * ROWS]
            for group in range(groups)
        ]
        emit(pl.ds(at * depth + part * ROWS, ROWS), interleave(tiles))


def load_coefficients(spectral, coefficients, arrivals):
    parts = coefficients.shape[0]
    copies = [
        pltpu.make_async_copy(
            spectral.at[:, :, part * LANES : (part + 1) * LANES],
            coefficients.at[part],
            arrivals.at[part],
        )
        for part in range(parts)
    ]
    for copy in copies:
        copy.start()
    return copies


def keep_edges(rows, tiles, edges):
    half = len(tiles) // 2
    edges[0, rows], edges[1, rows] = tiles[half - 1], tiles[half]


def wide_sums_kernel(ys, shifts, spectral, other, own, kept, *refs):
    columns, edges, coefficients, arrivals, *tables, left, right = refs
    items, depth = shifts.shape
    copies = load_coefficients(spectral, coefficients, arrivals)
    fill_tables(*tables)
    shift_columns(shifts, ys, columns)
    for copy in copies:
        copy.wait()
    g = lax.axis_index("gx")

    def emit(rows, tiles):
        half = len(tiles) // 2
        keep_edges(rows, tiles, edges)
        for tile, (low, high) in enumerate(zip(tiles[:half], tiles[half:])):
            there = slice(tile * LANES, (tile + 1) * LANES)
            other[rows, there] = jnp.where(g == 0, high, low)
            own[rows, there] = jnp.where(g == 0, low, high)

    for at, y in enumerate(ys):
        row_sums(
            *(g, at, y, depth, items, columns, coefficients, *tables),
            *(left.at[at % 2], right.at[at % 2], emit),
        )
    edge_columns(ys, depth, edges, kept)


def last_sums_kernel(ys, shifts, outer_kept, inner_kept, spectral, one, two, own, *refs):
    mine, theirs, kept, columns, edges, coefficients, arrivals, *tables, left, right = refs
    items, depth = shifts.shape
    copies = load_coefficients(spectral, coefficients, arrivals)
    fill_tables(*tables)
    shift_columns(shifts, ys, columns)
    for copy in copies:
        copy.wait()
    g = lax.axis_index("gx")

    def emit(rows, tiles):
        half = len(tiles) // 2
        keep_edges(rows, tiles, edges)
        others = []
        for tile, (low, high) in enumerate(zip(tiles[:half], tiles[half:])):
            own[rows, tile * LANES : (tile + 1) * LANES] = jnp.where(g == 0, low, high)
            others.append(jnp.where(g == 0, high, low))
        start = 0
        for ref in (one, two):
            count = ref.shape[1] // LANES
            for tile in range(count):
                ref[rows, tile * LANES : (tile + 1) * LANES] = jnp.where(
                    g == 0, others[start + tile], others[half - start - count + tile]
                )
            start += count

    for at, y in enumerate(ys):
        row_sums(
            *(g, at, y, depth, items, columns, coefficients, *tables),
            *(left.at[at % 2], right.at[at % 2], emit),
        )
    edge_columns(ys, depth, edges, kept)
    sides_of = [
        jnp.concatenate(
            [outer_kept[side, :1], inner_kept[side], kept[side], outer_kept[side, 1:]], axis=0
        )
        for side in range(2)
    ]
    mine[...] = jnp.where(g == 0, sides_of[0], sides_of[1])
    theirs[...] = jnp.where(g == 0, sides_of[1], sides_of[0])


SCALARS = pl.BlockSpec(memory_space=pltpu.SMEM)
ON_CHIP = pl.BlockSpec(memory_space=pltpu.VMEM)
IN_HBM = pl.BlockSpec(memory_space=pltpu.HBM)


def call(kernel, name, out_shape, args, flags=None, scratch=(), far=(), mib=20, flops=1):
    specs = [ON_CHIP] * len(args) + [IN_HBM] * len(far)
    args = list(args) + list(far)
    if flags is not None:
        specs = [SCALARS] + specs
        args = [flags] + args
    return pl.pallas_call(
        kernel,
        out_shape=out_shape,
        in_specs=specs,
        out_specs=jax.tree.map(lambda _: ON_CHIP, out_shape),
        scratch_shapes=list(scratch),
        compiler_params=params(mib),
        cost_estimate=pl.CostEstimate(flops=flops, bytes_accessed=1, transcendentals=0),
        name=name,
    )(*args)


def roll(values, shift, axis):
    return pltpu.roll(values, shift % values.shape[axis], axis)


def lane_of(shape):
    return lax.broadcasted_iota(jnp.int32, shape, 1)


def row_of(shape):
    return lax.broadcasted_iota(jnp.int32, shape, 0)


def column_to(z, packed, target):
    return pltpu.roll(packed, (target - z) % LANES, 1)


def packed_with(z, packed, plane, lane):
    column = jnp.broadcast_to(plane[:, lane : lane + 1], (ROWS, LANES))
    return jnp.where(lane_of((ROWS, LANES)) == z, column, packed)


def inverse_of(values):
    guess = pl.reciprocal(values, approx=True)
    return guess * (2.0 - values * guess)


def ordered(z, sums, depth):
    spread = pl.ds(z, ROWS, stride=depth)
    return jnp.concatenate([sums[at, spread] for at in range(sums.shape[0])], axis=1)


def place_tiles(sums, rows, first, values):
    for at in range(values.shape[1] // LANES):
        sums[(first >> 7) + at, rows] = values[:, at * LANES : (at + 1) * LANES]


def boundary_plane(g, plane):
    return jnp.where(g == 0, roll(plane[:, -LANES:], 1, 1), plane[:, :LANES])


def outer_field_kernel(depth, flags, own, other, pressure, to_near, to_middle, boundary):
    g, even = flags[0], flags[16] == 0
    low, high = slice(0, depth), slice(depth, 2 * depth)
    south, north = own[low] + other[low], own[high] + other[high]
    to_near[low] = jnp.exp(-jnp.where(even, north, south))
    to_middle[low] = jnp.exp(-jnp.where(even, south, north))

    def layer(z, packed):
        plane = pressure[z]
        keep_rows(depth + z, plane, even, to_near, to_middle, slice(None))
        return packed_with(z, packed, boundary_plane(g, plane), 0)

    boundary[...] = lax.fori_loop(0, depth, layer, jnp.zeros((ROWS, LANES), F32), unroll=8)


def wide_field_kernel(depth, flags, *refs):
    own_outer, outer, own_inner, inner, to_near, to_middle = refs[:6]
    from_near, from_middle, sums_here, sums_there = refs[6:10]
    wide, south_weight, north_weight, south_terms, north_rows, column = refs[10:]
    even = flags[16] == 0
    low, high = slice(0, depth), slice(depth, 2 * depth)
    wide[low] = own_outer[low] + outer[low]
    wide[depth:-depth] = own_inner[...] + inner[...]
    wide[-depth:] = own_outer[high] + outer[high]
    near_weight = 2.0 * inverse_of(to_near[low] + from_near[low])
    middle_weight = (2.0 * flags[15].astype(F32)) * inverse_of(to_middle[low] + from_middle[low])
    south = jnp.where(even, middle_weight, near_weight)
    south_weight[...] = south
    north_weight[...] = jnp.where(even, near_weight, middle_weight)
    south_terms[...] = south * jnp.where(even, from_middle[high], from_near[high])
    north_rows[...] = jnp.where(even, from_near[high], from_middle[high])
    column[...] = jnp.exp(-(sums_here[...] + sums_there[...]))


def lane_slice(start, size):
    return pl.ds(pl.multiple_of(start, LANES), size)


def assemble(sums, depth, wide, own, piece, there):
    inside = wide.shape[0] - depth
    place_tiles(sums, slice(0, inside), 0, wide[:inside, there])
    place_tiles(sums, slice(inside, -depth), 0, own[:, there] + piece[...])
    place_tiles(sums, slice(-depth, None), 0, wide[inside:, there])


def first_field_kernel(depth, flags, *refs):
    wide, own, middle = refs[:3]
    log_perm, resist, low_side, high_side, boundary, sums = refs[3:]
    g, start = flags[0], flags[3]
    assemble(sums, depth, wide, own, middle, lane_slice(start, log_perm.shape[2]))
    edge = lane_slice(own.shape[1] // 2 - LANES - start, 2 * LANES)

    def layer(z, carry):
        low, high, bound = carry
        plane = ordered(z, sums, depth)
        inverse = jnp.exp(-plane)
        log_perm[z] = plane
        resist[z] = inverse
        both = resist[z, :, edge]
        return (
            packed_with(z, low, both, LANES - 1),
            packed_with(z, high, both, LANES),
            packed_with(z, bound, boundary_plane(g, inverse), 0),
        )

    zero = jnp.zeros((ROWS, LANES), F32)
    low_side[...], high_side[...], boundary[...] = lax.fori_loop(
        0, depth, layer, (zero, zero, zero), unroll=8
    )


def second_field_kernel(depth, flags, *refs):
    wide, own, middle, log_near, resist_near = refs[:5]
    log_perm, resist, sums = refs[5:]
    third, known = middle.shape[1], log_near.shape[2]
    there = lane_slice(flags[5], third)
    assemble(sums, depth, wide, own, middle, there)
    extra = resist.shape[2] - third
    target = lane_slice(flags[5] - flags[7], third)
    extra_target = lane_slice(flags[8], extra)
    extra_source = lane_slice(flags[9], extra)

    def layer(z, carry):
        plane = ordered(z, sums, depth)
        log_perm[z, :, lane_slice(flags[3], known)] = log_near[z]
        log_perm[z, :, there] = plane
        resist[z, :, target] = jnp.exp(-plane)
        resist[z, :, extra_target] = resist_near[z, :, extra_source]
        return carry

    lax.fori_loop(0, depth, layer, 0, unroll=8)


def keep_rows(z, value, even, to_near, to_middle, here):
    south, north = value[0:1, :], value[ROWS - 1 : ROWS, :]
    to_near[pl.ds(z, 1), here] = jnp.where(even, north, south)
    to_middle[pl.ds(z, 1), here] = jnp.where(even, south, north)


def with_first(plane, edge):
    first = jnp.where(lane_of((ROWS, LANES)) == 0, edge, plane[:, :LANES])
    return jnp.concatenate([first, plane[:, LANES:]], axis=1)


def with_last(plane, edge):
    last = jnp.where(lane_of((ROWS, LANES)) == LANES - 1, edge, plane[:, -LANES:])
    return jnp.concatenate([plane[:, :-LANES], last], axis=1)


def coupling(z, field, start, size, east_weight, north_weight, south_terms, north_rows, west, column):
    here = lane_slice(start, size)
    plane = field[z, :, here]
    row = row_of(plane.shape)
    at_start = start == 0
    inner = field[z, :, lane_slice(jnp.where(at_start, size, size - LANES), LANES)]
    west_value = jnp.where(at_start, column_to(z, column, 0), roll(inner, 1, 1))
    east_value = jnp.where(at_start, roll(inner, -1, 1), column_to(z, column, LANES - 1))
    to_east, to_north = east_weight * plane, north_weight * plane
    from_west = with_first(roll(to_east, 1, 1), column_to(z, west, 0) * west_value)
    from_east = east_weight * with_last(roll(plane, -1, 1), east_value)
    from_south = jnp.where(row == 0, south_terms[pl.ds(z, 1), here], roll(to_north, 1, 0))
    from_north = north_weight * jnp.where(
        row == ROWS - 1, north_rows[pl.ds(z, 1), here], roll(plane, -1, 0)
    )
    return (from_west + from_east) + (from_south + from_north)


def edge_weights(flags, start, bound, column, low_side, high_side):
    g = flags[0]
    middle = 2.0 * inverse_of(low_side + high_side)
    across = 2.0 * inverse_of(bound + column)
    none = jnp.zeros_like(across)
    west = jnp.where(start == 0, jnp.where(g == 0, none, across), middle)
    east = jnp.where(start == 0, middle, jnp.where(g == 0, across, none))
    return west, east


def first_sweep_kernel(depth, vert, block, flags, *refs):
    resist, low_side, high_side, r_bound, r_column = refs[:5]
    south_weight, north_weight, south_terms, north_rows = refs[5:9]
    pressure, p_column, source = refs[9:12]
    w_east, w_north, west_out, particular, inverse, ratio, lead, reduced = refs[12:20]
    grounds, rights, verticals = refs[20:]
    start, offset = flags[6 + block], flags[10 + block]
    size = inverse.shape[2]
    shape = (ROWS, size)
    here = lane_slice(start, size)
    inside = lane_slice(offset, size)
    west_weight, east_weight = edge_weights(
        flags, start, r_bound[...], r_column[...], low_side[...], high_side[...]
    )
    west_out[...] = west_weight
    column = p_column[...]
    row = row_of(shape)

    def weigh(z, carry):
        plane = resist[z, :, inside]
        east = 2.0 * inverse_of(plane + roll(plane, -1, 1))
        east = with_last(east, column_to(z, east_weight, LANES - 1))
        west = with_first(roll(east, 1, 1), column_to(z, west_weight, 0))
        north = 2.0 * inverse_of(plane + roll(plane, -1, 0))
        north = jnp.where(row == ROWS - 1, north_weight[pl.ds(z, 1), here], north)
        south = jnp.where(row == 0, south_weight[pl.ds(z, 1), here], roll(north, 1, 0))
        w_east[z], w_north[z] = east, north
        grounds[z] = STORE + ((east + west) + (north + south))
        verticals[z] = (2.0 * vert) * inverse_of(
            plane + resist[jnp.minimum(z + 1, depth - 1), :, inside]
        )
        rights[z] = source[z, :, here] + coupling(
            z, pressure, start, size, east, north, south_terms, north_rows, west_weight, column
        )
        return carry

    lax.fori_loop(0, depth, weigh, 0, unroll=4)

    def layer(z, carry):
        conduct, flow, product, first_first, first_part = carry
        weight = verticals[z]
        reciprocal = inverse_of(conduct + weight)
        quotient = weight * reciprocal
        led = product * reciprocal
        inverse[z] = reciprocal
        ratio[z] = quotient
        lead[z] = led
        particular[z] = reciprocal * flow
        return (
            grounds[z + 1] + conduct * quotient,
            rights[z + 1] + flow * quotient,
            product * quotient,
            first_first + led * product,
            first_part + led * flow,
        )

    zero = jnp.zeros(shape, F32)
    conduct, flow, product, first_first, first_part = lax.fori_loop(
        0,
        depth - 1,
        layer,
        (grounds[0], rights[0], jnp.ones(shape, F32), zero, zero),
        unroll=8,
    )
    reciprocal = inverse_of(conduct)
    led = product * reciprocal
    inverse[depth - 1] = reciprocal
    ratio[depth - 1] = zero
    lead[depth - 1] = led
    particular[depth - 1] = flow * reciprocal
    reduced[0] = first_first + led * product + resist[0, :, inside] * (0.5 / vert)
    reduced[1] = led
    reduced[2] = reciprocal + resist[depth - 1, :, inside] * (0.5 / vert)
    reduced[3] = first_part + led * flow
    reduced[4] = flow * reciprocal


def pair_kernel(flags, own_one, own_two, near_one, near_two, across, kept):
    me = flags[14]
    even, lower = me % 2 == 0, me < 2
    for block, (own, near) in enumerate(((own_one, near_one), (own_two, near_two))):
        size = own.shape[2]
        there = slice(block * size, (block + 1) * size)
        first, second = [
            [jnp.where(flip, own[at], near[at]) for at in range(5)]
            for flip in (even, jnp.logical_not(even))
        ]
        reciprocal = inverse_of(first[2] + second[0])
        step = (first[4] - second[3]) * reciprocal
        through = jnp.where(lower, second[1], first[1])
        share = through * reciprocal
        across[0, :, there] = jnp.where(lower, second[2], first[0]) - through * share
        across[1, :, there] = jnp.where(lower, second[4], first[3]) + jnp.where(
            lower, through * step, -through * step
        )
        kept[0, :, there] = share
        kept[1, :, there] = reciprocal
        kept[2, :, there] = step


def ends(me, inner, middle):
    zero = jnp.zeros_like(inner)
    odd = me % 2 == 1
    enters = jnp.where(odd, inner, jnp.where(me == 2, middle, zero))
    leaves = jnp.where(odd, jnp.where(me == 1, middle, zero), inner)
    return enters, leaves


def back_substitute(depth, lines, emit):
    last = depth - 1
    values = tuple(
        (particular[last] + lead[last] * enters) - inverse[last] * leaves
        for enters, leaves, particular, inverse, ratio, lead in lines
    )
    state = emit(last, values, jnp.zeros((ROWS, LANES), F32))

    def layer(step, carry):
        following, state = carry
        z = last - step
        values = tuple(
            (particular[z] + lead[z] * enters) + ratio[z] * beyond
            for (enters, _, particular, _, ratio, lead), beyond in zip(lines, following)
        )
        return values, emit(z, values, state)

    return lax.fori_loop(1, depth, layer, (values, state), unroll=4)[1]


def half_kernel(depth, flags, *refs):
    across, other, kept = refs[:3]
    blocks = (refs[3:7], refs[7:11])
    pressure, colour = refs[11:13]
    half, to_near, to_middle, boundary, joined = refs[13:]
    me, g, even = flags[14], flags[0], flags[16] == 0
    size = blocks[0][0].shape[2]
    spans = [lane_slice(flags[6 + block], size) for block in range(2)]
    lines = []
    for block, state in enumerate(blocks):
        there = slice(block * size, (block + 1) * size)
        sum_of = inverse_of(across[0, :, there] + other[0, :, there])
        joined[:, there] = sum_of
        lead_of = across[1, :, there] - other[1, :, there]
        middle = jnp.where(me < 2, lead_of, -lead_of) * sum_of
        inner = kept[2, :, there] + kept[0, :, there] * middle
        lines.append((*ends(me, inner, middle), *state))
    chosen = [colour[:, here] == 0 for here in spans]

    def emit(z, values, packed):
        for block, (value, here) in enumerate(zip(values, spans)):
            value = jnp.where(chosen[block], value, pressure[z, :, here])
            half[z, :, here] = value
            keep_rows(z, value, even, to_near, to_middle, here)
            if not block:
                packed = packed_with(z, packed, boundary_plane(g, value), 0)
        return packed

    boundary[...] = back_substitute(depth, lines, emit)


def second_sweep_kernel(depth, flags, *refs):
    half, h_near, h_middle, h_column, source, kept, south_weight = refs[:7]
    blocks = (refs[7:13], refs[13:19])
    particulars, near, far = refs[19:21], refs[21], refs[22]
    south_terms, north_rows = refs[23:]
    me, even = flags[14], flags[16] == 0
    size = particulars[0].shape[2]
    starts = [flags[6 + block] for block in range(2)]
    spans = [lane_slice(start, size) for start in starts]
    column = h_column[...]
    south_terms[...] = south_weight[...] * jnp.where(even, h_middle[...], h_near[...])
    north_rows[...] = jnp.where(even, h_near[...], h_middle[...])

    def local(z, block):
        east, north, west = blocks[block][:3]
        return source[z, :, spans[block]] + coupling(
            z,
            half,
            starts[block],
            size,
            east[z],
            north[z],
            south_terms,
            north_rows,
            west[...],
            column,
        )

    def layer(z, carry):
        result = []
        for block, (flow, first_part) in enumerate(carry):
            inverse, ratio, lead = blocks[block][3:6]
            particulars[block][z] = flow * inverse[z]
            first_part = first_part + lead[z] * flow
            result.append((local(z + 1, block) + flow * ratio[z], first_part))
        return tuple(result)

    carry = tuple((local(0, block), jnp.zeros((ROWS, size), F32)) for block in range(2))
    carry = lax.fori_loop(0, depth - 1, layer, carry, unroll=2)
    last = depth - 1
    for block, (flow, first_part) in enumerate(carry):
        inverse, ratio, lead = blocks[block][3:6]
        there = slice(block * size, (block + 1) * size)
        first_part = first_part + lead[last] * flow
        last_part = flow * inverse[last]
        particulars[block][last] = last_part
        asked = jnp.where(me % 2 == 0, last_part, first_part)
        shared = kept[0, :, there] * asked
        outer = jnp.where(me == 1, last_part, jnp.where(me == 2, first_part, 0.0))
        given = outer + jnp.where((me == 0) | (me == 3), shared, -shared)
        near[0, :, there] = asked
        near[1, :, there] = given
        far[:, there] = given


def smoothed_kernel(depth, flags, *refs):
    own, near, skip, cross, kept, joined = refs[:6]
    blocks = (refs[6:10], refs[10:14])
    half, colour, smoothed = refs[14:]
    me = flags[14]
    size = blocks[0][0].shape[2]
    spans = [lane_slice(flags[6 + block], size) for block in range(2)]
    lines = []
    for block, state in enumerate(blocks):
        there = slice(block * size, (block + 1) * size)
        lead_of = (own[1, :, there] + near[1, :, there]) - (skip[:, there] + cross[:, there])
        middle = jnp.where(me < 2, lead_of, -lead_of) * joined[:, there]
        step = own[0, :, there] - near[0, :, there]
        step = jnp.where(me % 2 == 0, step, -step) * kept[1, :, there]
        lines.append((*ends(me, step + kept[0, :, there] * middle, middle), *state))
    chosen = [colour[:, here] == 1 for here in spans]

    def emit(z, values, state):
        for value, here, mine in zip(values, spans, chosen):
            smoothed[z, :, here] = jnp.where(mine, value, half[z, :, here])
        return state

    back_substitute(depth, lines, emit)


PAIR = [(0, 1), (1, 0)]
NEAR = [(0, 1), (1, 0), (2, 3), (3, 2)]
MIDDLE = [(1, 2), (2, 1)]
SKIP = [(0, 2), (2, 0), (1, 3), (3, 1)]
CROSS = [(0, 3), (3, 0), (1, 2), (2, 1)]


def exchange_edges(edges):
    to_near, to_middle, *column = edges
    return [
        lax.ppermute(to_near, "gy", NEAR),
        lax.ppermute(to_middle, "gy", MIDDLE),
        *[lax.ppermute(piece, "gx", PAIR) for piece in column],
    ]


def fast_body(spectral, shifts, colour, pressure, source):
    depth, items, width = pressure.shape
    vert = float((depth * 4) ** 2 // 4)
    waves = spectral.shape[3]
    rows = depth * items
    gx, gz, gy = (lax.axis_index(axis) for axis in ("gx", "gz", "gy"))
    block_size, third = width // 2, 3 * width // 8
    known = width - third

    def placed(start, size):
        return jnp.where(gx == 1, start, width - start - size)

    block_one, block_two = placed(0, block_size), placed(block_size, block_size)
    start_one = placed(0, known)
    extra = known - block_size
    flags = jnp.stack(
        [
            gx,
            placed(0, LANES),
            placed(LANES, known - LANES),
            start_one,
            jnp.zeros_like(gx),
            placed(known, third),
            block_one,
            block_two,
            placed(block_size, extra) - block_two,
            placed(block_size, extra) - start_one,
            block_one - start_one,
            jnp.zeros_like(gx),
            gy > 0,
            gy < 3,
            gz,
            (gy == 1) | (gy == 2),
            gy % 2,
        ]
    ).astype(jnp.int32)

    def shaped(*shape, dtype=F32):
        return jax.ShapeDtypeStruct(shape, dtype)

    groups = NX // LANES
    parts = waves // LANES
    inner_ys, last_ys = (1, 2, 3), tuple(range(4, items - 1))
    last_rows = len(last_ys) * depth
    column_type = shaped(ROWS, LANES)
    coefficients = spectral.reshape(2, rows, waves)

    def scratch(count):
        return [
            pltpu.VMEM((count, LANES), jnp.int32),
            pltpu.VMEM((2, count, LANES), F32),
            pltpu.VMEM((parts, 2, rows, LANES), F32),
            pltpu.SemaphoreType.DMA((parts,)),
            pltpu.VMEM((3, 2 * LANES, LANES), jnp.bfloat16),
            pltpu.VMEM((2, groups, LANES), F32),
            pltpu.VMEM((2, groups * depth, 4 * LANES), jnp.bfloat16),
            pltpu.VMEM((2, groups * depth, LANES), F32),
        ]

    def wide_sums(ys, name, shift_rows, cost):
        return call(
            functools.partial(wide_sums_kernel, ys),
            name,
            [shaped(len(ys) * depth, width)] * 2 + [shaped(2, len(ys), LANES)],
            [shift_rows],
            scratch=scratch(len(ys) * depth),
            far=[coefficients],
            mib=SUMS_GRANT,
            flops=cost,
        )

    shift_rows = shifts.T
    sums, own_outer, outer_kept = wide_sums((0, items - 1), "outer_row_sums", shift_rows, 1)
    outer = lax.ppermute(sums, "gx", PAIR)
    shift_rows, _ = lax.optimization_barrier((shift_rows, own_outer))
    sums, own_inner, inner_kept = wide_sums(inner_ys, "inner_row_sums", shift_rows, 1 << 30)
    inner = lax.ppermute(sums, "gx", PAIR)
    last_one, last_two, own_last, mine, theirs = call(
        functools.partial(last_sums_kernel, last_ys),
        "last_row_sums",
        [shaped(last_rows, size) for size in (known, third, width)] + [column_type] * 2,
        [shift_rows, outer_kept, inner_kept],
        scratch=[pltpu.VMEM((2, len(last_ys), LANES), F32)] + scratch(last_rows),
        far=[coefficients],
        mib=SUMS_GRANT,
        flops=1 << 30,
    )
    column_sums = [theirs, lax.ppermute(mine, "gx", PAIR)]
    last_one, last_two = (lax.ppermute(piece, "gx", PAIR) for piece in (last_one, last_two))
    edge_row, edge_column = shaped(depth, width), shaped(ROWS, LANES)
    edges = [edge_row, edge_row, edge_column]
    to_near, to_middle, p_column = call(
        functools.partial(outer_field_kernel, depth),
        "outer_field",
        [shaped(2 * depth, width)] * 2 + [edge_column],
        [own_outer, outer, pressure],
        flags,
    )
    from_near, from_middle, p_column = exchange_edges([to_near, to_middle, p_column])
    wide, *row_edges, r_column = call(
        functools.partial(wide_field_kernel, depth),
        "wide_field",
        [shaped(rows - last_rows, width)] + [edge_row] * 4 + [edge_column],
        [
            *(own_outer, outer, own_inner, inner, to_near, to_middle),
            *(from_near, from_middle, *column_sums),
        ],
        flags,
    )
    log_near, resist_near, *columns = call(
        functools.partial(first_field_kernel, depth),
        "first_field",
        [shaped(depth, items, known)] * 2 + [edge_column] * 3,
        [wide, own_last, last_one],
        flags,
        [pltpu.VMEM((known // LANES, rows, LANES), F32)],
    )
    block = shaped(depth, items, block_size)

    state_types = [block] * 2 + [edge_column] + [block] * 4

    def first_sweep(at, resist):
        return call(
            functools.partial(first_sweep_kernel, depth, vert, at),
            "first_sweep",
            state_types + [shaped(5, items, block_size)],
            [resist, *columns, r_column, *row_edges, pressure, p_column, source],
            flags,
            [pltpu.VMEM((depth, items, block_size), F32)] * 3,
        )

    *state_one, reduced_one = first_sweep(0, resist_near)
    near_one = lax.ppermute(reduced_one, "gz", NEAR)
    last_two, _ = lax.optimization_barrier((last_two, reduced_one))
    log_perm, resist_far = call(
        functools.partial(second_field_kernel, depth),
        "second_field",
        [shaped(depth, items, width), block],
        [wide, own_last, last_two, log_near, resist_near],
        flags,
        [pltpu.VMEM((third // LANES, rows, LANES), F32)],
    )
    *state_two, reduced_two = first_sweep(1, resist_far)
    near_two = lax.ppermute(reduced_two, "gz", NEAR)
    across, kept = call(
        pair_kernel,
        "join_pair",
        [shaped(2, items, width), shaped(3, items, width)],
        [reduced_one, reduced_two, near_one, near_two],
        flags,
    )
    other = lax.ppermute(across, "gz", SKIP)
    half, *h_edges, joined = call(
        functools.partial(half_kernel, depth),
        "half",
        [shaped(depth, items, width), *edges, shaped(items, width)],
        [across, other, kept, *state_one[3:], *state_two[3:], pressure, colour],
        flags,
    )
    h_edges = exchange_edges(h_edges)
    weights = [[*state[:3], *state[4:]] for state in (state_one, state_two)]
    current_one, current_two, to_near, to_far = call(
        functools.partial(second_sweep_kernel, depth),
        "second_sweep",
        [block, block, shaped(2, items, width), shaped(items, width)],
        [half, *h_edges, source, kept, row_edges[0], *weights[0], *weights[1]],
        flags,
        [pltpu.VMEM((depth, width), F32)] * 2,
    )
    from_near, from_skip, from_cross = (
        lax.ppermute(planes, "gz", pairs)
        for planes, pairs in ((to_near, NEAR), (to_far, SKIP), (to_far, CROSS))
    )
    (smoothed,) = call(
        functools.partial(smoothed_kernel, depth),
        "smoothed",
        [shaped(depth, items, width)],
        [
            *(to_near, from_near, from_skip, from_cross, kept, joined),
            *(current_one, *state_one[4:]),
            *(current_two, *state_two[4:]),
            *(half, colour),
        ],
        flags,
    )
    return (log_perm, smoothed)


def solution(mesh):
    body = fast_body if suits(mesh) else generic_body
    in_specs = (
        P(None, "gz", "gy", "gx"),
        P("gz", "gy"),
        P("gy", "gx"),
        P("gz", "gy", "gx"),
        P("gz", "gy", "gx"),
    )
    out_specs = (P("gz", "gy", "gx"), P("gz", "gy", "gx"))
    return jax.shard_map(body, mesh=mesh, in_specs=in_specs, out_specs=out_specs, check_vma=False)
```

profile of v0, /device:TPU:0, one launch (start us, length us, event | category | flops | bytes accessed | tf_op | source)
XLA Modules:
  0.0 75.8 jit_solution(11789739191409745582)
XLA Ops:
  0.6 4.6 %outer_row_sums.1 = (f32[64,1024]{1,0:T(8,128)}, f32[64,1024]{1,0:T(8,128)}, f32[2,2,128]{2,1,0:T(2,128)}) custom-call(s32[8,32]{1,0:T(8,128)} %bitcast.20, f32[2,256,1024]{2,1,0:T(8,128)} %bitcast.17), custom_call_target="tpu_custom_call" | custom-call | flops 1 | bytes 1 | tf_op jit(solution)/shard_map/outer_row_sums/pallas_call | solution.py:504
  5.3 3.0 %collective-permute-start = (f32[64,1024]{1,0:T(8,128)}, f32[64,1024]{1,0:T(8,128)S(1)}, u32[]{:S(2)}, u32[]{:S(2)}) collective-permute-start(f32[64,1024]{1,0:T(8,128)} %get-tuple-element.59), channel_id=1, source_target_pairs={{0,16},{16,0},{1,17},{17,1},{2,18},{18,2},{3,19},{19,3},{4,20},{20... | collective-permute-start | bytes 786440 | tf_op jit(solution)/shard_map/ppermute | solution.py:1021
  8.3 5.1 %inner_row_sums.1 = (f32[96,1024]{1,0:T(8,128)}, f32[96,1024]{1,0:T(8,128)}, f32[2,3,128]{2,1,0:T(4,128)}) custom-call(s32[8,32]{1,0:T(8,128)} %bitcast.21, f32[2,256,1024]{2,1,0:T(8,128)} %bitcast.18), custom_call_target="tpu_custom_call" | custom-call | flops 1073741824 | bytes 1 | tf_op jit(solution)/shard_map/inner_row_sums/pallas_call | solution.py:504
  13.7 1.1 %collective-permute-done.other.refs_1_ = f32[64,1024]{1,0:T(8,128)S(1)} collective-permute-done((f32[64,1024]{1,0:T(8,128)}, f32[64,1024]{1,0:T(8,128)S(1)}, u32[]{:S(2)}, u32[]{:S(2)}) %collective-permute-start) | collective-permute-done | bytes 262176 | tf_op jit(solution)/shard_map/ppermute | solution.py:1021
  14.8 1.2 %outer_field.1 = (f32[64,1024]{1,0:T(8,128)S(1)}, f32[64,1024]{1,0:T(8,128)S(1)}, f32[8,128]{1,0:T(8,128)S(1)}) custom-call(s32[17]{0:T(128)S(1)} %stack.75.flags, f32[64,1024]{1,0:T(8,128)S(1)} %copy-done.3, f32[64,1024]{1,0:T(8,128)S(1)} %collective-permute-done.other.refs_1_, f32[32,8,1024]{2,1,0:T(8,128)S(1)} %copy-done), custom_call_target="tpu_custom_call" | custom-call | flops 1 | bytes 1 | tf_op jit(solution)/shard_map/outer_field/pallas_call | solution.py:504
  16.1 0.8 %collective-permute-start.3 = (f32[64,1024]{1,0:T(8,128)S(1)}, f32[64,1024]{1,0:T(8,128)S(1)}, u32[]{:S(2)}, u32[]{:S(2)}) collective-permute-start(f32[64,1024]{1,0:T(8,128)S(1)} %get-tuple-element.64.refs_5_), channel_id=1, source_target_pairs={{1,2},{2,1},{5,6},{6,5},{9,10},{10,9},{13,14},{14,13},{17,18},{18,... | collective-permute-start | bytes 786440 | tf_op jit(solution)/shard_map/ppermute | solution.py:943
  16.9 5.2 %last_row_sums.1 = (f32[96,640]{1,0:T(8,128)}, f32[96,384]{1,0:T(8,128)}, f32[96,1024]{1,0:T(8,128)}, f32[8,128]{1,0:T(8,128)}, f32[8,128]{1,0:T(8,128)}) custom-call(s32[8,32]{1,0:T(8,128)} %bitcast.22, f32[2,2,128]{2,1,0:T(2,128)} %get-tuple-element.65.outer_kept, f32[2,3,128]{2,1,0:T(4,128)} %get-tuple-element.66.inner_kept, f32[2,256,1024]{2,1,0:T(8,128)} %bitcast.19), custom_call_target="tpu_custom_call" | custom-call | flops 1073741824 | bytes 1 | tf_op jit(solution)/shard_map/last_row_sums/pallas_call | solution.py:504
  22.2 2.0 %collective-permute-start.6 = (f32[96,640]{1,0:T(8,128)}, f32[96,640]{1,0:T(8,128)S(1)}, u32[]{:S(2)}, u32[]{:S(2)}) collective-permute-start(f32[96,640]{1,0:T(8,128)} %get-tuple-element.72), channel_id=1, source_target_pairs={{0,16},{16,0},{1,17},{17,1},{2,18},{18,2},{3,19},{19,3},{4,20},{20... | collective-permute-start | bytes 737288 | tf_op jit(solution)/shard_map/ppermute | solution.py:1036
  24.3 4.9 %collective-permute-done.4.refs_9_ = f32[8,128]{1,0:T(8,128)S(1)} collective-permute-done((f32[8,128]{1,0:T(8,128)}, f32[8,128]{1,0:T(8,128)S(1)}, u32[]{:S(2)}, u32[]{:S(2)}) %collective-permute-start.4) | collective-permute-done | bytes 4128 | tf_op jit(solution)/shard_map/ppermute | solution.py:1035
  29.2 2.4 %collective-permute-start.5 = (f32[96,384]{1,0:T(8,128)}, f32[96,384]{1,0:T(8,128)S(1)}, u32[]{:S(2)}, u32[]{:S(2)}) collective-permute-start(f32[96,384]{1,0:T(8,128)} %get-tuple-element.71), channel_id=1, source_target_pairs={{0,16},{16,0},{1,17},{17,1},{2,18},{18,2},{3,19},{19,3},{4,20},{20... | collective-permute-start | bytes 442376 | tf_op jit(solution)/shard_map/ppermute | solution.py:1036
  31.7 0.7 copy-done.6
  32.4 0.7 wide_field.1
  33.1 1.5 %first_field.1 = (f32[32,8,640]{2,1,0:T(8,128)S(1)}, f32[32,8,640]{2,1,0:T(8,128)S(1)}, f32[8,128]{1,0:T(8,128)S(1)}, f32[8,128]{1,0:T(8,128)S(1)}, f32[8,128]{1,0:T(8,128)S(1)}) custom-call(s32[17]{0:T(128)S(1)} %stack.75.flags, f32[160,1024]{1,0:T(8,128)S(1)} %get-tuple-element.69.refs_0_, f32[96,1024]{1,0:T(8,128)S(1)} %copy-done.2, ...), custom_call_target="tpu_custom_call" | custom-call | flops 1 | bytes 1 | tf_op jit(solution)/shard_map/first_field/pallas_call | solution.py:504
  34.6 1.2 %collective-permute-done.7.refs_10_ = f32[8,128]{1,0:T(8,128)S(1)} collective-permute-done((f32[8,128]{1,0:T(8,128)S(1)}, f32[8,128]{1,0:T(8,128)S(1)}, u32[]{:S(2)}, u32[]{:S(2)}) %collective-permute-start.7) | collective-permute-done | bytes 4128 | tf_op jit(solution)/shard_map/ppermute | solution.py:944
  35.8 2.8 %first_sweep.2 = (f32[32,8,512]{2,1,0:T(8,128)S(1)}, f32[32,8,512]{2,1,0:T(8,128)S(1)}, f32[8,128]{1,0:T(8,128)S(1)}, f32[32,8,512]{2,1,0:T(8,128)S(1)}, f32[32,...) custom-call(s32[17]{0:T(128)S(1)} %stack.75.flags, ...), custom_call_target="tpu_custom_call" | custom-call | flops 1 | bytes 1 | tf_op jit(solution)/shard_map/first_sweep/pallas_call | solution.py:504
  38.5 1.8 %collective-permute-start.8 = (f32[5,8,512]{2,1,0:T(8,128)S(1)}, f32[5,8,512]{2,1,0:T(8,128)S(1)}, u32[]{:S(2)}, u32[]{:S(2)}) collective-permute-start(f32[5,8,512]{2,1,0:T(8,128)S(1)} %get-tuple-element.83.own_one), channel_id=1, source_target_pairs={{0,4},{4,0},{8,12},{12,8},{1,5},{5,1},{9,13},{13,9},{2,6},{6,2},{1... | collective-permute-start | bytes 245768 | tf_op jit(solution)/shard_map/ppermute | solution.py:1080
  40.3 1.9 %second_field.1 = (f32[32,8,1024]{2,1,0:T(8,128)}, f32[32,8,512]{2,1,0:T(8,128)S(1)}) custom-call(s32[17]{0:T(128)S(1)} %stack.75.flags, f32[160,1024]{1,0:T(8,128)S(1)} %get-tuple-element.69.refs_0_, f32[96,1024]{1,0:T(8,128)S(1)} %copy-done.2, f32[96,384]{1,0:T(8,128)S(1)} %collective-permute-done.5.refs_2_, f32[32,8,640]{2,1,0:T(8,128)S(1)} %get-tuple-element.85.refs_3_, ...), custom_call_target="tpu_custom_call" | custom-call | flops 1 | bytes 1 | tf_op jit(solution)/shard_map/second_field/pallas_call | solution.py:504
  42.3 2.7 %first_sweep.3 = (f32[32,8,512]{2,1,0:T(8,128)S(1)}, f32[32,8,512]{2,1,0:T(8,128)S(1)}, f32[8,128]{1,0:T(8,128)S(1)}, f32[32,8,512]{2,1,0:T(8,128)S(1)}, f32[32,...) custom-call(s32[17]{0:T(128)S(1)} %stack.75.flags, ...), custom_call_target="tpu_custom_call" | custom-call | flops 1 | bytes 1 | tf_op jit(solution)/shard_map/first_sweep/pallas_call | solution.py:504
  45.0 0.4 collective-permute-start.9
  45.4 4.3 %collective-permute-done.9.near_two = f32[5,8,512]{2,1,0:T(8,128)S(1)} collective-permute-done((f32[5,8,512]{2,1,0:T(8,128)S(1)}, f32[5,8,512]{2,1,0:T(8,128)S(1)}, u32[]{:S(2)}, u32[]{:S(2)}) %collective-permute-start.9) | collective-permute-done | bytes 81952 | tf_op jit(solution)/shard_map/ppermute | solution.py:1091
  49.7 0.6 join_pair.1
  50.3 2.7 %collective-permute-start.10 = (f32[2,8,1024]{2,1,0:T(8,128)S(1)}, f32[2,8,1024]{2,1,0:T(8,128)S(1)}, u32[]{:S(2)}, u32[]{:S(2)}) collective-permute-start(f32[2,8,1024]{2,1,0:T(8,128)S(1)} %get-tuple-element.89.refs_0_), channel_id=1, source_target_pairs={{0,8},{8,0},{4,12},{12,4},{1,9},{9,1},{5,13},{13,5},{2,10},{10,2},... | collective-permute-start | bytes 196616 | tf_op jit(solution)/shard_map/ppermute | solution.py:1099
  53.0 3.1 %collective-permute-done.10.refs_1_ = f32[2,8,1024]{2,1,0:T(8,128)S(1)} collective-permute-done((f32[2,8,1024]{2,1,0:T(8,128)S(1)}, f32[2,8,1024]{2,1,0:T(8,128)S(1)}, u32[]{:S(2)}, u32[]{:S(2)}) %collective-permute-start.10) | collective-permute-done | bytes 65568 | tf_op jit(solution)/shard_map/ppermute | solution.py:1099
  56.1 2.4 %half.1 = (f32[32,8,1024]{2,1,0:T(8,128)S(1)}, f32[32,1024]{1,0:T(8,128)S(1)}, f32[32,1024]{1,0:T(8,128)S(1)}, f32[8,128]{1,0:T(8,128)S(1)}, f32[8,1024]{1,0:T(8,128)S(1)}) custom-call(s32[17]{0:T(128)S(1)} %stack.75.flags, f32[2,8,1024]{2,1,0:T(8,128)S(1)} %get-tuple-element.89.refs_0_, f32[2,8,1024]{2,1,0:T(8,128)S(1)} %collective-permute-done.10.refs_1_, ...), custom_call_target="tpu_custom_call" | custom-call | flops 1 | bytes 1 | tf_op jit(solution)/shard_map/half/pallas_call | solution.py:504
  58.4 0.7 collective-permute-start.12
  59.1 1.8 %collective-permute-start.13 = (f32[8,128]{1,0:T(8,128)S(1)}, f32[8,128]{1,0:T(8,128)S(1)}, u32[]{:S(2)}, u32[]{:S(2)}) collective-permute-start(f32[8,128]{1,0:T(8,128)S(1)} %get-tuple-element.102), channel_id=1, source_target_pairs={{0,16},{16,0},{1,17},{17,1},{2,18},{18,2},{3,19},{19,3},{4,20},{20... | collective-permute-start | bytes 12296 | tf_op jit(solution)/shard_map/ppermute | solution.py:944
  60.9 1.9 %collective-permute-done.13.refs_3_ = f32[8,128]{1,0:T(8,128)S(1)} collective-permute-done((f32[8,128]{1,0:T(8,128)S(1)}, f32[8,128]{1,0:T(8,128)S(1)}, u32[]{:S(2)}, u32[]{:S(2)}) %collective-permute-start.13) | collective-permute-done | bytes 4128 | tf_op jit(solution)/shard_map/ppermute | solution.py:944
  62.8 2.8 %second_sweep.1 = (f32[32,8,512]{2,1,0:T(8,128)S(1)}, f32[32,8,512]{2,1,0:T(8,128)S(1)}, f32[2,8,1024]{2,1,0:T(8,128)S(1)}, f32[8,1024]{1,0:T(8,128)S(1)}) custom-call(s32[17]{0:T(128)S(1)} %stack.75.flags, f32[32,8,1024]{2,1,0:T(8,128)S(1)} %get-tuple-element.99.refs_0_.refs_14_, f32[32,1024]{1,0:T(8,128)S(1)} %collective-permute-done.11.refs_1_, ...), custom_call_target="tpu_custom_call" | custom-call | flops 1 | bytes 1 | tf_op jit(solution)/shard_map/second_sweep/pallas_call | solution.py:504
  65.6 3.5 %collective-permute-start.16 = (f32[8,1024]{1,0:T(8,128)S(1)}, f32[8,1024]{1,0:T(8,128)S(1)}, u32[]{:S(2)}, u32[]{:S(2)}) collective-permute-start(f32[8,1024]{1,0:T(8,128)S(1)} %get-tuple-element.110), channel_id=1, source_target_pairs={{0,12},{12,0},{4,8},{8,4},{1,13},{13,1},{5,9},{9,5},{2,14},{14,2},... | collective-permute-start | bytes 98312 | tf_op jit(solution)/shard_map/ppermute | solution.py:1118
  69.1 2.6 %collective-permute-done.16.refs_3_ = f32[8,1024]{1,0:T(8,128)S(1)} collective-permute-done((f32[8,1024]{1,0:T(8,128)S(1)}, f32[8,1024]{1,0:T(8,128)S(1)}, u32[]{:S(2)}, u32[]{:S(2)}) %collective-permute-start.16) | collective-permute-done | bytes 32800 | tf_op jit(solution)/shard_map/ppermute | solution.py:1118
  71.7 2.2 %collective-permute-done.15.refs_2_ = f32[8,1024]{1,0:T(8,128)S(1)} collective-permute-done((f32[8,1024]{1,0:T(8,128)S(1)}, f32[8,1024]{1,0:T(8,128)S(1)}, u32[]{:S(2)}, u32[]{:S(2)}) %collective-permute-start.15) | collective-permute-done | bytes 32800 | tf_op jit(solution)/shard_map/ppermute | solution.py:1118
  73.9 1.9 %smoothed.1 = f32[32,8,1024]{2,1,0:T(8,128)} custom-call(s32[17]{0:T(128)S(1)} %stack.75.flags, f32[2,8,1024]{2,1,0:T(8,128)S(1)} %get-tuple-element.109.refs_0_, f32[2,8,1024]{2,1,0:T(8,128)S(1)} %collective-permute-done.14.refs_1_, f32[8,1024]{1,0:T(8,128)S(1)} %collective-permute-done.15.refs_2_, f32[8,1024]{1,0:T(8,128)S(1)} %collective-permute-done.16.refs_3_, ...), custom_call_target="tpu_custom_call" | custom-call | flops 1 | bytes 1 | tf_op jit(solution)/shard_map/smoothed/pallas_call | solution.py:504
  (30 shorter events, 0.6 us)
Async XLA Ops:
  5.3 9.6 %copy-start = (f32[32,8,1024]{2,1,0:T(8,128)S(1)}, f32[32,8,1024]{2,1,0:T(8,128)}, u32[]{:S(2)}) copy-start(f32[32,8,1024]{2,1,0:T(8,128)} %refs_11_.5) | copy-start | bytes 3145732
  5.3 9.6 %copy-start.3 = (f32[64,1024]{1,0:T(8,128)S(1)}, f32[64,1024]{1,0:T(8,128)}, u32[]{:S(2)}) copy-start(f32[64,1024]{1,0:T(8,128)} %get-tuple-element.58.own.refs_0_) | copy-start | bytes 786436
  5.3 9.5 %collective-permute-start = (f32[64,1024]{1,0:T(8,128)}, f32[64,1024]{1,0:T(8,128)S(1)}, u32[]{:S(2)}, u32[]{:S(2)}) collective-permute-start(f32[64,1024]{1,0:T(8,128)} %get-tuple-element.59), channel_id=1, source_target_pairs={{0,16},{16,0},{1,17},{17,1},{2,18},{18,2},{3,19},{19,3},{4,20},{20... | collective-permute-start | bytes 786440 | tf_op jit(solution)/shard_map/ppermute | solution.py:1021
  13.5 18.2 %collective-permute-start.1 = (f32[96,1024]{1,0:T(8,128)}, f32[96,1024]{1,0:T(8,128)S(1)}, u32[]{:S(2)}, u32[]{:S(2)}) collective-permute-start(f32[96,1024]{1,0:T(8,128)} %get-tuple-element.62), channel_id=1, source_target_pairs={{0,16},{16,0},{1,17},{17,1},{2,18},{18,2},{3,19},{19,3},{4,20},{20... | collective-permute-start | bytes 1179656 | tf_op jit(solution)/shard_map/ppermute | solution.py:1024
  16.0 15.6 %copy-start.4 = (f32[96,1024]{1,0:T(8,128)S(1)}, f32[96,1024]{1,0:T(8,128)}, u32[]{:S(2)}) copy-start(f32[96,1024]{1,0:T(8,128)} %get-tuple-element.61.refs_2_) | copy-start | bytes 1179652
  16.0 15.6 %collective-permute-start.2 = (f32[64,1024]{1,0:T(8,128)S(1)}, f32[64,1024]{1,0:T(8,128)S(1)}, u32[]{:S(2)}, u32[]{:S(2)}) collective-permute-start(f32[64,1024]{1,0:T(8,128)S(1)} %get-tuple-element.63.refs_4_), channel_id=1, source_target_pairs={{0,1},{1,0},{2,3},{3,2},{4,5},{5,4},{6,7},{7,6},{8,9},{9,8},{10,11... | collective-permute-start | bytes 786440 | tf_op jit(solution)/shard_map/ppermute | solution.py:942
  16.1 15.5 %collective-permute-start.3 = (f32[64,1024]{1,0:T(8,128)S(1)}, f32[64,1024]{1,0:T(8,128)S(1)}, u32[]{:S(2)}, u32[]{:S(2)}) collective-permute-start(f32[64,1024]{1,0:T(8,128)S(1)} %get-tuple-element.64.refs_5_), channel_id=1, source_target_pairs={{1,2},{2,1},{5,6},{6,5},{9,10},{10,9},{13,14},{14,13},{17,18},{18,... | collective-permute-start | bytes 786440 | tf_op jit(solution)/shard_map/ppermute | solution.py:943
  22.2 10.9 %copy-start.2 = (f32[96,1024]{1,0:T(8,128)S(1)}, f32[96,1024]{1,0:T(8,128)}, u32[]{:S(2)}) copy-start(f32[96,1024]{1,0:T(8,128)} %get-tuple-element.70.refs_1_) | copy-start | bytes 1179652
  22.2 13.6 %copy-start.1 = (f32[32,8,1024]{2,1,0:T(8,128)S(1)}, f32[32,8,1024]{2,1,0:T(8,128)}, u32[]{:S(2)}) copy-start(f32[32,8,1024]{2,1,0:T(8,128)} %refs_4_.1) | copy-start | bytes 3145732
  22.2 10.9 %collective-permute-start.6 = (f32[96,640]{1,0:T(8,128)}, f32[96,640]{1,0:T(8,128)S(1)}, u32[]{:S(2)}, u32[]{:S(2)}) collective-permute-start(f32[96,640]{1,0:T(8,128)} %get-tuple-element.72), channel_id=1, source_target_pairs={{0,16},{16,0},{1,17},{17,1},{2,18},{18,2},{3,19},{19,3},{4,20},{20... | collective-permute-start | bytes 737288 | tf_op jit(solution)/shard_map/ppermute | solution.py:1036
  24.2 5.0 %collective-permute-start.4 = (f32[8,128]{1,0:T(8,128)}, f32[8,128]{1,0:T(8,128)S(1)}, u32[]{:S(2)}, u32[]{:S(2)}) collective-permute-start(f32[8,128]{1,0:T(8,128)} %get-tuple-element.68), channel_id=1, source_target_pairs={{0,16},{16,0},{1,17},{17,1},{2,18},{18,2},{3,19},{19,3},{4,20},{20... | collective-permute-start | bytes 12296 | tf_op jit(solution)/shard_map/ppermute | solution.py:1035
  29.2 11.1 %collective-permute-start.5 = (f32[96,384]{1,0:T(8,128)}, f32[96,384]{1,0:T(8,128)S(1)}, u32[]{:S(2)}, u32[]{:S(2)}) collective-permute-start(f32[96,384]{1,0:T(8,128)} %get-tuple-element.71), channel_id=1, source_target_pairs={{0,16},{16,0},{1,17},{17,1},{2,18},{18,2},{3,19},{19,3},{4,20},{20... | collective-permute-start | bytes 442376 | tf_op jit(solution)/shard_map/ppermute | solution.py:1036
  31.6 4.2 %collective-permute-start.7 = (f32[8,128]{1,0:T(8,128)S(1)}, f32[8,128]{1,0:T(8,128)S(1)}, u32[]{:S(2)}, u32[]{:S(2)}) collective-permute-start(f32[8,128]{1,0:T(8,128)S(1)} %get-tuple-element.82), channel_id=1, source_target_pairs={{0,16},{16,0},{1,17},{17,1},{2,18},{18,2},{3,19},{19,3},{4,20},{20... | collective-permute-start | bytes 12296 | tf_op jit(solution)/shard_map/ppermute | solution.py:944
  31.7 0.7 copy-start.6
  38.5 6.9 %collective-permute-start.8 = (f32[5,8,512]{2,1,0:T(8,128)S(1)}, f32[5,8,512]{2,1,0:T(8,128)S(1)}, u32[]{:S(2)}, u32[]{:S(2)}) collective-permute-start(f32[5,8,512]{2,1,0:T(8,128)S(1)} %get-tuple-element.83.own_one), channel_id=1, source_target_pairs={{0,4},{4,0},{8,12},{12,8},{1,5},{5,1},{9,13},{13,9},{2,6},{6,2},{1... | collective-permute-start | bytes 245768 | tf_op jit(solution)/shard_map/ppermute | solution.py:1080
  42.3 13.8 %copy-start.5 = (s32[8,1024]{1,0:T(8,128)S(1)}, s32[8,1024]{1,0:T(8,128)}, u32[]{:S(2)}) copy-start(s32[8,1024]{1,0:T(8,128)} %refs_15_.1) | copy-start | bytes 98308
  45.0 4.7 %collective-permute-start.9 = (f32[5,8,512]{2,1,0:T(8,128)S(1)}, f32[5,8,512]{2,1,0:T(8,128)S(1)}, u32[]{:S(2)}, u32[]{:S(2)}) collective-permute-start(f32[5,8,512]{2,1,0:T(8,128)S(1)} %get-tuple-element.88.own_two), channel_id=1, source_target_pairs={{0,4},{4,0},{8,12},{12,8},{1,5},{5,1},{9,13},{13,9},{2,6},{6,2},{1... | collective-permute-start | bytes 245768 | tf_op jit(solution)/shard_map/ppermute | solution.py:1091
  50.3 5.8 %collective-permute-start.10 = (f32[2,8,1024]{2,1,0:T(8,128)S(1)}, f32[2,8,1024]{2,1,0:T(8,128)S(1)}, u32[]{:S(2)}, u32[]{:S(2)}) collective-permute-start(f32[2,8,1024]{2,1,0:T(8,128)S(1)} %get-tuple-element.89.refs_0_), channel_id=1, source_target_pairs={{0,8},{8,0},{4,12},{12,4},{1,9},{9,1},{5,13},{13,5},{2,10},{10,2},... | collective-permute-start | bytes 196616 | tf_op jit(solution)/shard_map/ppermute | solution.py:1099
  58.4 4.3 %collective-permute-start.11 = (f32[32,1024]{1,0:T(8,128)S(1)}, f32[32,1024]{1,0:T(8,128)S(1)}, u32[]{:S(2)}, u32[]{:S(2)}) collective-permute-start(f32[32,1024]{1,0:T(8,128)S(1)} %get-tuple-element.100), channel_id=1, source_target_pairs={{0,1},{1,0},{2,3},{3,2},{4,5},{5,4},{6,7},{7,6},{8,9},{9,8},{10,11... | collective-permute-start | bytes 393224 | tf_op jit(solution)/shard_map/ppermute | solution.py:942
  58.4 4.3 %collective-permute-start.12 = (f32[32,1024]{1,0:T(8,128)S(1)}, f32[32,1024]{1,0:T(8,128)S(1)}, u32[]{:S(2)}, u32[]{:S(2)}) collective-permute-start(f32[32,1024]{1,0:T(8,128)S(1)} %get-tuple-element.101), channel_id=1, source_target_pairs={{1,2},{2,1},{5,6},{6,5},{9,10},{10,9},{13,14},{14,13},{17,18},{18,... | collective-permute-start | bytes 393224 | tf_op jit(solution)/shard_map/ppermute | solution.py:943
  59.1 3.7 %collective-permute-start.13 = (f32[8,128]{1,0:T(8,128)S(1)}, f32[8,128]{1,0:T(8,128)S(1)}, u32[]{:S(2)}, u32[]{:S(2)}) collective-permute-start(f32[8,128]{1,0:T(8,128)S(1)} %get-tuple-element.102), channel_id=1, source_target_pairs={{0,16},{16,0},{1,17},{17,1},{2,18},{18,2},{3,19},{19,3},{4,20},{20... | collective-permute-start | bytes 12296 | tf_op jit(solution)/shard_map/ppermute | solution.py:944
  65.5 8.4 %collective-permute-start.14 = (f32[2,8,1024]{2,1,0:T(8,128)S(1)}, f32[2,8,1024]{2,1,0:T(8,128)S(1)}, u32[]{:S(2)}, u32[]{:S(2)}) collective-permute-start(f32[2,8,1024]{2,1,0:T(8,128)S(1)} %get-tuple-element.109.refs_0_), channel_id=1, source_target_pairs={{0,4},{4,0},{8,12},{12,8},{1,5},{5,1},{9,13},{13,9},{2,6},{6,2},{1... | collective-permute-start | bytes 196616 | tf_op jit(solution)/shard_map/ppermute | solution.py:1118
  65.6 6.1 %collective-permute-start.16 = (f32[8,1024]{1,0:T(8,128)S(1)}, f32[8,1024]{1,0:T(8,128)S(1)}, u32[]{:S(2)}, u32[]{:S(2)}) collective-permute-start(f32[8,1024]{1,0:T(8,128)S(1)} %get-tuple-element.110), channel_id=1, source_target_pairs={{0,12},{12,0},{4,8},{8,4},{1,13},{13,1},{5,9},{9,5},{2,14},{14,2},... | collective-permute-start | bytes 98312 | tf_op jit(solution)/shard_map/ppermute | solution.py:1118
  69.1 4.8 %collective-permute-start.15 = (f32[8,1024]{1,0:T(8,128)S(1)}, f32[8,1024]{1,0:T(8,128)S(1)}, u32[]{:S(2)}, u32[]{:S(2)}) collective-permute-start(f32[8,1024]{1,0:T(8,128)S(1)} %get-tuple-element.110), channel_id=1, source_target_pairs={{0,8},{8,0},{4,12},{12,4},{1,9},{9,1},{5,13},{13,5},{2,10},{10,2},... | collective-permute-start | bytes 98312 | tf_op jit(solution)/shard_map/ppermute | solution.py:1118
where the time goes:
time: 77 us; the launch traced here: 75.8 us
  Pallas kernels  33.3 us (43%)
  waiting for transfers between devices  21.4 us (28%)
  starting transfers between devices  19.5 us (25%)
  between operations  0.82 us (1%)
  local copies, waits for them, and re-layouts  0.79 us (1%)
    pallas_call x13, Pallas kernels, call(): pl.pallas_call(kernel, out_shape=out_shape, in_specs=specs, out_specs=jax...  33.3 us
    ppermute x1, waiting for transfers between devices, fast_body(): column_sums = [theirs, lax.ppermute(mine, 'gx', PAIR)]  4.92 us
    ppermute x3, waiting for transfers between devices, fast_body(): lax.ppermute(planes, 'gz', pairs)  4.81 us
    ppermute x2, starting transfers between devices, fast_body(): lax.ppermute(piece, 'gx', PAIR)  4.45 us
    ppermute x1, waiting for transfers between devices, fast_body(): near_two = lax.ppermute(reduced_two, 'gz', NEAR)  4.32 us
    ppermute x3, starting transfers between devices, fast_body(): lax.ppermute(planes, 'gz', pairs)  3.58 us
    ppermute x2, waiting for transfers between devices, exchange_edges(): lax.ppermute(piece, 'gx', PAIR)  3.11 us
    ppermute x1, waiting for transfers between devices, fast_body(): other = lax.ppermute(across, 'gz', SKIP)  3.1 us
  transfers between devices with their start and end apart: 17, of which 8 were waited for; matrix products, arithmetic and copies ran while one was open for 0% of the time, Pallas kernels for 28%

commit v1 on v0

--- a/solution.py
+++ b/solution.py
@@ -329,7 +329,8 @@
     diagonal = diagonal_of(depth)
     for at in range(len(ys)):
         rows = slice(at * depth, (at + 1) * depth)
-        for side, lane in enumerate((LANES - 1, 0)):
+        for side in range(edges.shape[0]):
+            lane = 0 if side % 2 else LANES - 1
             column = jnp.broadcast_to(edges[side, rows, lane : lane + 1], (depth, depth))
             row = jnp.sum(jnp.where(diagonal, column, 0.0), axis=0, keepdims=True)
             kept[side, at : at + 1, :depth] = row
@@ -418,8 +419,9 @@
 
 
 def keep_edges(rows, tiles, edges):
-    half = len(tiles) // 2
-    edges[0, rows], edges[1, rows] = tiles[half - 1], tiles[half]
+    count = len(tiles) // 4
+    for side in range(edges.shape[0]):
+        edges[side, rows] = tiles[(side // 2 + 1) * count - 1 + side % 2]
 
 
 def wide_sums_kernel(ys, shifts, spectral, other, own, kept, *refs):
@@ -448,8 +450,8 @@
     edge_columns(ys, depth, edges, kept)
 
 
-def last_sums_kernel(ys, shifts, outer_kept, inner_kept, spectral, one, two, own, *refs):
-    mine, theirs, kept, columns, edges, coefficients, arrivals, *tables, left, right = refs
+def last_sums_kernel(ys, shifts, outer_kept, inner_kept, p_column, spectral, one, two, own, *refs):
+    columns_own, kept, columns, edges, coefficients, arrivals, *tables, left, right = refs
     items, depth = shifts.shape
     copies = load_coefficients(spectral, coefficients, arrivals)
     fill_tables(*tables)
@@ -484,10 +486,18 @@
         jnp.concatenate(
             [outer_kept[side, :1], inner_kept[side], kept[side], outer_kept[side, 1:]], axis=0
         )
-        for side in range(2)
+        for side in range(6)
     ]
-    mine[...] = jnp.where(g == 0, sides_of[0], sides_of[1])
-    theirs[...] = jnp.where(g == 0, sides_of[1], sides_of[0])
+    low, high = sides_of[:3], sides_of[3:]
+    own_sides = [jnp.where(g == 0, *pair) for pair in ((low[0], high[1]), (low[1], high[2]))]
+    own_sides.append(jnp.where(g == 0, low[2], high[0]))
+    other_sides = [jnp.where(g == 0, *pair) for pair in ((high[1], low[0]), (high[2], low[1]))]
+    other_sides.append(jnp.where(g == 0, high[0], low[2]))
+    for at in range(3):
+        columns_own[at], columns_own[3 + at] = own_sides[at], other_sides[at]
+    extra = slice(one.shape[0] - ROWS, one.shape[0])
+    for at, piece in enumerate((*other_sides, own_sides[2], p_column[...])):
+        one[extra, at * LANES : (at + 1) * LANES] = piece
 
 
 SCALARS = pl.BlockSpec(memory_space=pltpu.SMEM)
@@ -570,8 +580,9 @@
 
 def wide_field_kernel(depth, flags, *refs):
     own_outer, outer, own_inner, inner, to_near, to_middle = refs[:6]
-    from_near, from_middle, sums_here, sums_there = refs[6:10]
-    wide, south_weight, north_weight, south_terms, north_rows, column = refs[10:]
+    from_near, from_middle, pressure = refs[6:9]
+    wide, south_weight, north_weight, p_south, p_north, p_west, p_east = refs[9:16]
+    south_rows, north_rows = refs[16:]
     even = flags[16] == 0
     low, high = slice(0, depth), slice(depth, 2 * depth)
     wide[low] = own_outer[low] + outer[low]
@@ -582,9 +593,19 @@
     south = jnp.where(even, middle_weight, near_weight)
     south_weight[...] = south
     north_weight[...] = jnp.where(even, near_weight, middle_weight)
-    south_terms[...] = south * jnp.where(even, from_middle[high], from_near[high])
+    south_rows[...] = jnp.where(even, from_middle[high], from_near[high])
     north_rows[...] = jnp.where(even, from_near[high], from_middle[high])
-    column[...] = jnp.exp(-(sums_here[...] + sums_there[...]))
+    row = row_of(pressure.shape[1:])
+
+    def layer(z, carry):
+        plane = pressure[z]
+        p_south[z] = jnp.where(row == 0, south_rows[pl.ds(z, 1), :], roll(plane, 1, 0))
+        p_north[z] = jnp.where(row == ROWS - 1, north_rows[pl.ds(z, 1), :], roll(plane, -1, 0))
+        p_west[z] = roll(plane, 1, 1)
+        p_east[z] = roll(plane, -1, 1)
+        return carry
+
+    lax.fori_loop(0, depth, layer, 0, unroll=4)
 
 
 def lane_slice(start, size):
@@ -594,42 +615,35 @@
 def assemble(sums, depth, wide, own, piece, there):
     inside = wide.shape[0] - depth
     place_tiles(sums, slice(0, inside), 0, wide[:inside, there])
-    place_tiles(sums, slice(inside, -depth), 0, own[:, there] + piece[...])
+    place_tiles(sums, slice(inside, -depth), 0, own[:, there] + piece[: own.shape[0]])
     place_tiles(sums, slice(-depth, None), 0, wide[inside:, there])
 
 
 def first_field_kernel(depth, flags, *refs):
-    wide, own, middle = refs[:3]
-    log_perm, resist, low_side, high_side, boundary, sums = refs[3:]
-    g, start = flags[0], flags[3]
-    assemble(sums, depth, wide, own, middle, lane_slice(start, log_perm.shape[2]))
-    edge = lane_slice(own.shape[1] // 2 - LANES - start, 2 * LANES)
+    wide, own, middle, columns_own = refs[:4]
+    log_perm, resist, low_side, high_side, boundary, column, p_column, sums = refs[4:]
+    extra = slice(own.shape[0], own.shape[0] + ROWS)
+    came = [middle[extra, at * LANES : (at + 1) * LANES] for at in range(5)]
+    for at, ref in enumerate((low_side, high_side, boundary)):
+        ref[...] = jnp.exp(-(columns_own[at] + came[at]))
+    column[...] = jnp.exp(-(columns_own[5] + came[3]))
+    p_column[...] = came[4]
+    assemble(sums, depth, wide, own, middle, lane_slice(flags[3], log_perm.shape[2]))
 
     def layer(z, carry):
-        low, high, bound = carry
         plane = ordered(z, sums, depth)
-        inverse = jnp.exp(-plane)
         log_perm[z] = plane
-        resist[z] = inverse
-        both = resist[z, :, edge]
-        return (
-            packed_with(z, low, both, LANES - 1),
-            packed_with(z, high, both, LANES),
-            packed_with(z, bound, boundary_plane(g, inverse), 0),
-        )
-
-    zero = jnp.zeros((ROWS, LANES), F32)
-    low_side[...], high_side[...], boundary[...] = lax.fori_loop(
-        0, depth, layer, (zero, zero, zero), unroll=8
-    )
+        resist[z] = jnp.exp(-plane)
+        return carry
+
+    lax.fori_loop(0, depth, layer, 0, unroll=8)
 
 
 def second_field_kernel(depth, flags, *refs):
-    wide, own, middle, log_near, resist_near = refs[:5]
-    log_perm, resist, sums = refs[5:]
-    third, known = middle.shape[1], log_near.shape[2]
-    there = lane_slice(flags[5], third)
-    assemble(sums, depth, wide, own, middle, there)
+    wide, own, middle, resist_near = refs[:4]
+    log_perm, resist, sums = refs[4:]
+    third = middle.shape[1]
+    assemble(sums, depth, wide, own, middle, lane_slice(flags[5], third))
     extra = resist.shape[2] - third
     target = lane_slice(flags[5] - flags[7], third)
     extra_target = lane_slice(flags[8], extra)
@@ -637,10 +651,18 @@
 
     def layer(z, carry):
         plane = ordered(z, sums, depth)
-        log_perm[z, :, lane_slice(flags[3], known)] = log_near[z]
-        log_perm[z, :, there] = plane
+        log_perm[z] = plane
         resist[z, :, target] = jnp.exp(-plane)
         resist[z, :, extra_target] = resist_near[z, :, extra_source]
+        return carry
+
+    lax.fori_loop(0, depth, layer, 0, unroll=8)
+
+
+def join_columns_kernel(depth, flags, near, far, _, whole):
+    def layer(z, carry):
+        whole[z, :, lane_slice(flags[3], near.shape[2])] = near[z]
+        whole[z, :, lane_slice(flags[5], far.shape[2])] = far[z]
         return carry
 
     lax.fori_loop(0, depth, layer, 0, unroll=8)
@@ -691,11 +713,11 @@
 
 
 def first_sweep_kernel(depth, vert, block, flags, *refs):
-    resist, low_side, high_side, r_bound, r_column = refs[:5]
-    south_weight, north_weight, south_terms, north_rows = refs[5:9]
-    pressure, p_column, source = refs[9:12]
-    w_east, w_north, west_out, particular, inverse, ratio, lead, reduced = refs[12:20]
-    grounds, rights, verticals = refs[20:]
+    resist, low_side, high_side, r_bound, r_column, p_column = refs[:6]
+    south_weight, north_weight, p_south, p_north, p_west, p_east = refs[6:12]
+    source = refs[12]
+    w_east, w_north, west_out, particular, inverse, ratio, lead, reduced = refs[13:21]
+    grounds, rights, verticals = refs[21:]
     start, offset = flags[6 + block], flags[10 + block]
     size = inverse.shape[2]
     shape = (ROWS, size)
@@ -721,8 +743,16 @@
         verticals[z] = (2.0 * vert) * inverse_of(
             plane + resist[jnp.minimum(z + 1, depth - 1), :, inside]
         )
-        rights[z] = source[z, :, here] + coupling(
-            z, pressure, start, size, east, north, south_terms, north_rows, west_weight, column
+        p_first, p_last = p_west[z, :, here], p_east[z, :, here]
+        p_first = with_first(
+            p_first, jnp.where(start == 0, column_to(z, column, 0), p_first[:, :LANES])
+        )
+        p_last = with_last(
+            p_last, jnp.where(start == 0, p_last[:, -LANES:], column_to(z, column, LANES - 1))
+        )
+        rights[z] = source[z, :, here] + (
+            (west * p_first + east * p_last)
+            + (south * p_south[z, :, here] + north * p_north[z, :, here])
         )
         return carry
 
@@ -752,7 +782,7 @@
         depth - 1,
         layer,
         (grounds[0], rights[0], jnp.ones(shape, F32), zero, zero),
-        unroll=8,
+        unroll=True,
     )
     reciprocal = inverse_of(conduct)
     led = product * reciprocal
@@ -815,7 +845,7 @@
         )
         return values, emit(z, values, state)
 
-    return lax.fori_loop(1, depth, layer, (values, state), unroll=4)[1]
+    return lax.fori_loop(1, depth, layer, (values, state), unroll=True)[1]
 
 
 def half_kernel(depth, flags, *refs):
@@ -887,7 +917,7 @@
         return tuple(result)
 
     carry = tuple((local(0, block), jnp.zeros((ROWS, size), F32)) for block in range(2))
-    carry = lax.fori_loop(0, depth - 1, layer, carry, unroll=2)
+    carry = lax.fori_loop(0, depth - 1, layer, carry, unroll=True)
     last = depth - 1
     for block, (flow, first_part) in enumerate(carry):
         inverse, ratio, lead = blocks[block][3:6]
@@ -995,7 +1025,7 @@
     def scratch(count):
         return [
             pltpu.VMEM((count, LANES), jnp.int32),
-            pltpu.VMEM((2, count, LANES), F32),
+            pltpu.VMEM((6, count, LANES), F32),
             pltpu.VMEM((parts, 2, rows, LANES), F32),
             pltpu.SemaphoreType.DMA((parts,)),
             pltpu.VMEM((3, 2 * LANES, LANES), jnp.bfloat16),
@@ -1008,7 +1038,7 @@
         return call(
             functools.partial(wide_sums_kernel, ys),
             name,
-            [shaped(len(ys) * depth, width)] * 2 + [shaped(2, len(ys), LANES)],
+            [shaped(len(ys) * depth, width)] * 2 + [shaped(6, len(ys), LANES)],
             [shift_rows],
             scratch=scratch(len(ys) * depth),
             far=[coefficients],
@@ -1022,18 +1052,6 @@
     shift_rows, _ = lax.optimization_barrier((shift_rows, own_outer))
     sums, own_inner, inner_kept = wide_sums(inner_ys, "inner_row_sums", shift_rows, 1 << 30)
     inner = lax.ppermute(sums, "gx", PAIR)
-    last_one, last_two, own_last, mine, theirs = call(
-        functools.partial(last_sums_kernel, last_ys),
-        "last_row_sums",
-        [shaped(last_rows, size) for size in (known, third, width)] + [column_type] * 2,
-        [shift_rows, outer_kept, inner_kept],
-        scratch=[pltpu.VMEM((2, len(last_ys), LANES), F32)] + scratch(last_rows),
-        far=[coefficients],
-        mib=SUMS_GRANT,
-        flops=1 << 30,
-    )
-    column_sums = [theirs, lax.ppermute(mine, "gx", PAIR)]
-    last_one, last_two = (lax.ppermute(piece, "gx", PAIR) for piece in (last_one, last_two))
     edge_row, edge_column = shaped(depth, width), shaped(ROWS, LANES)
     edges = [edge_row, edge_row, edge_column]
     to_near, to_middle, p_column = call(
@@ -1043,22 +1061,38 @@
         [own_outer, outer, pressure],
         flags,
     )
-    from_near, from_middle, p_column = exchange_edges([to_near, to_middle, p_column])
-    wide, *row_edges, r_column = call(
+    from_near, from_middle = exchange_edges([to_near, to_middle])
+    last_one, last_two, own_last, own_columns = call(
+        functools.partial(last_sums_kernel, last_ys),
+        "last_row_sums",
+        [
+            shaped(last_rows + ROWS, known),
+            shaped(last_rows, third),
+            shaped(last_rows, width),
+            shaped(6, ROWS, LANES),
+        ],
+        [shift_rows, outer_kept, inner_kept, p_column],
+        scratch=[pltpu.VMEM((6, len(last_ys), LANES), F32)] + scratch(last_rows),
+        far=[coefficients],
+        mib=SUMS_GRANT,
+    )
+    last_one, last_two = (lax.ppermute(piece, "gx", PAIR) for piece in (last_one, last_two))
+    wide, *around = call(
         functools.partial(wide_field_kernel, depth),
         "wide_field",
-        [shaped(rows - last_rows, width)] + [edge_row] * 4 + [edge_column],
+        [shaped(rows - last_rows, width)] + [edge_row] * 2 + [shaped(depth, items, width)] * 4,
         [
             *(own_outer, outer, own_inner, inner, to_near, to_middle),
-            *(from_near, from_middle, *column_sums),
+            *(from_near, from_middle, pressure),
         ],
         flags,
+        [pltpu.VMEM((depth, width), F32)] * 2,
     )
     log_near, resist_near, *columns = call(
         functools.partial(first_field_kernel, depth),
         "first_field",
-        [shaped(depth, items, known)] * 2 + [edge_column] * 3,
-        [wide, own_last, last_one],
+        [shaped(depth, items, known)] * 2 + [edge_column] * 5,
+        [wide, own_last, last_one, own_columns],
         flags,
         [pltpu.VMEM((known // LANES, rows, LANES), F32)],
     )
@@ -1071,7 +1105,7 @@
             functools.partial(first_sweep_kernel, depth, vert, at),
             "first_sweep",
             state_types + [shaped(5, items, block_size)],
-            [resist, *columns, r_column, *row_edges, pressure, p_column, source],
+            [resist, *columns, *around, source],
             flags,
             [pltpu.VMEM((depth, items, block_size), F32)] * 3,
         )
@@ -1079,16 +1113,23 @@
     *state_one, reduced_one = first_sweep(0, resist_near)
     near_one = lax.ppermute(reduced_one, "gz", NEAR)
     last_two, _ = lax.optimization_barrier((last_two, reduced_one))
-    log_perm, resist_far = call(
+    log_far, resist_far = call(
         functools.partial(second_field_kernel, depth),
         "second_field",
-        [shaped(depth, items, width), block],
-        [wide, own_last, last_two, log_near, resist_near],
+        [shaped(depth, items, third), block],
+        [wide, own_last, last_two, resist_near],
         flags,
         [pltpu.VMEM((third // LANES, rows, LANES), F32)],
     )
     *state_two, reduced_two = first_sweep(1, resist_far)
     near_two = lax.ppermute(reduced_two, "gz", NEAR)
+    (log_perm,) = call(
+        functools.partial(join_columns_kernel, depth),
+        "log_perm",
+        [shaped(depth, items, width)],
+        [log_near, log_far, reduced_two],
+        flags,
+    )
     across, kept = call(
         pair_kernel,
         "join_pair",
@@ -1110,7 +1151,7 @@
         functools.partial(second_sweep_kernel, depth),
         "second_sweep",
         [block, block, shaped(2, items, width), shaped(items, width)],
-        [half, *h_edges, source, kept, row_edges[0], *weights[0], *weights[1]],
+        [half, *h_edges, source, kept, around[0], *weights[0], *weights[1]],
         flags,
         [pltpu.VMEM((depth, width), F32)] * 2,
     )

time: 77 us -> 71.4 us (0.927)
  the two profiles are of different devices: /device:TPU:0 before, /device:TPU:2 now
where the time goes in v1:
time: 71.4 us; the launch traced here: 71.1 us
  Pallas kernels  32 us (45%)
  starting transfers between devices  19.7 us (28%)
  waiting for transfers between devices  17.8 us (25%)
  between operations  0.85 us (1%)
  local copies, waits for them, and re-layouts  0.72 us (1%)
    pallas_call x14, Pallas kernels, call(): pl.pallas_call(kernel, out_shape=out_shape, in_specs=specs, out_specs=jax...  32 us
    ppermute x2, waiting for transfers between devices, exchange_edges(): lax.ppermute(to_middle, 'gy', MIDDLE)  5.45 us
    ppermute x3, starting transfers between devices, fast_body(): lax.ppermute(planes, 'gz', pairs)  4.82 us
    ppermute x2, starting transfers between devices, exchange_edges(): lax.ppermute(to_middle, 'gy', MIDDLE)  4.67 us
    ppermute x1, waiting for transfers between devices, fast_body(): near_two = lax.ppermute(reduced_two, 'gz', NEAR)  3.11 us
    ppermute x3, waiting for transfers between devices, fast_body(): lax.ppermute(planes, 'gz', pairs)  2.71 us
    ppermute x1, starting transfers between devices, fast_body(): other = lax.ppermute(across, 'gz', SKIP)  2.65 us
    ppermute x1, waiting for transfers between devices, fast_body(): other = lax.ppermute(across, 'gz', SKIP)  2.58 us
  transfers between devices with their start and end apart: 15, of which 9 were waited for; matrix products, arithmetic and copies ran while one was open for 0% of the time, Pallas kernels for 26%

profile of v1, /device:TPU:2, one launch (start us, length us, event | category | flops | bytes accessed | tf_op | source)
XLA Modules:
  0.0 71.1 jit_solution(8692204669585401980)
XLA Ops:
  0.6 4.6 %outer_row_sums.1 = (f32[64,1024]{1,0:T(8,128)}, f32[64,1024]{1,0:T(8,128)}, f32[6,2,128]{2,1,0:T(2,128)}) custom-call(s32[8,32]{1,0:T(8,128)} %bitcast.20, f32[2,256,1024]{2,1,0:T(8,128)} %bitcast.17), custom_call_target="tpu_custom_call" | custom-call | flops 1 | bytes 1 | tf_op jit(solution)/shard_map/outer_row_sums/pallas_call | solution.py:514
  5.2 1.6 %collective-permute-start = (f32[64,1024]{1,0:T(8,128)}, f32[64,1024]{1,0:T(8,128)S(1)}, u32[]{:S(2)}, u32[]{:S(2)}) collective-permute-start(f32[64,1024]{1,0:T(8,128)} %get-tuple-element.61), channel_id=1, source_target_pairs={{0,16},{16,0},{1,17},{17,1},{2,18},{18,2},{3,19},{19,3},{4,20},{20... | collective-permute-start | bytes 786440 | tf_op jit(solution)/shard_map/ppermute | solution.py:1051
  6.8 5.1 %inner_row_sums.1 = (f32[96,1024]{1,0:T(8,128)}, f32[96,1024]{1,0:T(8,128)}, f32[6,3,128]{2,1,0:T(4,128)}) custom-call(s32[8,32]{1,0:T(8,128)} %bitcast.21, f32[2,256,1024]{2,1,0:T(8,128)} %bitcast.18), custom_call_target="tpu_custom_call" | custom-call | flops 1073741824 | bytes 1 | tf_op jit(solution)/shard_map/inner_row_sums/pallas_call | solution.py:514
  12.6 0.9 %collective-permute-done.other.refs_1_ = f32[64,1024]{1,0:T(8,128)S(1)} collective-permute-done((f32[64,1024]{1,0:T(8,128)}, f32[64,1024]{1,0:T(8,128)S(1)}, u32[]{:S(2)}, u32[]{:S(2)}) %collective-permute-start) | collective-permute-done | bytes 262176 | tf_op jit(solution)/shard_map/ppermute | solution.py:1051
  13.6 1.2 %outer_field.1 = (f32[64,1024]{1,0:T(8,128)S(1)}, f32[64,1024]{1,0:T(8,128)S(1)}, f32[8,128]{1,0:T(8,128)S(1)}) custom-call(s32[17]{0:T(128)S(1)} %stack.75.flags, f32[64,1024]{1,0:T(8,128)S(1)} %copy-done.3, f32[64,1024]{1,0:T(8,128)S(1)} %collective-permute-done.other.refs_1_, f32[32,8,1024]{2,1,0:T(8,128)S(1)} %copy-done), custom_call_target="tpu_custom_call" | custom-call | flops 1 | bytes 1 | tf_op jit(solution)/shard_map/outer_field/pallas_call | solution.py:514
  14.8 0.6 copy-done.7
  15.4 5.2 %last_row_sums.1 = (f32[104,640]{1,0:T(8,128)}, f32[96,384]{1,0:T(8,128)}, f32[96,1024]{1,0:T(8,128)}, f32[6,8,128]{2,1,0:T(8,128)}) custom-call(s32[8,32]{1,0:T(8,128)} %bitcast.22, f32[6,2,128]{2,1,0:T(2,128)} %get-tuple-element.68.outer_kept, f32[6,3,128]{2,1,0:T(4,128)} %get-tuple-element.69.inner_kept, f32[8,128]{1,0:T(8,128)} %copy-done.7, ...), custom_call_target="tpu_custom_call" | custom-call | flops 1 | bytes 1 | tf_op jit(solution)/shard_map/last_row_sums/pallas_call | solution.py:514
  20.6 1.6 %collective-permute-start.4 = (f32[104,640]{1,0:T(8,128)}, f32[104,640]{1,0:T(8,128)S(1)}, u32[]{:S(2)}, u32[]{:S(2)}) collective-permute-start(f32[104,640]{1,0:T(8,128)} %get-tuple-element.72), channel_id=1, source_target_pairs={{0,16},{16,0},{1,17},{17,1},{2,18},{18,2},{3,19},{19,3},{4,20},{20... | collective-permute-start | bytes 798728 | tf_op jit(solution)/shard_map/ppermute | solution.py:1079
  22.2 2.8 %collective-permute-start.3 = (f32[64,1024]{1,0:T(8,128)S(1)}, f32[64,1024]{1,0:T(8,128)S(1)}, u32[]{:S(2)}, u32[]{:S(2)}) collective-permute-start(f32[64,1024]{1,0:T(8,128)S(1)} %get-tuple-element.66.refs_5_), channel_id=1, source_target_pairs={{1,2},{2,1},{5,6},{6,5},{9,10},{10,9},{13,14},{14,13},{17,18},{18,... | collective-permute-start | bytes 786440 | tf_op jit(solution)/shard_map/ppermute | solution.py:973
  25.1 4.8 %collective-permute-done.3.refs_7_ = f32[64,1024]{1,0:T(8,128)S(1)} collective-permute-done((f32[64,1024]{1,0:T(8,128)S(1)}, f32[64,1024]{1,0:T(8,128)S(1)}, u32[]{:S(2)}, u32[]{:S(2)}) %collective-permute-start.3) | collective-permute-done | bytes 262176 | tf_op jit(solution)/shard_map/ppermute | solution.py:973
  29.9 1.8 %wide_field.1 = (f32[160,1024]{1,0:T(8,128)S(1)}, f32[32,1024]{1,0:T(8,128)S(1)}, f32[32,1024]{1,0:T(8,128)S(1)}, f32[32,8,1024]{2,1,0:T(8,128)S(1)}, f32[32,8,1...) custom-call(s32[17]{0:T(128)S(1)} %stack.75.flags, f32[64,1024]{1,0:T(8,128)S(1)} %copy-done.3, ...), custom_call_target="tpu_custom_call" | custom-call | flops 1 | bytes 1 | tf_op jit(solution)/shard_map/wide_field/pallas_call | solution.py:514
  31.7 1.1 %first_field.1 = (f32[32,8,640]{2,1,0:T(8,128)S(1)}, f32[32,8,640]{2,1,0:T(8,128)S(1)}, f32[8,128]{1,0:T(8,128)S(1)}, f32[8,128]{1,0:T(8,128)S(1)}, f32[8,128]{1...) custom-call(s32[17]{0:T(128)S(1)} %stack.75.flags, f32[160,1024]{1,0:T(8,128)S(1)} %get-tuple-element.67.refs_0_, ...), custom_call_target="tpu_custom_call" | custom-call | flops 1 | bytes 1 | tf_op jit(solution)/shard_map/first_field/pallas_call | solution.py:514
  32.8 2.6 %first_sweep.2 = (f32[32,8,512]{2,1,0:T(8,128)S(1)}, f32[32,8,512]{2,1,0:T(8,128)S(1)}, f32[8,128]{1,0:T(8,128)S(1)}, f32[32,8,512]{2,1,0:T(8,128)S(1)}, f32[32,...) custom-call(s32[17]{0:T(128)S(1)} %stack.75.flags, ...), custom_call_target="tpu_custom_call" | custom-call | flops 1 | bytes 1 | tf_op jit(solution)/shard_map/first_sweep/pallas_call | solution.py:514
  35.5 0.9 %second_field.1 = (f32[32,8,384]{2,1,0:T(8,128)S(1)}, f32[32,8,512]{2,1,0:T(8,128)S(1)}) custom-call(s32[17]{0:T(128)S(1)} %stack.75.flags, f32[160,1024]{1,0:T(8,128)S(1)} %get-tuple-element.67.refs_0_, f32[96,1024]{1,0:T(8,128)S(1)} %copy-done.2, f32[96,384]{1,0:T(8,128)S(1)} %collective-permute-done.5.refs_2_, ...), custom_call_target="tpu_custom_call" | custom-call | flops 1 | bytes 1 | tf_op jit(solution)/shard_map/second_field/pallas_call | solution.py:514
  36.4 2.6 %first_sweep.3 = (f32[32,8,512]{2,1,0:T(8,128)S(1)}, f32[32,8,512]{2,1,0:T(8,128)S(1)}, f32[8,128]{1,0:T(8,128)S(1)}, f32[32,8,512]{2,1,0:T(8,128)S(1)}, f32[32,...) custom-call(s32[17]{0:T(128)S(1)} %stack.75.flags, ...), custom_call_target="tpu_custom_call" | custom-call | flops 1 | bytes 1 | tf_op jit(solution)/shard_map/first_sweep/pallas_call | solution.py:514
  39.0 1.6 %collective-permute-start.7 = (f32[5,8,512]{2,1,0:T(8,128)S(1)}, f32[5,8,512]{2,1,0:T(8,128)S(1)}, u32[]{:S(2)}, u32[]{:S(2)}) collective-permute-start(f32[5,8,512]{2,1,0:T(8,128)S(1)} %get-tuple-element.92._.own_two), channel_id=1, source_target_pairs={{0,4},{4,0},{8,12},{12,8},{1,5},{5,1},{9,13},{13,9},{2,6},{6,2},{1... | collective-permute-start | bytes 245768 | tf_op jit(solution)/shard_map/ppermute | solution.py:1125
  41.1 3.1 %collective-permute-done.7.near_two = f32[5,8,512]{2,1,0:T(8,128)S(1)} collective-permute-done((f32[5,8,512]{2,1,0:T(8,128)S(1)}, f32[5,8,512]{2,1,0:T(8,128)S(1)}, u32[]{:S(2)}, u32[]{:S(2)}) %collective-permute-start.7) | collective-permute-done | bytes 81952 | tf_op jit(solution)/shard_map/ppermute | solution.py:1125
  44.2 0.9 %collective-permute-done.6.near_one = f32[5,8,512]{2,1,0:T(8,128)S(1)} collective-permute-done((f32[5,8,512]{2,1,0:T(8,128)S(1)}, f32[5,8,512]{2,1,0:T(8,128)S(1)}, u32[]{:S(2)}, u32[]{:S(2)}) %collective-permute-start.6) | collective-permute-done | bytes 81952 | tf_op jit(solution)/shard_map/ppermute | solution.py:1114
  45.7 2.6 %collective-permute-start.8 = (f32[2,8,1024]{2,1,0:T(8,128)S(1)}, f32[2,8,1024]{2,1,0:T(8,128)S(1)}, u32[]{:S(2)}, u32[]{:S(2)}) collective-permute-start(f32[2,8,1024]{2,1,0:T(8,128)S(1)} %get-tuple-element.93.refs_0_), channel_id=1, source_target_pairs={{0,8},{8,0},{4,12},{12,4},{1,9},{9,1},{5,13},{13,5},{2,10},{10,2},... | collective-permute-start | bytes 196616 | tf_op jit(solution)/shard_map/ppermute | solution.py:1140
  48.3 2.6 %collective-permute-done.8.refs_1_ = f32[2,8,1024]{2,1,0:T(8,128)S(1)} collective-permute-done((f32[2,8,1024]{2,1,0:T(8,128)S(1)}, f32[2,8,1024]{2,1,0:T(8,128)S(1)}, u32[]{:S(2)}, u32[]{:S(2)}) %collective-permute-start.8) | collective-permute-done | bytes 65568 | tf_op jit(solution)/shard_map/ppermute | solution.py:1140
  50.9 1.1 %half.1 = (f32[32,8,1024]{2,1,0:T(8,128)S(1)}, f32[32,1024]{1,0:T(8,128)S(1)}, f32[32,1024]{1,0:T(8,128)S(1)}, f32[8,128]{1,0:T(8,128)S(1)}, f32[8,1024]{1,0:T(8,128)S(1)}) custom-call(s32[17]{0:T(128)S(1)} %stack.75.flags, f32[2,8,1024]{2,1,0:T(8,128)S(1)} %get-tuple-element.93.refs_0_, f32[2,8,1024]{2,1,0:T(8,128)S(1)} %collective-permute-done.8.refs_1_, ...), custom_call_target="tpu_custom_call" | custom-call | flops 1 | bytes 1 | tf_op jit(solution)/shard_map/half/pallas_call | solution.py:514
  52.1 1.9 %collective-permute-start.10 = (f32[32,1024]{1,0:T(8,128)S(1)}, f32[32,1024]{1,0:T(8,128)S(1)}, u32[]{:S(2)}, u32[]{:S(2)}) collective-permute-start(f32[32,1024]{1,0:T(8,128)S(1)} %get-tuple-element.105), channel_id=1, source_target_pairs={{1,2},{2,1},{5,6},{6,5},{9,10},{10,9},{13,14},{14,13},{17,18},{18,... | collective-permute-start | bytes 393224 | tf_op jit(solution)/shard_map/ppermute | solution.py:973
  54.1 1.5 %collective-permute-start.11 = (f32[8,128]{1,0:T(8,128)S(1)}, f32[8,128]{1,0:T(8,128)S(1)}, u32[]{:S(2)}, u32[]{:S(2)}) collective-permute-start(f32[8,128]{1,0:T(8,128)S(1)} %get-tuple-element.106), channel_id=1, source_target_pairs={{0,16},{16,0},{1,17},{17,1},{2,18},{18,2},{3,19},{19,3},{4,20},{20... | collective-permute-start | bytes 12296 | tf_op jit(solution)/shard_map/ppermute | solution.py:974
  55.6 2.1 %collective-permute-done.11.refs_3_ = f32[8,128]{1,0:T(8,128)S(1)} collective-permute-done((f32[8,128]{1,0:T(8,128)S(1)}, f32[8,128]{1,0:T(8,128)S(1)}, u32[]{:S(2)}, u32[]{:S(2)}) %collective-permute-start.11) | collective-permute-done | bytes 4128 | tf_op jit(solution)/shard_map/ppermute | solution.py:974
  57.7 0.7 collective-permute-done.10.refs_2_
  58.4 1.6 %second_sweep.1 = (f32[32,8,512]{2,1,0:T(8,128)S(1)}, f32[32,8,512]{2,1,0:T(8,128)S(1)}, f32[2,8,1024]{2,1,0:T(8,128)S(1)}, f32[8,1024]{1,0:T(8,128)S(1)}) custom-call(s32[17]{0:T(128)S(1)} %stack.75.flags, f32[32,8,1024]{2,1,0:T(8,128)S(1)} %get-tuple-element.103.refs_0_.refs_14_, f32[32,1024]{1,0:T(8,128)S(1)} %collective-permute-done.9.refs_1_, ...), custom_call_target="tpu_custom_call" | custom-call | flops 1 | bytes 1 | tf_op jit(solution)/shard_map/second_sweep/pallas_call | solution.py:514
  60.0 1.6 %collective-permute-start.12 = (f32[2,8,1024]{2,1,0:T(8,128)S(1)}, f32[2,8,1024]{2,1,0:T(8,128)S(1)}, u32[]{:S(2)}, u32[]{:S(2)}) collective-permute-start(f32[2,8,1024]{2,1,0:T(8,128)S(1)} %get-tuple-element.113.refs_0_), channel_id=1, source_target_pairs={{0,4},{4,0},{8,12},{12,8},{1,5},{5,1},{9,13},{13,9},{2,6},{6,2},{1... | collective-permute-start | bytes 196616 | tf_op jit(solution)/shard_map/ppermute | solution.py:1159
  61.7 2.7 %collective-permute-start.14 = (f32[8,1024]{1,0:T(8,128)S(1)}, f32[8,1024]{1,0:T(8,128)S(1)}, u32[]{:S(2)}, u32[]{:S(2)}) collective-permute-start(f32[8,1024]{1,0:T(8,128)S(1)} %get-tuple-element.114), channel_id=1, source_target_pairs={{0,12},{12,0},{4,8},{8,4},{1,13},{13,1},{5,9},{9,5},{2,14},{14,2},... | collective-permute-start | bytes 98312 | tf_op jit(solution)/shard_map/ppermute | solution.py:1159
  64.9 1.6 %log_perm.1 = f32[32,8,1024]{2,1,0:T(8,128)} custom-call(s32[17]{0:T(128)S(1)} %stack.75.flags, f32[32,8,640]{2,1,0:T(8,128)S(1)} %get-tuple-element.74.near, f32[32,8,384]{2,1,0:T(8,128)S(1)} %get-tuple-element.90.far, f32[5,8,512]{2,1,0:T(8,128)S(1)} %get-tuple-element.92._.own_two), custom_call_target="tpu_custom_call" | custom-call | flops 1 | bytes 1 | tf_op jit(solution)/shard_map/log_perm/pallas_call | solution.py:514
  66.5 0.9 %collective-permute-done.14.refs_3_ = f32[8,1024]{1,0:T(8,128)S(1)} collective-permute-done((f32[8,1024]{1,0:T(8,128)S(1)}, f32[8,1024]{1,0:T(8,128)S(1)}, u32[]{:S(2)}, u32[]{:S(2)}) %collective-permute-start.14) | collective-permute-done | bytes 32800 | tf_op jit(solution)/shard_map/ppermute | solution.py:1159
  67.4 1.8 %collective-permute-done.13.refs_2_ = f32[8,1024]{1,0:T(8,128)S(1)} collective-permute-done((f32[8,1024]{1,0:T(8,128)S(1)}, f32[8,1024]{1,0:T(8,128)S(1)}, u32[]{:S(2)}, u32[]{:S(2)}) %collective-permute-start.13) | collective-permute-done | bytes 32800 | tf_op jit(solution)/shard_map/ppermute | solution.py:1159
  69.2 1.9 %smoothed.1 = f32[32,8,1024]{2,1,0:T(8,128)} custom-call(s32[17]{0:T(128)S(1)} %stack.75.flags, f32[2,8,1024]{2,1,0:T(8,128)S(1)} %get-tuple-element.113.refs_0_, f32[2,8,1024]{2,1,0:T(8,128)S(1)} %collective-permute-done.12.refs_1_, f32[8,1024]{1,0:T(8,128)S(1)} %collective-permute-done.13.refs_2_, f32[8,1024]{1,0:T(8,128)S(1)} %collective-permute-done.14.refs_3_, ...), custom_call_target="tpu_custom_call" | custom-call | flops 1 | bytes 1 | tf_op jit(solution)/shard_map/smoothed/pallas_call | solution.py:514
  (29 shorter events, 2.4 us)
Async XLA Ops:
  5.2 8.3 %copy-start = (f32[32,8,1024]{2,1,0:T(8,128)S(1)}, f32[32,8,1024]{2,1,0:T(8,128)}, u32[]{:S(2)}) copy-start(f32[32,8,1024]{2,1,0:T(8,128)} %refs_11_.1) | copy-start | bytes 3145732
  5.2 8.3 %copy-start.3 = (f32[64,1024]{1,0:T(8,128)S(1)}, f32[64,1024]{1,0:T(8,128)}, u32[]{:S(2)}) copy-start(f32[64,1024]{1,0:T(8,128)} %get-tuple-element.60.own.refs_0_) | copy-start | bytes 786436
  5.2 8.3 %collective-permute-start = (f32[64,1024]{1,0:T(8,128)}, f32[64,1024]{1,0:T(8,128)S(1)}, u32[]{:S(2)}, u32[]{:S(2)}) collective-permute-start(f32[64,1024]{1,0:T(8,128)} %get-tuple-element.61), channel_id=1, source_target_pairs={{0,16},{16,0},{1,17},{17,1},{2,18},{18,2},{3,19},{19,3},{4,20},{20... | collective-permute-start | bytes 786440 | tf_op jit(solution)/shard_map/ppermute | solution.py:1051
  12.0 17.9 %copy-start.4 = (f32[96,1024]{1,0:T(8,128)S(1)}, f32[96,1024]{1,0:T(8,128)}, u32[]{:S(2)}) copy-start(f32[96,1024]{1,0:T(8,128)} %get-tuple-element.63.refs_2_) | copy-start | bytes 1179652
  12.0 13.1 %collective-permute-start.1 = (f32[96,1024]{1,0:T(8,128)}, f32[96,1024]{1,0:T(8,128)S(1)}, u32[]{:S(2)}, u32[]{:S(2)}) collective-permute-start(f32[96,1024]{1,0:T(8,128)} %get-tuple-element.64), channel_id=1, source_target_pairs={{0,16},{16,0},{1,17},{17,1},{2,18},{18,2},{3,19},{19,3},{4,20},{20... | collective-permute-start | bytes 1179656 | tf_op jit(solution)/shard_map/ppermute | solution.py:1054
  14.8 0.6 copy-start.7
  20.6 11.1 %copy-start.2 = (f32[96,1024]{1,0:T(8,128)S(1)}, f32[96,1024]{1,0:T(8,128)}, u32[]{:S(2)}) copy-start(f32[96,1024]{1,0:T(8,128)} %get-tuple-element.71.refs_1_) | copy-start | bytes 1179652
  20.6 11.1 %copy-start.6 = (f32[6,8,128]{2,1,0:T(8,128)S(1)}, f32[6,8,128]{2,1,0:T(8,128)}, u32[]{:S(2)}) copy-start(f32[6,8,128]{2,1,0:T(8,128)} %get-tuple-element.73.refs_3_) | copy-start | bytes 73732
  20.6 11.1 %collective-permute-start.4 = (f32[104,640]{1,0:T(8,128)}, f32[104,640]{1,0:T(8,128)S(1)}, u32[]{:S(2)}, u32[]{:S(2)}) collective-permute-start(f32[104,640]{1,0:T(8,128)} %get-tuple-element.72), channel_id=1, source_target_pairs={{0,16},{16,0},{1,17},{17,1},{2,18},{18,2},{3,19},{19,3},{4,20},{20... | collective-permute-start | bytes 798728 | tf_op jit(solution)/shard_map/ppermute | solution.py:1079
  22.2 2.9 %collective-permute-start.2 = (f32[64,1024]{1,0:T(8,128)S(1)}, f32[64,1024]{1,0:T(8,128)S(1)}, u32[]{:S(2)}, u32[]{:S(2)}) collective-permute-start(f32[64,1024]{1,0:T(8,128)S(1)} %get-tuple-element.65.refs_4_), channel_id=1, source_target_pairs={{0,1},{1,0},{2,3},{3,2},{4,5},{5,4},{6,7},{7,6},{8,9},{9,8},{10,11... | collective-permute-start | bytes 786440 | tf_op jit(solution)/shard_map/ppermute | solution.py:972
  22.2 7.7 %collective-permute-start.3 = (f32[64,1024]{1,0:T(8,128)S(1)}, f32[64,1024]{1,0:T(8,128)S(1)}, u32[]{:S(2)}, u32[]{:S(2)}) collective-permute-start(f32[64,1024]{1,0:T(8,128)S(1)} %get-tuple-element.66.refs_5_), channel_id=1, source_target_pairs={{1,2},{2,1},{5,6},{6,5},{9,10},{10,9},{13,14},{14,13},{17,18},{18,... | collective-permute-start | bytes 786440 | tf_op jit(solution)/shard_map/ppermute | solution.py:973
  25.0 10.5 %collective-permute-start.5 = (f32[96,384]{1,0:T(8,128)}, f32[96,384]{1,0:T(8,128)S(1)}, u32[]{:S(2)}, u32[]{:S(2)}) collective-permute-start(f32[96,384]{1,0:T(8,128)} %get-tuple-element.75), channel_id=1, source_target_pairs={{0,16},{16,0},{1,17},{17,1},{2,18},{18,2},{3,19},{19,3},{4,20},{20... | collective-permute-start | bytes 442376 | tf_op jit(solution)/shard_map/ppermute | solution.py:1079
  29.9 2.9 %copy-start.1 = (f32[32,8,1024]{2,1,0:T(8,128)S(1)}, f32[32,8,1024]{2,1,0:T(8,128)}, u32[]{:S(2)}) copy-start(f32[32,8,1024]{2,1,0:T(8,128)} %refs_4_.1) | copy-start | bytes 3145732
  36.4 14.5 %copy-start.5 = (s32[8,1024]{1,0:T(8,128)S(1)}, s32[8,1024]{1,0:T(8,128)}, u32[]{:S(2)}) copy-start(s32[8,1024]{1,0:T(8,128)} %refs_15_.1) | copy-start | bytes 98308
  39.0 5.2 %collective-permute-start.7 = (f32[5,8,512]{2,1,0:T(8,128)S(1)}, f32[5,8,512]{2,1,0:T(8,128)S(1)}, u32[]{:S(2)}, u32[]{:S(2)}) collective-permute-start(f32[5,8,512]{2,1,0:T(8,128)S(1)} %get-tuple-element.92._.own_two), channel_id=1, source_target_pairs={{0,4},{4,0},{8,12},{12,8},{1,5},{5,1},{9,13},{13,9},{2,6},{6,2},{1... | collective-permute-start | bytes 245768 | tf_op jit(solution)/shard_map/ppermute | solution.py:1125
  40.6 4.4 %collective-permute-start.6 = (f32[5,8,512]{2,1,0:T(8,128)S(1)}, f32[5,8,512]{2,1,0:T(8,128)S(1)}, u32[]{:S(2)}, u32[]{:S(2)}) collective-permute-start(f32[5,8,512]{2,1,0:T(8,128)S(1)} %get-tuple-element.88.own_one), channel_id=1, source_target_pairs={{0,4},{4,0},{8,12},{12,8},{1,5},{5,1},{9,13},{13,9},{2,6},{6,2},{1... | collective-permute-start | bytes 245768 | tf_op jit(solution)/shard_map/ppermute | solution.py:1114
  45.7 5.2 %collective-permute-start.8 = (f32[2,8,1024]{2,1,0:T(8,128)S(1)}, f32[2,8,1024]{2,1,0:T(8,128)S(1)}, u32[]{:S(2)}, u32[]{:S(2)}) collective-permute-start(f32[2,8,1024]{2,1,0:T(8,128)S(1)} %get-tuple-element.93.refs_0_), channel_id=1, source_target_pairs={{0,8},{8,0},{4,12},{12,4},{1,9},{9,1},{5,13},{13,5},{2,10},{10,2},... | collective-permute-start | bytes 196616 | tf_op jit(solution)/shard_map/ppermute | solution.py:1140
  52.1 5.7 %collective-permute-start.9 = (f32[32,1024]{1,0:T(8,128)S(1)}, f32[32,1024]{1,0:T(8,128)S(1)}, u32[]{:S(2)}, u32[]{:S(2)}) collective-permute-start(f32[32,1024]{1,0:T(8,128)S(1)} %get-tuple-element.104), channel_id=1, source_target_pairs={{0,1},{1,0},{2,3},{3,2},{4,5},{5,4},{6,7},{7,6},{8,9},{9,8},{10,11... | collective-permute-start | bytes 393224 | tf_op jit(solution)/shard_map/ppermute | solution.py:972
  52.1 6.3 %collective-permute-start.10 = (f32[32,1024]{1,0:T(8,128)S(1)}, f32[32,1024]{1,0:T(8,128)S(1)}, u32[]{:S(2)}, u32[]{:S(2)}) collective-permute-start(f32[32,1024]{1,0:T(8,128)S(1)} %get-tuple-element.105), channel_id=1, source_target_pairs={{1,2},{2,1},{5,6},{6,5},{9,10},{10,9},{13,14},{14,13},{17,18},{18,... | collective-permute-start | bytes 393224 | tf_op jit(solution)/shard_map/ppermute | solution.py:973
  54.1 3.7 %collective-permute-start.11 = (f32[8,128]{1,0:T(8,128)S(1)}, f32[8,128]{1,0:T(8,128)S(1)}, u32[]{:S(2)}, u32[]{:S(2)}) collective-permute-start(f32[8,128]{1,0:T(8,128)S(1)} %get-tuple-element.106), channel_id=1, source_target_pairs={{0,16},{16,0},{1,17},{17,1},{2,18},{18,2},{3,19},{19,3},{4,20},{20... | collective-permute-start | bytes 12296 | tf_op jit(solution)/shard_map/ppermute | solution.py:974
  60.0 9.1 %collective-permute-start.12 = (f32[2,8,1024]{2,1,0:T(8,128)S(1)}, f32[2,8,1024]{2,1,0:T(8,128)S(1)}, u32[]{:S(2)}, u32[]{:S(2)}) collective-permute-start(f32[2,8,1024]{2,1,0:T(8,128)S(1)} %get-tuple-element.113.refs_0_), channel_id=1, source_target_pairs={{0,4},{4,0},{8,12},{12,8},{1,5},{5,1},{9,13},{13,9},{2,6},{6,2},{1... | collective-permute-start | bytes 196616 | tf_op jit(solution)/shard_map/ppermute | solution.py:1159
  61.7 5.7 %collective-permute-start.14 = (f32[8,1024]{1,0:T(8,128)S(1)}, f32[8,1024]{1,0:T(8,128)S(1)}, u32[]{:S(2)}, u32[]{:S(2)}) collective-permute-start(f32[8,1024]{1,0:T(8,128)S(1)} %get-tuple-element.114), channel_id=1, source_target_pairs={{0,12},{12,0},{4,8},{8,4},{1,13},{13,1},{5,9},{9,5},{2,14},{14,2},... | collective-permute-start | bytes 98312 | tf_op jit(solution)/shard_map/ppermute | solution.py:1159
  64.4 4.8 %collective-permute-start.13 = (f32[8,1024]{1,0:T(8,128)S(1)}, f32[8,1024]{1,0:T(8,128)S(1)}, u32[]{:S(2)}, u32[]{:S(2)}) collective-permute-start(f32[8,1024]{1,0:T(8,128)S(1)} %get-tuple-element.114), channel_id=1, source_target_pairs={{0,8},{8,0},{4,12},{12,4},{1,9},{9,1},{5,13},{13,5},{2,10},{10,2},... | collective-permute-start | bytes 98312 | tf_op jit(solution)/shard_map/ppermute | solution.py:1159

commit v2 on v1

--- a/solution.py
+++ b/solution.py
@@ -424,6 +424,21 @@
         edges[side, rows] = tiles[(side // 2 + 1) * count - 1 + side % 2]
 
 
+def inner_sums_kernel(ys, shifts, spectral, pressure, other, own, kept, p_column, *refs):
+    tile, sem, *refs = refs
+    g = lax.axis_index("gx")
+    width = pressure.shape[2]
+    there = lane_slice(jnp.where(g == 0, width - LANES, 0), LANES)
+    copy = pltpu.make_async_copy(pressure.at[:, :, there], tile, sem)
+    copy.start()
+    wide_sums_kernel(ys, shifts, spectral, other, own, kept, *refs)
+    copy.wait()
+    packed = jnp.zeros((ROWS, LANES), F32)
+    for z in range(tile.shape[0]):
+        packed = packed_with(z, packed, boundary_plane(g, tile[z]), 0)
+    p_column[...] = packed
+
+
 def wide_sums_kernel(ys, shifts, spectral, other, own, kept, *refs):
     columns, edges, coefficients, arrivals, *tables, left, right = refs
     items, depth = shifts.shape
@@ -505,7 +520,9 @@
 IN_HBM = pl.BlockSpec(memory_space=pltpu.HBM)
 
 
-def call(kernel, name, out_shape, args, flags=None, scratch=(), far=(), mib=20, flops=1):
+def call(
+    kernel, name, out_shape, args, flags=None, scratch=(), far=(), mib=20, flops=1, out=ON_CHIP
+):
     specs = [ON_CHIP] * len(args) + [IN_HBM] * len(far)
     args = list(args) + list(far)
     if flags is not None:
@@ -515,7 +532,7 @@
         kernel,
         out_shape=out_shape,
         in_specs=specs,
-        out_specs=jax.tree.map(lambda _: ON_CHIP, out_shape),
+        out_specs=jax.tree.map(lambda _: out, out_shape),
         scratch_shapes=list(scratch),
         compiler_params=params(mib),
         cost_estimate=pl.CostEstimate(flops=flops, bytes_accessed=1, transcendentals=0),
@@ -545,8 +562,7 @@
 
 
 def inverse_of(values):
-    guess = pl.reciprocal(values, approx=True)
-    return guess * (2.0 - values * guess)
+    return pl.reciprocal(values, approx=True)
 
 
 def ordered(z, sums, depth):
@@ -563,19 +579,15 @@
     return jnp.where(g == 0, roll(plane[:, -LANES:], 1, 1), plane[:, :LANES])
 
 
-def outer_field_kernel(depth, flags, own, other, pressure, to_near, to_middle, boundary):
-    g, even = flags[0], flags[16] == 0
+def outer_field_kernel(depth, flags, own, other, pressure, to_near, to_middle):
+    even = flags[16] == 0
     low, high = slice(0, depth), slice(depth, 2 * depth)
     south, north = own[low] + other[low], own[high] + other[high]
     to_near[low] = jnp.exp(-jnp.where(even, north, south))
     to_middle[low] = jnp.exp(-jnp.where(even, south, north))
 
-    def layer(z, packed):
-        plane = pressure[z]
-        keep_rows(depth + z, plane, even, to_near, to_middle, slice(None))
-        return packed_with(z, packed, boundary_plane(g, plane), 0)
-
-    boundary[...] = lax.fori_loop(0, depth, layer, jnp.zeros((ROWS, LANES), F32), unroll=8)
+    for z in range(depth):
+        keep_rows(depth + z, pressure[z], even, to_near, to_middle, slice(None))
 
 
 def wide_field_kernel(depth, flags, *refs):
@@ -605,7 +617,7 @@
         p_east[z] = roll(plane, -1, 1)
         return carry
 
-    lax.fori_loop(0, depth, layer, 0, unroll=4)
+    lax.fori_loop(0, depth, layer, 0, unroll=True)
 
 
 def lane_slice(start, size):
@@ -636,7 +648,7 @@
         resist[z] = jnp.exp(-plane)
         return carry
 
-    lax.fori_loop(0, depth, layer, 0, unroll=8)
+    lax.fori_loop(0, depth, layer, 0, unroll=True)
 
 
 def second_field_kernel(depth, flags, *refs):
@@ -656,7 +668,7 @@
         resist[z, :, extra_target] = resist_near[z, :, extra_source]
         return carry
 
-    lax.fori_loop(0, depth, layer, 0, unroll=8)
+    lax.fori_loop(0, depth, layer, 0, unroll=True)
 
 
 def join_columns_kernel(depth, flags, near, far, _, whole):
@@ -665,7 +677,7 @@
         whole[z, :, lane_slice(flags[5], far.shape[2])] = far[z]
         return carry
 
-    lax.fori_loop(0, depth, layer, 0, unroll=8)
+    lax.fori_loop(0, depth, layer, 0, unroll=True)
 
 
 def keep_rows(z, value, even, to_near, to_middle, here):
@@ -756,7 +768,7 @@
         )
         return carry
 
-    lax.fori_loop(0, depth, weigh, 0, unroll=4)
+    lax.fori_loop(0, depth, weigh, 0, unroll=True)
 
     def layer(z, carry):
         conduct, flow, product, first_first, first_part = carry
@@ -797,27 +809,22 @@
     reduced[4] = flow * reciprocal
 
 
-def pair_kernel(flags, own_one, own_two, near_one, near_two, across, kept):
+def pair_kernel(flags, own, near, across, kept):
     me = flags[14]
     even, lower = me % 2 == 0, me < 2
-    for block, (own, near) in enumerate(((own_one, near_one), (own_two, near_two))):
-        size = own.shape[2]
-        there = slice(block * size, (block + 1) * size)
-        first, second = [
-            [jnp.where(flip, own[at], near[at]) for at in range(5)]
-            for flip in (even, jnp.logical_not(even))
-        ]
-        reciprocal = inverse_of(first[2] + second[0])
-        step = (first[4] - second[3]) * reciprocal
-        through = jnp.where(lower, second[1], first[1])
-        share = through * reciprocal
-        across[0, :, there] = jnp.where(lower, second[2], first[0]) - through * share
-        across[1, :, there] = jnp.where(lower, second[4], first[3]) + jnp.where(
-            lower, through * step, -through * step
-        )
-        kept[0, :, there] = share
-        kept[1, :, there] = reciprocal
-        kept[2, :, there] = step
+    first, second = [
+        [jnp.where(flip, own[at], near[at]) for at in range(5)]
+        for flip in (even, jnp.logical_not(even))
+    ]
+    reciprocal = inverse_of(first[2] + second[0])
+    step = (first[4] - second[3]) * reciprocal
+    through = jnp.where(lower, second[1], first[1])
+    share = through * reciprocal
+    across[0] = jnp.where(lower, second[2], first[0]) - through * share
+    across[1] = jnp.where(lower, second[4], first[3]) + jnp.where(
+        lower, through * step, -through * step
+    )
+    kept[0], kept[1], kept[2] = share, reciprocal, step
 
 
 def ends(me, inner, middle):
@@ -836,34 +843,31 @@
     )
     state = emit(last, values, jnp.zeros((ROWS, LANES), F32))
 
-    def layer(step, carry):
-        following, state = carry
-        z = last - step
+    for z in range(last - 1, -1, -1):
         values = tuple(
             (particular[z] + lead[z] * enters) + ratio[z] * beyond
-            for (enters, _, particular, _, ratio, lead), beyond in zip(lines, following)
-        )
-        return values, emit(z, values, state)
-
-    return lax.fori_loop(1, depth, layer, (values, state), unroll=True)[1]
+            for (enters, _, particular, _, ratio, lead), beyond in zip(lines, values)
+        )
+        state = emit(z, values, state)
+    return state
 
 
 def half_kernel(depth, flags, *refs):
-    across, other, kept = refs[:3]
-    blocks = (refs[3:7], refs[7:11])
-    pressure, colour = refs[11:13]
-    half, to_near, to_middle, boundary, joined = refs[13:]
+    pairs = (refs[0:3], refs[3:6])
+    blocks = (refs[6:10], refs[10:14])
+    pressure, colour = refs[14:16]
+    half, to_near, to_middle, boundary, joined = refs[16:]
     me, g, even = flags[14], flags[0], flags[16] == 0
     size = blocks[0][0].shape[2]
     spans = [lane_slice(flags[6 + block], size) for block in range(2)]
     lines = []
     for block, state in enumerate(blocks):
-        there = slice(block * size, (block + 1) * size)
-        sum_of = inverse_of(across[0, :, there] + other[0, :, there])
-        joined[:, there] = sum_of
-        lead_of = across[1, :, there] - other[1, :, there]
+        across, other, kept = pairs[block]
+        sum_of = inverse_of(across[0] + other[0])
+        joined[block] = sum_of
+        lead_of = across[1] - other[1]
         middle = jnp.where(me < 2, lead_of, -lead_of) * sum_of
-        inner = kept[2, :, there] + kept[0, :, there] * middle
+        inner = kept[2] + kept[0] * middle
         lines.append((*ends(me, inner, middle), *state))
     chosen = [colour[:, here] == 0 for here in spans]
 
@@ -880,10 +884,11 @@
 
 
 def second_sweep_kernel(depth, flags, *refs):
-    half, h_near, h_middle, h_column, source, kept, south_weight = refs[:7]
-    blocks = (refs[7:13], refs[13:19])
-    particulars, near, far = refs[19:21], refs[21], refs[22]
-    south_terms, north_rows = refs[23:]
+    half, h_near, h_middle, h_column, source, south_weight = refs[:6]
+    shares = refs[6:8]
+    blocks = (refs[8:14], refs[14:20])
+    particulars, near, far = refs[20:22], refs[22], refs[23]
+    south_terms, north_rows = refs[24:]
     me, even = flags[14], flags[16] == 0
     size = particulars[0].shape[2]
     starts = [flags[6 + block] for block in range(2)]
@@ -926,7 +931,7 @@
         last_part = flow * inverse[last]
         particulars[block][last] = last_part
         asked = jnp.where(me % 2 == 0, last_part, first_part)
-        shared = kept[0, :, there] * asked
+        shared = shares[block][0] * asked
         outer = jnp.where(me == 1, last_part, jnp.where(me == 2, first_part, 0.0))
         given = outer + jnp.where((me == 0) | (me == 3), shared, -shared)
         near[0, :, there] = asked
@@ -935,28 +940,45 @@
 
 
 def smoothed_kernel(depth, flags, *refs):
-    own, near, skip, cross, kept, joined = refs[:6]
-    blocks = (refs[6:10], refs[10:14])
-    half, colour, smoothed = refs[14:]
+    own, near, skip, cross, joined = refs[:5]
+    keeps = refs[5:7]
+    blocks = (refs[7:11], refs[11:15])
+    half, colour, result = refs[15:18]
+    smoothed, sems = refs[18:]
     me = flags[14]
     size = blocks[0][0].shape[2]
     spans = [lane_slice(flags[6 + block], size) for block in range(2)]
     lines = []
     for block, state in enumerate(blocks):
         there = slice(block * size, (block + 1) * size)
+        kept = keeps[block]
         lead_of = (own[1, :, there] + near[1, :, there]) - (skip[:, there] + cross[:, there])
-        middle = jnp.where(me < 2, lead_of, -lead_of) * joined[:, there]
+        middle = jnp.where(me < 2, lead_of, -lead_of) * joined[block]
         step = own[0, :, there] - near[0, :, there]
-        step = jnp.where(me % 2 == 0, step, -step) * kept[1, :, there]
-        lines.append((*ends(me, step + kept[0, :, there] * middle, middle), *state))
+        step = jnp.where(me % 2 == 0, step, -step) * kept[1]
+        lines.append((*ends(me, step + kept[0] * middle, middle), *state))
     chosen = [colour[:, here] == 1 for here in spans]
+    count = sems.shape[0]
+    layers = depth // count
+    copies = [
+        pltpu.make_async_copy(
+            smoothed.at[pl.ds(at * layers, layers)],
+            result.at[pl.ds(at * layers, layers)],
+            sems.at[at],
+        )
+        for at in range(count)
+    ]
 
     def emit(z, values, state):
         for value, here, mine in zip(values, spans, chosen):
             smoothed[z, :, here] = jnp.where(mine, value, half[z, :, here])
+        if z % layers == 0:
+            copies[z // layers].start()
         return state
 
     back_substitute(depth, lines, emit)
+    for copy in copies:
+        copy.wait()
 
 
 PAIR = [(0, 1), (1, 0)]
@@ -1034,31 +1056,41 @@
             pltpu.VMEM((2, groups * depth, LANES), F32),
         ]
 
-    def wide_sums(ys, name, shift_rows, cost):
-        return call(
-            functools.partial(wide_sums_kernel, ys),
-            name,
-            [shaped(len(ys) * depth, width)] * 2 + [shaped(6, len(ys), LANES)],
-            [shift_rows],
-            scratch=scratch(len(ys) * depth),
-            far=[coefficients],
-            mib=SUMS_GRANT,
-            flops=cost,
-        )
+    def wide_types(ys):
+        return [shaped(len(ys) * depth, width)] * 2 + [shaped(6, len(ys), LANES)]
 
     shift_rows = shifts.T
-    sums, own_outer, outer_kept = wide_sums((0, items - 1), "outer_row_sums", shift_rows, 1)
+    outer_ys = (0, items - 1)
+    sums, own_outer, outer_kept = call(
+        functools.partial(wide_sums_kernel, outer_ys),
+        "outer_row_sums",
+        wide_types(outer_ys),
+        [shift_rows],
+        scratch=scratch(2 * depth),
+        far=[coefficients],
+        mib=SUMS_GRANT,
+    )
     outer = lax.ppermute(sums, "gx", PAIR)
     shift_rows, _ = lax.optimization_barrier((shift_rows, own_outer))
-    sums, own_inner, inner_kept = wide_sums(inner_ys, "inner_row_sums", shift_rows, 1 << 30)
+    sums, own_inner, inner_kept, p_column = call(
+        functools.partial(inner_sums_kernel, inner_ys),
+        "inner_row_sums",
+        wide_types(inner_ys) + [column_type],
+        [shift_rows],
+        scratch=[pltpu.VMEM((depth, ROWS, LANES), F32), pltpu.SemaphoreType.DMA]
+        + scratch(len(inner_ys) * depth),
+        far=[coefficients, pressure],
+        mib=20,
+    )
     inner = lax.ppermute(sums, "gx", PAIR)
     edge_row, edge_column = shaped(depth, width), shaped(ROWS, LANES)
     edges = [edge_row, edge_row, edge_column]
-    to_near, to_middle, p_column = call(
+    pressure_rows, _ = lax.optimization_barrier((pressure, own_inner))
+    to_near, to_middle = call(
         functools.partial(outer_field_kernel, depth),
         "outer_field",
-        [shaped(2 * depth, width)] * 2 + [edge_column],
-        [own_outer, outer, pressure],
+        [shaped(2 * depth, width)] * 2,
+        [own_outer, outer, pressure_rows],
         flags,
     )
     from_near, from_middle = exchange_edges([to_near, to_middle])
@@ -1074,9 +1106,9 @@
         [shift_rows, outer_kept, inner_kept, p_column],
         scratch=[pltpu.VMEM((6, len(last_ys), LANES), F32)] + scratch(last_rows),
         far=[coefficients],
-        mib=SUMS_GRANT,
-    )
-    last_one, last_two = (lax.ppermute(piece, "gx", PAIR) for piece in (last_one, last_two))
+        mib=20,
+    )
+    last_one = lax.ppermute(last_one, "gx", PAIR)
     wide, *around = call(
         functools.partial(wide_field_kernel, depth),
         "wide_field",
@@ -1088,6 +1120,8 @@
         flags,
         [pltpu.VMEM((depth, width), F32)] * 2,
     )
+    last_two, _ = lax.optimization_barrier((last_two, wide))
+    last_two = lax.ppermute(last_two, "gx", PAIR)
     log_near, resist_near, *columns = call(
         functools.partial(first_field_kernel, depth),
         "first_field",
@@ -1130,19 +1164,23 @@
         [log_near, log_far, reduced_two],
         flags,
     )
-    across, kept = call(
-        pair_kernel,
-        "join_pair",
-        [shaped(2, items, width), shaped(3, items, width)],
-        [reduced_one, reduced_two, near_one, near_two],
-        flags,
-    )
-    other = lax.ppermute(across, "gz", SKIP)
+    def join(reduced, near):
+        across, kept = call(
+            pair_kernel,
+            "join_pair",
+            [shaped(2, items, block_size), shaped(3, items, block_size)],
+            [reduced, near],
+            flags,
+        )
+        return across, lax.ppermute(across, "gz", SKIP), kept
+
+    pair_one, pair_two = join(reduced_one, near_one), join(reduced_two, near_two)
+    keeps = [pair_one[2], pair_two[2]]
     half, *h_edges, joined = call(
         functools.partial(half_kernel, depth),
         "half",
-        [shaped(depth, items, width), *edges, shaped(items, width)],
-        [across, other, kept, *state_one[3:], *state_two[3:], pressure, colour],
+        [shaped(depth, items, width), *edges, shaped(2, items, block_size)],
+        [*pair_one, *pair_two, *state_one[3:], *state_two[3:], pressure, colour],
         flags,
     )
     h_edges = exchange_edges(h_edges)
@@ -1151,7 +1189,7 @@
         functools.partial(second_sweep_kernel, depth),
         "second_sweep",
         [block, block, shaped(2, items, width), shaped(items, width)],
-        [half, *h_edges, source, kept, around[0], *weights[0], *weights[1]],
+        [half, *h_edges, source, around[0], *keeps, *weights[0], *weights[1]],
         flags,
         [pltpu.VMEM((depth, width), F32)] * 2,
     )
@@ -1164,12 +1202,14 @@
         "smoothed",
         [shaped(depth, items, width)],
         [
-            *(to_near, from_near, from_skip, from_cross, kept, joined),
+            *(to_near, from_near, from_skip, from_cross, joined, *keeps),
             *(current_one, *state_one[4:]),
             *(current_two, *state_two[4:]),
             *(half, colour),
         ],
         flags,
+        [pltpu.VMEM((depth, items, width), F32), pltpu.SemaphoreType.DMA((4,))],
+        out=IN_HBM,
     )
     return (log_perm, smoothed)
 

time: 71.4 us -> 67 us (0.938)
  Pallas kernels: 32 us -> 26.1 us
  local copies, waits for them, and re-layouts: 0.72 us -> 2.09 us
    pallas_call x14 -> x15, Pallas kernels: 32 us -> 26.1 us  [call(): pl.pallas_call(kernel, out_shape=out_shape, in_specs=specs, out_specs=jax...]
    ppermute x2, waiting for transfers between devices: 5.45 us -> 0.68 us  [exchange_edges(): lax.ppermute(to_middle, 'gy', MIDDLE)]
    ppermute x3 -> x4, waiting for transfers between devices: 2.59 us -> 6.37 us  [the longest x1 3.72 us: fast_body(): last_one = lax.ppermute(last_one, 'gx', PAIR)]
    ppermute x1, waiting for transfers between devices: 3.11 us -> 0.01 us  [fast_body(): near_two = lax.ppermute(reduced_two, 'gz', NEAR)]
    ppermute x3 -> x4, starting transfers between devices: 4.41 us -> 7.27 us  [the longest x2 5.28 us: join(): return (across, lax.ppermute(across, 'gz', SKIP), kept)]
    ppermute x1, waiting for transfers between devices: 0.01 us -> 2.65 us  [fast_body(): inner = lax.ppermute(sums, 'gx', PAIR)]
    unnamed x16 -> x20, local copies, waits for them, and re-layouts: 0.63 us -> 2 us
    ppermute x1, starting transfers between devices: 0.45 us -> 1.65 us  [fast_body(): near_one = lax.ppermute(reduced_one, 'gz', NEAR)]
  transfers between devices with their start and end apart: 15 -> 16, of which waited for: 9 -> 9; matrix products, arithmetic and copies ran while one was open for 0% -> 0% of each run, Pallas kernels for 26% -> 25%
where the time goes in v2:
time: 67 us; the launch traced here: 66.8 us
  Pallas kernels  26.1 us (39%)
  starting transfers between devices  20.2 us (30%)
  waiting for transfers between devices  17.6 us (26%)
  local copies, waits for them, and re-layouts  2.09 us (3%)
  between operations  0.84 us (1%)
    pallas_call x15, Pallas kernels, call(): pl.pallas_call(kernel, out_shape=out_shape, in_specs=specs, out_specs=jax...  26.1 us
    ppermute x2, starting transfers between devices, join(): return (across, lax.ppermute(across, 'gz', SKIP), kept)  5.28 us
    ppermute x2, starting transfers between devices, exchange_edges(): lax.ppermute(to_middle, 'gy', MIDDLE)  4.23 us
    ppermute x1, waiting for transfers between devices, fast_body(): last_one = lax.ppermute(last_one, 'gx', PAIR)  3.72 us
    ppermute x3, starting transfers between devices, fast_body(): lax.ppermute(planes, 'gz', pairs)  3.7 us
    ppermute x3, waiting for transfers between devices, fast_body(): lax.ppermute(planes, 'gz', pairs)  3.21 us
    ppermute x1, waiting for transfers between devices, exchange_edges(): lax.ppermute(piece, 'gx', PAIR)  3.05 us
    ppermute x1, waiting for transfers between devices, fast_body(): inner = lax.ppermute(sums, 'gx', PAIR)  2.65 us
  transfers between devices with their start and end apart: 16, of which 9 were waited for; matrix products, arithmetic and copies ran while one was open for 0% of the time, Pallas kernels for 25%

profile of v2, /device:TPU:2, one launch (start us, length us, event | category | flops | bytes accessed | tf_op | source)
XLA Modules:
  0.0 66.8 jit_solution(13100851086600517327)
XLA Ops:
  0.6 4.7 %outer_row_sums.1 = (f32[64,1024]{1,0:T(8,128)}, f32[64,1024]{1,0:T(8,128)}, f32[6,2,128]{2,1,0:T(2,128)}) custom-call(s32[8,32]{1,0:T(8,128)} %bitcast.20, f32[2,256,1024]{2,1,0:T(8,128)} %bitcast.17), custom_call_target="tpu_custom_call" | custom-call | flops 1 | bytes 1 | tf_op jit(solution)/shard_map/outer_row_sums/pallas_call | solution.py:531
  5.4 1.6 %collective-permute-start = (f32[64,1024]{1,0:T(8,128)}, f32[64,1024]{1,0:T(8,128)}, u32[]{:S(2)}, u32[]{:S(2)}) collective-permute-start(f32[64,1024]{1,0:T(8,128)} %get-tuple-element.65), channel_id=1, source_target_pairs={{0,16},{16,0},{1,17},{17,1},{2,18},{18,2},{3,19},{19,3},{4,20},{20... | collective-permute-start | bytes 786440 | tf_op jit(solution)/shard_map/ppermute | solution.py:1073
  7.0 1.2 %copy-done.1 = f32[32,8,1024]{2,1,0:T(8,128)S(1)} copy-done((f32[32,8,1024]{2,1,0:T(8,128)S(1)}, f32[32,8,1024]{2,1,0:T(8,128)}, u32[]{:S(2)}) %copy-start.1) | copy-done | bytes 1048600
  8.2 3.4 %inner_row_sums.1 = (f32[96,1024]{1,0:T(8,128)}, f32[96,1024]{1,0:T(8,128)S(1)}, f32[6,3,128]{2,1,0:T(4,128)S(1)}, f32[8,128]{1,0:T(8,128)S(1)}) custom-call(s32[8,32]{1,0:T(8,128)S(1)} %bitcast.21, f32[2,256,1024]{2,1,0:T(8,128)S(1)} %bitcast.18, f32[32,8,1024]{2,1,0:T(8,128)S(1)} %copy-done.1), custom_call_target="tpu_custom_call" | custom-call | flops 1 | bytes 1 | tf_op jit(solution)/shard_map/inner_row_sums/pallas_call | solution.py:531
  11.6 0.7 %copy-done.5 = f32[96,1024]{1,0:T(8,128)} copy-done((f32[96,1024]{1,0:T(8,128)}, f32[96,1024]{1,0:T(8,128)S(1)}, u32[]{:S(2)}) %copy-start.5) | copy-done | bytes 393240
  13.0 0.8 %collective-permute-done.other.refs_1_ = f32[64,1024]{1,0:T(8,128)} collective-permute-done((f32[64,1024]{1,0:T(8,128)}, f32[64,1024]{1,0:T(8,128)}, u32[]{:S(2)}, u32[]{:S(2)}) %collective-permute-start) | collective-permute-done | bytes 262176 | tf_op jit(solution)/shard_map/ppermute | solution.py:1073
  13.8 1.3 %outer_field.1 = (f32[64,1024]{1,0:T(8,128)S(1)}, f32[64,1024]{1,0:T(8,128)S(1)}) custom-call(s32[17]{0:T(128)S(1)} %stack.75.flags, f32[64,1024]{1,0:T(8,128)S(1)} %copy-done.4, f32[64,1024]{1,0:T(8,128)} %collective-permute-done.other.refs_1_, f32[32,8,1024]{2,1,0:T(8,128)S(1)} %copy-done.2), custom_call_target="tpu_custom_call" | custom-call | flops 1 | bytes 1 | tf_op jit(solution)/shard_map/outer_field/pallas_call | solution.py:531
  15.2 2.3 %collective-permute-start.3 = (f32[64,1024]{1,0:T(8,128)S(1)}, f32[64,1024]{1,0:T(8,128)S(1)}, u32[]{:S(2)}, u32[]{:S(2)}) collective-permute-start(f32[64,1024]{1,0:T(8,128)S(1)} %get-tuple-element.71.refs_5_), channel_id=1, source_target_pairs={{1,2},{2,1},{5,6},{6,5},{9,10},{10,9},{13,14},{14,13},{17,18},{18,... | collective-permute-start | bytes 786440 | tf_op jit(solution)/shard_map/ppermute | solution.py:995
  17.5 2.7 %last_row_sums.1 = (f32[104,640]{1,0:T(8,128)S(1)}, f32[96,384]{1,0:T(8,128)S(1)}, f32[96,1024]{1,0:T(8,128)S(1)}, f32[6,8,128]{2,1,0:T(8,128)S(1)}) custom-call(s32[8,32]{1,0:T(8,128)S(1)} %bitcast.22, f32[6,2,128]{2,1,0:T(2,128)S(1)} %copy-done.9, f32[6,3,128]{2,1,0:T(4,128)S(1)} %get-tuple-element.74.inner_kept, f32[8,128]{1,0:T(8,128)S(1)} %get-tuple-element.75.p_column, ...), custom_call_target="tpu_custom_call" | custom-call | flops 1 | bytes 1 | tf_op jit(solution)/shard_map/last_row_sums/pallas_call | solution.py:531
  20.2 1.9 %collective-permute-start.4 = (f32[104,640]{1,0:T(8,128)S(1)}, f32[104,640]{1,0:T(8,128)S(1)}, u32[]{:S(2)}, u32[]{:S(2)}) collective-permute-start(f32[104,640]{1,0:T(8,128)S(1)} %get-tuple-element.77), channel_id=1, source_target_pairs={{0,16},{16,0},{1,17},{17,1},{2,18},{18,2},{3,19},{19,3},{4,20},{20... | collective-permute-start | bytes 798728 | tf_op jit(solution)/shard_map/ppermute | solution.py:1111
  22.1 2.6 %collective-permute-done.1.refs_3_ = f32[96,1024]{1,0:T(8,128)} collective-permute-done((f32[96,1024]{1,0:T(8,128)}, f32[96,1024]{1,0:T(8,128)}, u32[]{:S(2)}, u32[]{:S(2)}) %collective-permute-start.1) | collective-permute-done | bytes 393248 | tf_op jit(solution)/shard_map/ppermute | solution.py:1085
  24.7 1.8 %wide_field.1 = (f32[160,1024]{1,0:T(8,128)S(1)}, f32[32,1024]{1,0:T(8,128)S(1)}, f32[32,1024]{1,0:T(8,128)S(1)}, f32[32,8,1024]{2,1,0:T(8,128)S(1)}, f32[32,8,1...) custom-call(s32[17]{0:T(128)S(1)} %stack.75.flags, f32[64,1024]{1,0:T(8,128)S(1)} %copy-done.4, ...), custom_call_target="tpu_custom_call" | custom-call | flops 1 | bytes 1 | tf_op jit(solution)/shard_map/wide_field/pallas_call | solution.py:531
  26.6 3.7 %collective-permute-done.4.refs_2_ = f32[104,640]{1,0:T(8,128)S(1)} collective-permute-done((f32[104,640]{1,0:T(8,128)S(1)}, f32[104,640]{1,0:T(8,128)S(1)}, u32[]{:S(2)}, u32[]{:S(2)}) %collective-permute-start.4) | collective-permute-done | bytes 266272 | tf_op jit(solution)/shard_map/ppermute | solution.py:1111
  30.3 1.1 %first_field.1 = (f32[32,8,640]{2,1,0:T(8,128)S(1)}, f32[32,8,640]{2,1,0:T(8,128)S(1)}, f32[8,128]{1,0:T(8,128)S(1)}, f32[8,128]{1,0:T(8,128)S(1)}, f32[8,128]{1...) custom-call(s32[17]{0:T(128)S(1)} %stack.75.flags, f32[160,1024]{1,0:T(8,128)S(1)} %get-tuple-element.72.refs_0_, ...), custom_call_target="tpu_custom_call" | custom-call | flops 1 | bytes 1 | tf_op jit(solution)/shard_map/first_field/pallas_call | solution.py:531
  31.4 1.5 %first_sweep.2 = (f32[32,8,512]{2,1,0:T(8,128)S(1)}, f32[32,8,512]{2,1,0:T(8,128)S(1)}, f32[8,128]{1,0:T(8,128)S(1)}, f32[32,8,512]{2,1,0:T(8,128)S(1)}, f32[32,...) custom-call(s32[17]{0:T(128)S(1)} %stack.75.flags, ...), custom_call_target="tpu_custom_call" | custom-call | flops 1 | bytes 1 | tf_op jit(solution)/shard_map/first_sweep/pallas_call | solution.py:531
  32.9 1.6 %collective-permute-start.6 = (f32[5,8,512]{2,1,0:T(8,128)S(1)}, f32[5,8,512]{2,1,0:T(8,128)S(1)}, u32[]{:S(2)}, u32[]{:S(2)}) collective-permute-start(f32[5,8,512]{2,1,0:T(8,128)S(1)} %get-tuple-element.94.own), channel_id=1, source_target_pairs={{0,4},{4,0},{8,12},{12,8},{1,5},{5,1},{9,13},{13,9},{2,6},{6,2},{1... | collective-permute-start | bytes 245768 | tf_op jit(solution)/shard_map/ppermute | solution.py:1148
  34.5 0.9 %second_field.1 = (f32[32,8,384]{2,1,0:T(8,128)S(1)}, f32[32,8,512]{2,1,0:T(8,128)S(1)}) custom-call(s32[17]{0:T(128)S(1)} %stack.75.flags, f32[160,1024]{1,0:T(8,128)S(1)} %get-tuple-element.72.refs_0_, f32[96,1024]{1,0:T(8,128)S(1)} %get-tuple-element.76.refs_1_, f32[96,384]{1,0:T(8,128)S(1)} %collective-permute-done.5.refs_2_, ...), custom_call_target="tpu_custom_call" | custom-call | flops 1 | bytes 1 | tf_op jit(solution)/shard_map/second_field/pallas_call | solution.py:531
  35.4 1.5 %first_sweep.3 = (f32[32,8,512]{2,1,0:T(8,128)S(1)}, f32[32,8,512]{2,1,0:T(8,128)S(1)}, f32[8,128]{1,0:T(8,128)S(1)}, f32[32,8,512]{2,1,0:T(8,128)S(1)}, f32[32,...) custom-call(s32[17]{0:T(128)S(1)} %stack.75.flags, ...), custom_call_target="tpu_custom_call" | custom-call | flops 1 | bytes 1 | tf_op jit(solution)/shard_map/first_sweep/pallas_call | solution.py:531
  37.4 0.8 %collective-permute-done.6.near = f32[5,8,512]{2,1,0:T(8,128)S(1)} collective-permute-done((f32[5,8,512]{2,1,0:T(8,128)S(1)}, f32[5,8,512]{2,1,0:T(8,128)S(1)}, u32[]{:S(2)}, u32[]{:S(2)}) %collective-permute-start.6) | collective-permute-done | bytes 81952 | tf_op jit(solution)/shard_map/ppermute | solution.py:1148
  38.8 2.7 %collective-permute-start.7 = (f32[2,8,512]{2,1,0:T(8,128)S(1)}, f32[2,8,512]{2,1,0:T(8,128)S(1)}, u32[]{:S(2)}, u32[]{:S(2)}) collective-permute-start(f32[2,8,512]{2,1,0:T(8,128)S(1)} %get-tuple-element.99.refs_0_), channel_id=1, source_target_pairs={{0,8},{8,0},{4,12},{12,4},{1,9},{9,1},{5,13},{13,5},{2,10},{10,2},... | collective-permute-start | bytes 98312 | tf_op jit(solution)/shard_map/ppermute | solution.py:1175
  42.1 2.6 %collective-permute-start.9 = (f32[2,8,512]{2,1,0:T(8,128)S(1)}, f32[2,8,512]{2,1,0:T(8,128)S(1)}, u32[]{:S(2)}, u32[]{:S(2)}) collective-permute-start(f32[2,8,512]{2,1,0:T(8,128)S(1)} %get-tuple-element.101.refs_3_), channel_id=1, source_target_pairs={{0,8},{8,0},{4,12},{12,4},{1,9},{9,1},{5,13},{13,5},{2,10},{10,2},... | collective-permute-start | bytes 98312 | tf_op jit(solution)/shard_map/ppermute | solution.py:1175
  44.7 2.6 %collective-permute-done.9.refs_4_ = f32[2,8,512]{2,1,0:T(8,128)S(1)} collective-permute-done((f32[2,8,512]{2,1,0:T(8,128)S(1)}, f32[2,8,512]{2,1,0:T(8,128)S(1)}, u32[]{:S(2)}, u32[]{:S(2)}) %collective-permute-start.9) | collective-permute-done | bytes 32800 | tf_op jit(solution)/shard_map/ppermute | solution.py:1175
  47.3 1.2 %half.1 = (f32[32,8,1024]{2,1,0:T(8,128)S(1)}, f32[32,1024]{1,0:T(8,128)S(1)}, f32[32,1024]{1,0:T(8,128)S(1)}, f32[8,128]{1,0:T(8,128)S(1)}, f32[2,8,512]{2,1,0:T(8,128)S(1)}) custom-call(s32[17]{0:T(128)S(1)} %stack.75.flags, f32[2,8,512]{2,1,0:T(8,128)S(1)} %get-tuple-element.99.refs_0_, f32[2,8,512]{2,1,0:T(8,128)S(1)} %collective-permute-done.7.refs_1_, ...), custom_call_target="tpu_custom_call" | custom-call | flops 1 | bytes 1 | tf_op jit(solution)/shard_map/half/pallas_call | solution.py:531
  48.5 1.9 %collective-permute-start.11 = (f32[32,1024]{1,0:T(8,128)S(1)}, f32[32,1024]{1,0:T(8,128)S(1)}, u32[]{:S(2)}, u32[]{:S(2)}) collective-permute-start(f32[32,1024]{1,0:T(8,128)S(1)} %get-tuple-element.113), channel_id=1, source_target_pairs={{1,2},{2,1},{5,6},{6,5},{9,10},{10,9},{13,14},{14,13},{17,18},{18,... | collective-permute-start | bytes 393224 | tf_op jit(solution)/shard_map/ppermute | solution.py:995
  51.1 3.0 %collective-permute-done.12.refs_3_ = f32[8,128]{1,0:T(8,128)S(1)} collective-permute-done((f32[8,128]{1,0:T(8,128)S(1)}, f32[8,128]{1,0:T(8,128)S(1)}, u32[]{:S(2)}, u32[]{:S(2)}) %collective-permute-start.12) | collective-permute-done | bytes 4128 | tf_op jit(solution)/shard_map/ppermute | solution.py:996
  54.1 0.7 %collective-permute-done.11.refs_2_ = f32[32,1024]{1,0:T(8,128)S(1)} collective-permute-done((f32[32,1024]{1,0:T(8,128)S(1)}, f32[32,1024]{1,0:T(8,128)S(1)}, u32[]{:S(2)}, u32[]{:S(2)}) %collective-permute-start.11) | collective-permute-done | bytes 131104 | tf_op jit(solution)/shard_map/ppermute | solution.py:995
  54.8 1.6 %second_sweep.1 = (f32[32,8,512]{2,1,0:T(8,128)S(1)}, f32[32,8,512]{2,1,0:T(8,128)S(1)}, f32[2,8,1024]{2,1,0:T(8,128)S(1)}, f32[8,1024]{1,0:T(8,128)S(1)}) custom-call(s32[17]{0:T(128)S(1)} %stack.75.flags, f32[32,8,1024]{2,1,0:T(8,128)S(1)} %get-tuple-element.111.refs_0_.refs_15_, f32[32,1024]{1,0:T(8,128)S(1)} %collective-permute-done.10.refs_1_, ...), custom_call_target="tpu_custom_call" | custom-call | flops 1 | bytes 1 | tf_op jit(solution)/shard_map/second_sweep/pallas_call | solution.py:531
  57.0 3.1 %collective-permute-start.15 = (f32[8,1024]{1,0:T(8,128)S(1)}, f32[8,1024]{1,0:T(8,128)S(1)}, u32[]{:S(2)}, u32[]{:S(2)}) collective-permute-start(f32[8,1024]{1,0:T(8,128)S(1)} %get-tuple-element.122), channel_id=1, source_target_pairs={{0,12},{12,0},{4,8},{8,4},{1,13},{13,1},{5,9},{9,5},{2,14},{14,2},... | collective-permute-start | bytes 98312 | tf_op jit(solution)/shard_map/ppermute | solution.py:1197
  60.1 1.6 %log_perm.1 = f32[32,8,1024]{2,1,0:T(8,128)} custom-call(s32[17]{0:T(128)S(1)} %stack.75.flags, f32[32,8,640]{2,1,0:T(8,128)S(1)} %get-tuple-element.79.near, f32[32,8,384]{2,1,0:T(8,128)S(1)} %get-tuple-element.96.far, f32[5,8,512]{2,1,0:T(8,128)S(1)} %get-tuple-element.98._.own), custom_call_target="tpu_custom_call" | custom-call | flops 1 | bytes 1 | tf_op jit(solution)/shard_map/log_perm/pallas_call | solution.py:531
  61.7 1.0 %collective-permute-done.15.refs_3_ = f32[8,1024]{1,0:T(8,128)S(1)} collective-permute-done((f32[8,1024]{1,0:T(8,128)S(1)}, f32[8,1024]{1,0:T(8,128)S(1)}, u32[]{:S(2)}, u32[]{:S(2)}) %collective-permute-start.15) | collective-permute-done | bytes 32800 | tf_op jit(solution)/shard_map/ppermute | solution.py:1197
  62.7 2.2 %collective-permute-done.14.refs_2_ = f32[8,1024]{1,0:T(8,128)S(1)} collective-permute-done((f32[8,1024]{1,0:T(8,128)S(1)}, f32[8,1024]{1,0:T(8,128)S(1)}, u32[]{:S(2)}, u32[]{:S(2)}) %collective-permute-start.14) | collective-permute-done | bytes 32800 | tf_op jit(solution)/shard_map/ppermute | solution.py:1197
  65.0 1.8 %smoothed.1 = f32[32,8,1024]{2,1,0:T(8,128)} custom-call(s32[17]{0:T(128)S(1)} %stack.75.flags, f32[2,8,1024]{2,1,0:T(8,128)S(1)} %get-tuple-element.121.refs_0_, f32[2,8,1024]{2,1,0:T(8,128)S(1)} %collective-permute-done.13.refs_1_, f32[8,1024]{1,0:T(8,128)S(1)} %collective-permute-done.14.refs_2_, f32[8,1024]{1,0:T(8,128)S(1)} %collective-permute-done.15.refs_3_, ...), custom_call_target="tpu_custom_call" | custom-call | flops 1 | bytes 1 | tf_op jit(solution)/shard_map/smoothed/pallas_call | solution.py:531
  (36 shorter events, 3.7 us)
Async XLA Ops:
  0.6 6.3 %copy-start.8 = (s32[32,8]{0,1:T(8,128)S(1)}, s32[32,8]{0,1:T(8,128)}, u32[]{:S(2)}) copy-start(s32[32,8]{0,1:T(8,128)} %param.6) | copy-start | bytes 3076
  0.6 6.3 %copy-start = (f32[2,32,8,1024]{3,2,1,0:T(8,128)S(1)}, f32[2,32,8,1024]{3,2,1,0:T(8,128)}, u32[]{:S(2)}) copy-start(f32[2,32,8,1024]{3,2,1,0:T(8,128)} %param.5) | copy-start | bytes 6291460
  5.4 8.4 %collective-permute-start = (f32[64,1024]{1,0:T(8,128)}, f32[64,1024]{1,0:T(8,128)}, u32[]{:S(2)}, u32[]{:S(2)}) collective-permute-start(f32[64,1024]{1,0:T(8,128)} %get-tuple-element.65), channel_id=1, source_target_pairs={{0,16},{16,0},{1,17},{17,1},{2,18},{18,2},{3,19},{19,3},{4,20},{20... | collective-permute-start | bytes 786440 | tf_op jit(solution)/shard_map/ppermute | solution.py:1073
  7.0 1.2 %copy-start.1 = (f32[32,8,1024]{2,1,0:T(8,128)S(1)}, f32[32,8,1024]{2,1,0:T(8,128)}, u32[]{:S(2)}) copy-start(f32[32,8,1024]{2,1,0:T(8,128)} %refs_14_.1) | copy-start | bytes 3145732
  8.2 5.6 %copy-start.2 = (f32[32,8,1024]{2,1,0:T(8,128)S(1)}, f32[32,8,1024]{2,1,0:T(8,128)}, u32[]{:S(2)}) copy-start(f32[32,8,1024]{2,1,0:T(8,128)} %refs_14_.1) | copy-start | bytes 3145732
  8.2 5.6 %copy-start.4 = (f32[64,1024]{1,0:T(8,128)S(1)}, f32[64,1024]{1,0:T(8,128)}, u32[]{:S(2)}) copy-start(f32[64,1024]{1,0:T(8,128)} %get-tuple-element.64.own.refs_0_) | copy-start | bytes 786436
  8.2 9.3 %copy-start.9 = (f32[6,2,128]{2,1,0:T(2,128)S(1)}, f32[6,2,128]{2,1,0:T(2,128)}, u32[]{:S(2)}) copy-start(f32[6,2,128]{2,1,0:T(2,128)} %get-tuple-element.73.outer_kept) | copy-start | bytes 18436
  11.6 0.7 %copy-start.5 = (f32[96,1024]{1,0:T(8,128)}, f32[96,1024]{1,0:T(8,128)S(1)}, u32[]{:S(2)}) copy-start(f32[96,1024]{1,0:T(8,128)S(1)} %get-tuple-element.67.refs_2_) | copy-start | bytes 1179652
  12.4 12.4 %collective-permute-start.1 = (f32[96,1024]{1,0:T(8,128)}, f32[96,1024]{1,0:T(8,128)}, u32[]{:S(2)}, u32[]{:S(2)}) collective-permute-start(f32[96,1024]{1,0:T(8,128)} %get-tuple-element.68), channel_id=1, source_target_pairs={{0,16},{16,0},{1,17},{17,1},{2,18},{18,2},{3,19},{19,3},{4,20},{20... | collective-permute-start | bytes 1179656 | tf_op jit(solution)/shard_map/ppermute | solution.py:1085
  13.0 11.8 %copy-start.6 = (f32[96,1024]{1,0:T(8,128)S(1)}, f32[96,1024]{1,0:T(8,128)}, u32[]{:S(2)}) copy-start(f32[96,1024]{1,0:T(8,128)} %copy-done.5) | copy-start | bytes 1179652
  15.1 9.6 %collective-permute-start.2 = (f32[64,1024]{1,0:T(8,128)S(1)}, f32[64,1024]{1,0:T(8,128)S(1)}, u32[]{:S(2)}, u32[]{:S(2)}) collective-permute-start(f32[64,1024]{1,0:T(8,128)S(1)} %get-tuple-element.70.refs_4_), channel_id=1, source_target_pairs={{0,1},{1,0},{2,3},{3,2},{4,5},{5,4},{6,7},{7,6},{8,9},{9,8},{10,11... | collective-permute-start | bytes 786440 | tf_op jit(solution)/shard_map/ppermute | solution.py:994
  15.2 9.6 %collective-permute-start.3 = (f32[64,1024]{1,0:T(8,128)S(1)}, f32[64,1024]{1,0:T(8,128)S(1)}, u32[]{:S(2)}, u32[]{:S(2)}) collective-permute-start(f32[64,1024]{1,0:T(8,128)S(1)} %get-tuple-element.71.refs_5_), channel_id=1, source_target_pairs={{1,2},{2,1},{5,6},{6,5},{9,10},{10,9},{13,14},{14,13},{17,18},{18,... | collective-permute-start | bytes 786440 | tf_op jit(solution)/shard_map/ppermute | solution.py:995
  20.1 11.2 %copy-start.3 = (f32[32,8,1024]{2,1,0:T(8,128)S(1)}, f32[32,8,1024]{2,1,0:T(8,128)}, u32[]{:S(2)}) copy-start(f32[32,8,1024]{2,1,0:T(8,128)} %refs_4_.1) | copy-start | bytes 3145732
  20.2 10.2 %collective-permute-start.4 = (f32[104,640]{1,0:T(8,128)S(1)}, f32[104,640]{1,0:T(8,128)S(1)}, u32[]{:S(2)}, u32[]{:S(2)}) collective-permute-start(f32[104,640]{1,0:T(8,128)S(1)} %get-tuple-element.77), channel_id=1, source_target_pairs={{0,16},{16,0},{1,17},{17,1},{2,18},{18,2},{3,19},{19,3},{4,20},{20... | collective-permute-start | bytes 798728 | tf_op jit(solution)/shard_map/ppermute | solution.py:1111
  26.5 8.0 %collective-permute-start.5 = (f32[96,384]{1,0:T(8,128)S(1)}, f32[96,384]{1,0:T(8,128)S(1)}, u32[]{:S(2)}, u32[]{:S(2)}) collective-permute-start(f32[96,384]{1,0:T(8,128)S(1)} %get-tuple-element.81), channel_id=1, source_target_pairs={{0,16},{16,0},{1,17},{17,1},{2,18},{18,2},{3,19},{19,3},{4,20},{20... | collective-permute-start | bytes 442376 | tf_op jit(solution)/shard_map/ppermute | solution.py:1124
  32.9 5.3 %collective-permute-start.6 = (f32[5,8,512]{2,1,0:T(8,128)S(1)}, f32[5,8,512]{2,1,0:T(8,128)S(1)}, u32[]{:S(2)}, u32[]{:S(2)}) collective-permute-start(f32[5,8,512]{2,1,0:T(8,128)S(1)} %get-tuple-element.94.own), channel_id=1, source_target_pairs={{0,4},{4,0},{8,12},{12,8},{1,5},{5,1},{9,13},{13,9},{2,6},{6,2},{1... | collective-permute-start | bytes 245768 | tf_op jit(solution)/shard_map/ppermute | solution.py:1148
  35.4 11.9 %copy-start.7 = (s32[8,1024]{1,0:T(8,128)S(1)}, s32[8,1024]{1,0:T(8,128)}, u32[]{:S(2)}) copy-start(s32[8,1024]{1,0:T(8,128)} %refs_16_.1) | copy-start | bytes 98308
  36.9 4.6 %collective-permute-start.8 = (f32[5,8,512]{2,1,0:T(8,128)S(1)}, f32[5,8,512]{2,1,0:T(8,128)S(1)}, u32[]{:S(2)}, u32[]{:S(2)}) collective-permute-start(f32[5,8,512]{2,1,0:T(8,128)S(1)} %get-tuple-element.98._.own), channel_id=1, source_target_pairs={{0,4},{4,0},{8,12},{12,8},{1,5},{5,1},{9,13},{13,9},{2,6},{6,2},{1... | collective-permute-start | bytes 245768 | tf_op jit(solution)/shard_map/ppermute | solution.py:1159
  38.8 5.9 %collective-permute-start.7 = (f32[2,8,512]{2,1,0:T(8,128)S(1)}, f32[2,8,512]{2,1,0:T(8,128)S(1)}, u32[]{:S(2)}, u32[]{:S(2)}) collective-permute-start(f32[2,8,512]{2,1,0:T(8,128)S(1)} %get-tuple-element.99.refs_0_), channel_id=1, source_target_pairs={{0,8},{8,0},{4,12},{12,4},{1,9},{9,1},{5,13},{13,5},{2,10},{10,2},... | collective-permute-start | bytes 98312 | tf_op jit(solution)/shard_map/ppermute | solution.py:1175
  42.1 5.2 %collective-permute-start.9 = (f32[2,8,512]{2,1,0:T(8,128)S(1)}, f32[2,8,512]{2,1,0:T(8,128)S(1)}, u32[]{:S(2)}, u32[]{:S(2)}) collective-permute-start(f32[2,8,512]{2,1,0:T(8,128)S(1)} %get-tuple-element.101.refs_3_), channel_id=1, source_target_pairs={{0,8},{8,0},{4,12},{12,4},{1,9},{9,1},{5,13},{13,5},{2,10},{10,2},... | collective-permute-start | bytes 98312 | tf_op jit(solution)/shard_map/ppermute | solution.py:1175
  48.5 5.7 %collective-permute-start.10 = (f32[32,1024]{1,0:T(8,128)S(1)}, f32[32,1024]{1,0:T(8,128)S(1)}, u32[]{:S(2)}, u32[]{:S(2)}) collective-permute-start(f32[32,1024]{1,0:T(8,128)S(1)} %get-tuple-element.112), channel_id=1, source_target_pairs={{0,1},{1,0},{2,3},{3,2},{4,5},{5,4},{6,7},{7,6},{8,9},{9,8},{10,11... | collective-permute-start | bytes 393224 | tf_op jit(solution)/shard_map/ppermute | solution.py:994
  48.5 6.3 %collective-permute-start.11 = (f32[32,1024]{1,0:T(8,128)S(1)}, f32[32,1024]{1,0:T(8,128)S(1)}, u32[]{:S(2)}, u32[]{:S(2)}) collective-permute-start(f32[32,1024]{1,0:T(8,128)S(1)} %get-tuple-element.113), channel_id=1, source_target_pairs={{1,2},{2,1},{5,6},{6,5},{9,10},{10,9},{13,14},{14,13},{17,18},{18,... | collective-permute-start | bytes 393224 | tf_op jit(solution)/shard_map/ppermute | solution.py:995
  50.5 3.7 %collective-permute-start.12 = (f32[8,128]{1,0:T(8,128)S(1)}, f32[8,128]{1,0:T(8,128)S(1)}, u32[]{:S(2)}, u32[]{:S(2)}) collective-permute-start(f32[8,128]{1,0:T(8,128)S(1)} %get-tuple-element.114), channel_id=1, source_target_pairs={{0,16},{16,0},{1,17},{17,1},{2,18},{18,2},{3,19},{19,3},{4,20},{20... | collective-permute-start | bytes 12296 | tf_op jit(solution)/shard_map/ppermute | solution.py:996
  56.4 8.5 %collective-permute-start.13 = (f32[2,8,1024]{2,1,0:T(8,128)S(1)}, f32[2,8,1024]{2,1,0:T(8,128)S(1)}, u32[]{:S(2)}, u32[]{:S(2)}) collective-permute-start(f32[2,8,1024]{2,1,0:T(8,128)S(1)} %get-tuple-element.121.refs_0_), channel_id=1, source_target_pairs={{0,4},{4,0},{8,12},{12,8},{1,5},{5,1},{9,13},{13,9},{2,6},{6,2},{1... | collective-permute-start | bytes 196616 | tf_op jit(solution)/shard_map/ppermute | solution.py:1197
  57.0 5.7 %collective-permute-start.15 = (f32[8,1024]{1,0:T(8,128)S(1)}, f32[8,1024]{1,0:T(8,128)S(1)}, u32[]{:S(2)}, u32[]{:S(2)}) collective-permute-start(f32[8,1024]{1,0:T(8,128)S(1)} %get-tuple-element.122), channel_id=1, source_target_pairs={{0,12},{12,0},{4,8},{8,4},{1,13},{13,1},{5,9},{9,5},{2,14},{14,2},... | collective-permute-start | bytes 98312 | tf_op jit(solution)/shard_map/ppermute | solution.py:1197
  60.1 4.8 %collective-permute-start.14 = (f32[8,1024]{1,0:T(8,128)S(1)}, f32[8,1024]{1,0:T(8,128)S(1)}, u32[]{:S(2)}, u32[]{:S(2)}) collective-permute-start(f32[8,1024]{1,0:T(8,128)S(1)} %get-tuple-element.122), channel_id=1, source_target_pairs={{0,8},{8,0},{4,12},{12,4},{1,9},{9,1},{5,13},{13,5},{2,10},{10,2},... | collective-permute-start | bytes 98312 | tf_op jit(solution)/shard_map/ppermute | solution.py:1197

commit v3 on v2

--- a/solution.py
+++ b/solution.py
@@ -515,7 +515,6 @@
         one[extra, at * LANES : (at + 1) * LANES] = piece
 
 
-SCALARS = pl.BlockSpec(memory_space=pltpu.SMEM)
 ON_CHIP = pl.BlockSpec(memory_space=pltpu.VMEM)
 IN_HBM = pl.BlockSpec(memory_space=pltpu.HBM)
 
@@ -525,11 +524,9 @@
 ):
     specs = [ON_CHIP] * len(args) + [IN_HBM] * len(far)
     args = list(args) + list(far)
-    if flags is not None:
-        specs = [SCALARS] + specs
-        args = [flags] + args
+    body = kernel if flags is None else lambda *refs: kernel(flags(), *refs)
     return pl.pallas_call(
-        kernel,
+        body,
         out_shape=out_shape,
         in_specs=specs,
         out_specs=jax.tree.map(lambda _: out, out_shape),
@@ -1002,37 +999,37 @@
     vert = float((depth * 4) ** 2 // 4)
     waves = spectral.shape[3]
     rows = depth * items
-    gx, gz, gy = (lax.axis_index(axis) for axis in ("gx", "gz", "gy"))
     block_size, third = width // 2, 3 * width // 8
     known = width - third
 
-    def placed(start, size):
-        return jnp.where(gx == 1, start, width - start - size)
-
-    block_one, block_two = placed(0, block_size), placed(block_size, block_size)
-    start_one = placed(0, known)
-    extra = known - block_size
-    flags = jnp.stack(
-        [
+    def flags():
+        gx, gz, gy = (lax.axis_index(axis) for axis in ("gx", "gz", "gy"))
+
+        def placed(start, size):
+            return jnp.where(gx == 1, start, width - start - size)
+
+        block_one, block_two = placed(0, block_size), placed(block_size, block_size)
+        start_one = placed(0, known)
+        extra = known - block_size
+        return [
             gx,
             placed(0, LANES),
             placed(LANES, known - LANES),
             start_one,
-            jnp.zeros_like(gx),
+            gx,
             placed(known, third),
             block_one,
             block_two,
             placed(block_size, extra) - block_two,
             placed(block_size, extra) - start_one,
             block_one - start_one,
-            jnp.zeros_like(gx),
+            0,
             gy > 0,
             gy < 3,
             gz,
-            (gy == 1) | (gy == 2),
+            ((gy == 1) | (gy == 2)).astype(jnp.int32),
             gy % 2,
         ]
-    ).astype(jnp.int32)
 
     def shaped(*shape, dtype=F32):
         return jax.ShapeDtypeStruct(shape, dtype)

time: 67 us -> 61.3 us (0.915)
  the two profiles are of different devices: /device:TPU:2 before, /device:TPU:6 now
where the time goes in v3:
time: 61.3 us; the launch traced here: 61.1 us
  waiting for transfers between devices  23.3 us (38%)
  starting transfers between devices  18.2 us (30%)
  Pallas kernels  17.6 us (29%)
  local copies, waits for them, and re-layouts  1.26 us (2%)
  between operations  0.81 us (1%)
    pallas_call x15, Pallas kernels, call(): pl.pallas_call(body, out_shape=out_shape, in_specs=specs, out_specs=jax.t...  17.6 us
    ppermute x1, waiting for transfers between devices, fast_body(): last_one = lax.ppermute(last_one, 'gx', PAIR)  5.52 us
    ppermute x2, starting transfers between devices, join(): return (across, lax.ppermute(across, 'gz', SKIP), kept)  4.95 us
    ppermute x2, starting transfers between devices, exchange_edges(): lax.ppermute(to_middle, 'gy', MIDDLE)  4.45 us
    ppermute x3, starting transfers between devices, fast_body(): lax.ppermute(planes, 'gz', pairs)  3.77 us
    ppermute x3, waiting for transfers between devices, fast_body(): lax.ppermute(planes, 'gz', pairs)  3.76 us
    ppermute x1, waiting for transfers between devices, exchange_edges(): lax.ppermute(piece, 'gx', PAIR)  3.47 us
    ppermute x1, waiting for transfers between devices, fast_body(): outer = lax.ppermute(sums, 'gx', PAIR)  3.22 us
  transfers between devices with their start and end apart: 16, of which 11 were waited for; matrix products, arithmetic and copies ran while one was open for 0% of the time, Pallas kernels for 17%

profile of v3, /device:TPU:6, one launch (start us, length us, event | category | flops | bytes accessed | tf_op | source)
XLA Modules:
  0.0 61.1 jit_solution(1106962179779885858)
XLA Ops:
  0.6 4.7 %outer_row_sums.1 = (f32[64,1024]{1,0:T(8,128)}, f32[64,1024]{1,0:T(8,128)}, f32[6,2,128]{2,1,0:T(2,128)}) custom-call(s32[8,32]{1,0:T(8,128)} %bitcast.5, f32[2,256,1024]{2,1,0:T(8,128)} %bitcast.2), custom_call_target="tpu_custom_call" | custom-call | flops 1 | bytes 1 | tf_op jit(solution)/shard_map/outer_row_sums/pallas_call | solution.py:528
  5.4 0.6 collective-permute-start
  5.9 1.2 %copy-done.1 = f32[32,8,1024]{2,1,0:T(8,128)S(1)} copy-done((f32[32,8,1024]{2,1,0:T(8,128)S(1)}, f32[32,8,1024]{2,1,0:T(8,128)}, u32[]{:S(2)}) %copy-start.1) | copy-done | bytes 1048600
  7.2 2.8 %inner_row_sums.1 = (f32[96,1024]{1,0:T(8,128)S(1)}, f32[96,1024]{1,0:T(8,128)S(1)}, f32[6,3,128]{2,1,0:T(4,128)S(1)}, f32[8,128]{1,0:T(8,128)S(1)}) custom-call(s32[8,32]{1,0:T(8,128)S(1)} %bitcast.6, f32[2,256,1024]{2,1,0:T(8,128)S(1)} %bitcast.3, f32[32,8,1024]{2,1,0:T(8,128)S(1)} %copy-done.1), custom_call_target="tpu_custom_call" | custom-call | flops 1 | bytes 1 | tf_op jit(solution)/shard_map/inner_row_sums/pallas_call | solution.py:528
  10.0 1.6 %collective-permute-start.1 = (f32[96,1024]{1,0:T(8,128)S(1)}, f32[96,1024]{1,0:T(8,128)S(1)}, u32[]{:S(2)}, u32[]{:S(2)}) collective-permute-start(f32[96,1024]{1,0:T(8,128)S(1)} %get-tuple-element.68), channel_id=1, source_target_pairs={{0,16},{16,0},{1,17},{17,1},{2,18},{18,2},{3,19},{19,3},{4,20},{20... | collective-permute-start | bytes 1179656 | tf_op jit(solution)/shard_map/ppermute | solution.py:1082
  11.6 3.2 %collective-permute-done.refs_1_ = f32[64,1024]{1,0:T(8,128)S(1)} collective-permute-done((f32[64,1024]{1,0:T(8,128)}, f32[64,1024]{1,0:T(8,128)S(1)}, u32[]{:S(2)}, u32[]{:S(2)}) %collective-permute-start) | collective-permute-done | bytes 262176 | tf_op jit(solution)/shard_map/ppermute | solution.py:1070
  15.2 2.5 %collective-permute-start.3 = (f32[64,1024]{1,0:T(8,128)S(1)}, f32[64,1024]{1,0:T(8,128)S(1)}, u32[]{:S(2)}, u32[]{:S(2)}) collective-permute-start(f32[64,1024]{1,0:T(8,128)S(1)} %get-tuple-element.71.refs_5_), channel_id=1, source_target_pairs={{1,2},{2,1},{5,6},{6,5},{9,10},{10,9},{13,14},{14,13},{17,18},{18,... | collective-permute-start | bytes 786440 | tf_op jit(solution)/shard_map/ppermute | solution.py:992
  17.8 2.7 %last_row_sums.1 = (f32[104,640]{1,0:T(8,128)S(1)}, f32[96,384]{1,0:T(8,128)S(1)}, f32[96,1024]{1,0:T(8,128)S(1)}, f32[6,8,128]{2,1,0:T(8,128)S(1)}) custom-call(s32[8,32]{1,0:T(8,128)S(1)} %bitcast.7, f32[6,2,128]{2,1,0:T(2,128)S(1)} %copy-done.7, f32[6,3,128]{2,1,0:T(4,128)S(1)} %get-tuple-element.74.inner_kept, f32[8,128]{1,0:T(8,128)S(1)} %get-tuple-element.75.p_column, ...), custom_call_target="tpu_custom_call" | custom-call | flops 1 | bytes 1 | tf_op jit(solution)/shard_map/last_row_sums/pallas_call | solution.py:528
  20.5 1.9 %collective-permute-done.1.refs_3_ = f32[96,1024]{1,0:T(8,128)S(1)} collective-permute-done((f32[96,1024]{1,0:T(8,128)S(1)}, f32[96,1024]{1,0:T(8,128)S(1)}, u32[]{:S(2)}, u32[]{:S(2)}) %collective-permute-start.1) | collective-permute-done | bytes 393248 | tf_op jit(solution)/shard_map/ppermute | solution.py:1082
  22.9 0.7 %wide_field.1 = (f32[160,1024]{1,0:T(8,128)S(1)}, f32[32,1024]{1,0:T(8,128)S(1)}, f32[32,1024]{1,0:T(8,128)S(1)}, f32[32,8,1024]{2,1,0:T(8,128)S(1)}, f32[32,8,1...) custom-call(f32[64,1024]{1,0:T(8,128)S(1)} %copy-done.4, ...), custom_call_target="tpu_custom_call" | custom-call | flops 1 | bytes 1 | tf_op jit(solution)/shard_map/wide_field/pallas_call | solution.py:528
  23.9 5.5 %collective-permute-done.4.refs_2_ = f32[104,640]{1,0:T(8,128)S(1)} collective-permute-done((f32[104,640]{1,0:T(8,128)S(1)}, f32[104,640]{1,0:T(8,128)S(1)}, u32[]{:S(2)}, u32[]{:S(2)}) %collective-permute-start.4) | collective-permute-done | bytes 266272 | tf_op jit(solution)/shard_map/ppermute | solution.py:1108
  29.4 0.5 first_field.1
  29.9 0.9 %first_sweep.2 = (f32[32,8,512]{2,1,0:T(8,128)S(1)}, f32[32,8,512]{2,1,0:T(8,128)S(1)}, f32[8,128]{1,0:T(8,128)S(1)}, f32[32,8,512]{2,1,0:T(8,128)S(1)}, f32[32,...) custom-call(f32[32,8,640]{2,1,0:T(8,128)S(1)} %get-tuple-element.82.refs_0, ...), custom_call_target="tpu_custom_call" | custom-call | flops 1 | bytes 1 | tf_op jit(solution)/shard_map/first_sweep/pallas_call | solution.py:528
  30.9 1.6 %collective-permute-start.6 = (f32[5,8,512]{2,1,0:T(8,128)S(1)}, f32[5,8,512]{2,1,0:T(8,128)S(1)}, u32[]{:S(2)}, u32[]{:S(2)}) collective-permute-start(f32[5,8,512]{2,1,0:T(8,128)S(1)} %get-tuple-element.94.refs_0_), channel_id=1, source_target_pairs={{0,4},{4,0},{8,12},{12,8},{1,5},{5,1},{9,13},{13,9},{2,6},{6,2},{1... | collective-permute-start | bytes 245768 | tf_op jit(solution)/shard_map/ppermute | solution.py:1145
  32.9 0.9 %first_sweep.3 = (f32[32,8,512]{2,1,0:T(8,128)S(1)}, f32[32,8,512]{2,1,0:T(8,128)S(1)}, f32[8,128]{1,0:T(8,128)S(1)}, f32[32,8,512]{2,1,0:T(8,128)S(1)}, f32[32,...) custom-call(f32[32,8,512]{2,1,0:T(8,128)S(1)} %get-tuple-element.97.refs_0, ...), custom_call_target="tpu_custom_call" | custom-call | flops 1 | bytes 1 | tf_op jit(solution)/shard_map/first_sweep/pallas_call | solution.py:528
  33.8 0.5 collective-permute-start.8
  34.3 1.1 %collective-permute-done.6.refs_1_ = f32[5,8,512]{2,1,0:T(8,128)S(1)} collective-permute-done((f32[5,8,512]{2,1,0:T(8,128)S(1)}, f32[5,8,512]{2,1,0:T(8,128)S(1)}, u32[]{:S(2)}, u32[]{:S(2)}) %collective-permute-start.6) | collective-permute-done | bytes 81952 | tf_op jit(solution)/shard_map/ppermute | solution.py:1145
  35.4 2.6 %collective-permute-start.7 = (f32[2,8,512]{2,1,0:T(8,128)S(1)}, f32[2,8,512]{2,1,0:T(8,128)S(1)}, u32[]{:S(2)}, u32[]{:S(2)}) collective-permute-start(f32[2,8,512]{2,1,0:T(8,128)S(1)} %get-tuple-element.99.refs_0_), channel_id=1, source_target_pairs={{0,8},{8,0},{4,12},{12,4},{1,9},{9,1},{5,13},{13,5},{2,10},{10,2},... | collective-permute-start | bytes 98312 | tf_op jit(solution)/shard_map/ppermute | solution.py:1172
  38.1 0.6 collective-permute-done.8.refs_1_
  38.7 2.3 %collective-permute-start.9 = (f32[2,8,512]{2,1,0:T(8,128)S(1)}, f32[2,8,512]{2,1,0:T(8,128)S(1)}, u32[]{:S(2)}, u32[]{:S(2)}) collective-permute-start(f32[2,8,512]{2,1,0:T(8,128)S(1)} %get-tuple-element.101.refs_3_), channel_id=1, source_target_pairs={{0,8},{8,0},{4,12},{12,4},{1,9},{9,1},{5,13},{13,5},{2,10},{10,2},... | collective-permute-start | bytes 98312 | tf_op jit(solution)/shard_map/ppermute | solution.py:1172
  41.0 2.6 %collective-permute-done.9.refs_4_ = f32[2,8,512]{2,1,0:T(8,128)S(1)} collective-permute-done((f32[2,8,512]{2,1,0:T(8,128)S(1)}, f32[2,8,512]{2,1,0:T(8,128)S(1)}, u32[]{:S(2)}, u32[]{:S(2)}) %collective-permute-start.9) | collective-permute-done | bytes 32800 | tf_op jit(solution)/shard_map/ppermute | solution.py:1172
  43.6 0.5 half.1
  44.1 1.9 %collective-permute-start.11 = (f32[32,1024]{1,0:T(8,128)S(1)}, f32[32,1024]{1,0:T(8,128)S(1)}, u32[]{:S(2)}, u32[]{:S(2)}) collective-permute-start(f32[32,1024]{1,0:T(8,128)S(1)} %get-tuple-element.113), channel_id=1, source_target_pairs={{1,2},{2,1},{5,6},{6,5},{9,10},{10,9},{13,14},{14,13},{17,18},{18,... | collective-permute-start | bytes 393224 | tf_op jit(solution)/shard_map/ppermute | solution.py:992
  46.3 3.5 %collective-permute-done.12.refs_3_ = f32[8,128]{1,0:T(8,128)S(1)} collective-permute-done((f32[8,128]{1,0:T(8,128)S(1)}, f32[8,128]{1,0:T(8,128)S(1)}, u32[]{:S(2)}, u32[]{:S(2)}) %collective-permute-start.12) | collective-permute-done | bytes 4128 | tf_op jit(solution)/shard_map/ppermute | solution.py:993
  49.7 0.7 %collective-permute-done.11.refs_2_ = f32[32,1024]{1,0:T(8,128)S(1)} collective-permute-done((f32[32,1024]{1,0:T(8,128)S(1)}, f32[32,1024]{1,0:T(8,128)S(1)}, u32[]{:S(2)}, u32[]{:S(2)}) %collective-permute-start.11) | collective-permute-done | bytes 131104 | tf_op jit(solution)/shard_map/ppermute | solution.py:992
  50.4 1.0 %second_sweep.1 = (f32[32,8,512]{2,1,0:T(8,128)S(1)}, f32[32,8,512]{2,1,0:T(8,128)S(1)}, f32[2,8,1024]{2,1,0:T(8,128)S(1)}, f32[8,1024]{1,0:T(8,128)S(1)}) custom-call(f32[32,8,1024]{2,1,0:T(8,128)S(1)} %get-tuple-element.111.refs_0_.refs_15_, f32[32,1024]{1,0:T(8,128)S(1)} %collective-permute-done.10.refs_1_, ...), custom_call_target="tpu_custom_call" | custom-call | flops 1 | bytes 1 | tf_op jit(solution)/shard_map/second_sweep/pallas_call | solution.py:528
  51.5 1.4 %collective-permute-start.13 = (f32[2,8,1024]{2,1,0:T(8,128)S(1)}, f32[2,8,1024]{2,1,0:T(8,128)S(1)}, u32[]{:S(2)}, u32[]{:S(2)}) collective-permute-start(f32[2,8,1024]{2,1,0:T(8,128)S(1)} %get-tuple-element.121.refs_0_), channel_id=1, source_target_pairs={{0,4},{4,0},{8,12},{12,8},{1,5},{5,1},{9,13},{13,9},{2,6},{6,2},{1... | collective-permute-start | bytes 196616 | tf_op jit(solution)/shard_map/ppermute | solution.py:1194
  52.9 2.3 %collective-permute-start.15 = (f32[8,1024]{1,0:T(8,128)S(1)}, f32[8,1024]{1,0:T(8,128)S(1)}, u32[]{:S(2)}, u32[]{:S(2)}) collective-permute-start(f32[8,1024]{1,0:T(8,128)S(1)} %get-tuple-element.122), channel_id=1, source_target_pairs={{0,12},{12,0},{4,8},{8,4},{1,13},{13,1},{5,9},{9,5},{2,14},{14,2},... | collective-permute-start | bytes 98312 | tf_op jit(solution)/shard_map/ppermute | solution.py:1194
  55.2 1.1 %log_perm.1 = f32[32,8,1024]{2,1,0:T(8,128)} custom-call(f32[32,8,640]{2,1,0:T(8,128)S(1)} %get-tuple-element.79.refs_0_, f32[32,8,384]{2,1,0:T(8,128)S(1)} %get-tuple-element.96.refs_1_, f32[5,8,512]{2,1,0:T(8,128)S(1)} %get-tuple-element.98.refs_2_.refs_0_), custom_call_target="tpu_custom_call" | custom-call | flops 1 | bytes 1 | tf_op jit(solution)/shard_map/log_perm/pallas_call | solution.py:528
  56.3 2.3 %collective-permute-done.15.refs_3_ = f32[8,1024]{1,0:T(8,128)S(1)} collective-permute-done((f32[8,1024]{1,0:T(8,128)S(1)}, f32[8,1024]{1,0:T(8,128)S(1)}, u32[]{:S(2)}, u32[]{:S(2)}) %collective-permute-start.15) | collective-permute-done | bytes 32800 | tf_op jit(solution)/shard_map/ppermute | solution.py:1194
  58.6 1.4 %collective-permute-done.14.refs_2_ = f32[8,1024]{1,0:T(8,128)S(1)} collective-permute-done((f32[8,1024]{1,0:T(8,128)S(1)}, f32[8,1024]{1,0:T(8,128)S(1)}, u32[]{:S(2)}, u32[]{:S(2)}) %collective-permute-start.14) | collective-permute-done | bytes 32800 | tf_op jit(solution)/shard_map/ppermute | solution.py:1194
  60.0 1.1 %smoothed.1 = f32[32,8,1024]{2,1,0:T(8,128)} custom-call(f32[2,8,1024]{2,1,0:T(8,128)S(1)} %get-tuple-element.121.refs_0_, f32[2,8,1024]{2,1,0:T(8,128)S(1)} %collective-permute-done.13.refs_1_, f32[8,1024]{1,0:T(8,128)S(1)} %collective-permute-done.14.refs_2_, f32[8,1024]{1,0:T(8,128)S(1)} %collective-permute-done.15.refs_3_, ...), custom_call_target="tpu_custom_call" | custom-call | flops 1 | bytes 1 | tf_op jit(solution)/shard_map/smoothed/pallas_call | solution.py:528
  (31 shorter events, 1.9 us)
Async XLA Ops:
  0.6 5.3 %copy-start.6 = (s32[32,8]{0,1:T(8,128)S(1)}, s32[32,8]{0,1:T(8,128)}, u32[]{:S(2)}) copy-start(s32[32,8]{0,1:T(8,128)} %param.6) | copy-start | bytes 3076
  0.6 5.3 %copy-start = (f32[2,32,8,1024]{3,2,1,0:T(8,128)S(1)}, f32[2,32,8,1024]{3,2,1,0:T(8,128)}, u32[]{:S(2)}) copy-start(f32[2,32,8,1024]{3,2,1,0:T(8,128)} %param.5) | copy-start | bytes 6291460
  5.4 9.5 %collective-permute-start = (f32[64,1024]{1,0:T(8,128)}, f32[64,1024]{1,0:T(8,128)S(1)}, u32[]{:S(2)}, u32[]{:S(2)}) collective-permute-start(f32[64,1024]{1,0:T(8,128)} %get-tuple-element.65), channel_id=1, source_target_pairs={{0,16},{16,0},{1,17},{17,1},{2,18},{18,2},{3,19},{19,3},{4,20},{20... | collective-permute-start | bytes 786440 | tf_op jit(solution)/shard_map/ppermute | solution.py:1070
  5.9 1.2 %copy-start.1 = (f32[32,8,1024]{2,1,0:T(8,128)S(1)}, f32[32,8,1024]{2,1,0:T(8,128)}, u32[]{:S(2)}) copy-start(f32[32,8,1024]{2,1,0:T(8,128)} %refs_14_.1) | copy-start | bytes 3145732
  7.2 7.7 %copy-start.2 = (f32[32,8,1024]{2,1,0:T(8,128)S(1)}, f32[32,8,1024]{2,1,0:T(8,128)}, u32[]{:S(2)}) copy-start(f32[32,8,1024]{2,1,0:T(8,128)} %refs_14_.1) | copy-start | bytes 3145732
  7.2 7.7 %copy-start.4 = (f32[64,1024]{1,0:T(8,128)S(1)}, f32[64,1024]{1,0:T(8,128)}, u32[]{:S(2)}) copy-start(f32[64,1024]{1,0:T(8,128)} %get-tuple-element.64.refs_0_) | copy-start | bytes 786436
  7.2 10.6 %copy-start.7 = (f32[6,2,128]{2,1,0:T(2,128)S(1)}, f32[6,2,128]{2,1,0:T(2,128)}, u32[]{:S(2)}) copy-start(f32[6,2,128]{2,1,0:T(2,128)} %get-tuple-element.73.outer_kept) | copy-start | bytes 18436
  10.0 12.4 %collective-permute-start.1 = (f32[96,1024]{1,0:T(8,128)S(1)}, f32[96,1024]{1,0:T(8,128)S(1)}, u32[]{:S(2)}, u32[]{:S(2)}) collective-permute-start(f32[96,1024]{1,0:T(8,128)S(1)} %get-tuple-element.68), channel_id=1, source_target_pairs={{0,16},{16,0},{1,17},{17,1},{2,18},{18,2},{3,19},{19,3},{4,20},{20... | collective-permute-start | bytes 1179656 | tf_op jit(solution)/shard_map/ppermute | solution.py:1082
  15.1 7.3 %collective-permute-start.2 = (f32[64,1024]{1,0:T(8,128)S(1)}, f32[64,1024]{1,0:T(8,128)S(1)}, u32[]{:S(2)}, u32[]{:S(2)}) collective-permute-start(f32[64,1024]{1,0:T(8,128)S(1)} %get-tuple-element.70.refs_4_), channel_id=1, source_target_pairs={{0,1},{1,0},{2,3},{3,2},{4,5},{5,4},{6,7},{7,6},{8,9},{9,8},{10,11... | collective-permute-start | bytes 786440 | tf_op jit(solution)/shard_map/ppermute | solution.py:991
  15.2 7.7 %collective-permute-start.3 = (f32[64,1024]{1,0:T(8,128)S(1)}, f32[64,1024]{1,0:T(8,128)S(1)}, u32[]{:S(2)}, u32[]{:S(2)}) collective-permute-start(f32[64,1024]{1,0:T(8,128)S(1)} %get-tuple-element.71.refs_5_), channel_id=1, source_target_pairs={{1,2},{2,1},{5,6},{6,5},{9,10},{10,9},{13,14},{14,13},{17,18},{18,... | collective-permute-start | bytes 786440 | tf_op jit(solution)/shard_map/ppermute | solution.py:992
  20.4 9.5 %copy-start.3 = (f32[32,8,1024]{2,1,0:T(8,128)S(1)}, f32[32,8,1024]{2,1,0:T(8,128)}, u32[]{:S(2)}) copy-start(f32[32,8,1024]{2,1,0:T(8,128)} %refs_4_.1) | copy-start | bytes 3145732
  20.4 8.9 %collective-permute-start.4 = (f32[104,640]{1,0:T(8,128)S(1)}, f32[104,640]{1,0:T(8,128)S(1)}, u32[]{:S(2)}, u32[]{:S(2)}) collective-permute-start(f32[104,640]{1,0:T(8,128)S(1)} %get-tuple-element.77), channel_id=1, source_target_pairs={{0,16},{16,0},{1,17},{17,1},{2,18},{18,2},{3,19},{19,3},{4,20},{20... | collective-permute-start | bytes 798728 | tf_op jit(solution)/shard_map/ppermute | solution.py:1108
  23.6 8.9 %collective-permute-start.5 = (f32[96,384]{1,0:T(8,128)S(1)}, f32[96,384]{1,0:T(8,128)S(1)}, u32[]{:S(2)}, u32[]{:S(2)}) collective-permute-start(f32[96,384]{1,0:T(8,128)S(1)} %get-tuple-element.81), channel_id=1, source_target_pairs={{0,16},{16,0},{1,17},{17,1},{2,18},{18,2},{3,19},{19,3},{4,20},{20... | collective-permute-start | bytes 442376 | tf_op jit(solution)/shard_map/ppermute | solution.py:1121
  30.9 4.5 %collective-permute-start.6 = (f32[5,8,512]{2,1,0:T(8,128)S(1)}, f32[5,8,512]{2,1,0:T(8,128)S(1)}, u32[]{:S(2)}, u32[]{:S(2)}) collective-permute-start(f32[5,8,512]{2,1,0:T(8,128)S(1)} %get-tuple-element.94.refs_0_), channel_id=1, source_target_pairs={{0,4},{4,0},{8,12},{12,8},{1,5},{5,1},{9,13},{13,9},{2,6},{6,2},{1... | collective-permute-start | bytes 245768 | tf_op jit(solution)/shard_map/ppermute | solution.py:1145
  32.8 10.7 %copy-start.5 = (s32[8,1024]{1,0:T(8,128)S(1)}, s32[8,1024]{1,0:T(8,128)}, u32[]{:S(2)}) copy-start(s32[8,1024]{1,0:T(8,128)} %refs_16_.1) | copy-start | bytes 98308
  33.8 4.9 %collective-permute-start.8 = (f32[5,8,512]{2,1,0:T(8,128)S(1)}, f32[5,8,512]{2,1,0:T(8,128)S(1)}, u32[]{:S(2)}, u32[]{:S(2)}) collective-permute-start(f32[5,8,512]{2,1,0:T(8,128)S(1)} %get-tuple-element.98.refs_2_.refs_0_), channel_id=1, source_target_pairs={{0,4},{4,0},{8,12},{12,8},{1,5},{5,1},{9,13},{13,9},{2,6},{6,2},{1... | collective-permute-start | bytes 245768 | tf_op jit(solution)/shard_map/ppermute | solution.py:1156
  35.4 5.6 %collective-permute-start.7 = (f32[2,8,512]{2,1,0:T(8,128)S(1)}, f32[2,8,512]{2,1,0:T(8,128)S(1)}, u32[]{:S(2)}, u32[]{:S(2)}) collective-permute-start(f32[2,8,512]{2,1,0:T(8,128)S(1)} %get-tuple-element.99.refs_0_), channel_id=1, source_target_pairs={{0,8},{8,0},{4,12},{12,4},{1,9},{9,1},{5,13},{13,5},{2,10},{10,2},... | collective-permute-start | bytes 98312 | tf_op jit(solution)/shard_map/ppermute | solution.py:1172
  38.7 4.9 %collective-permute-start.9 = (f32[2,8,512]{2,1,0:T(8,128)S(1)}, f32[2,8,512]{2,1,0:T(8,128)S(1)}, u32[]{:S(2)}, u32[]{:S(2)}) collective-permute-start(f32[2,8,512]{2,1,0:T(8,128)S(1)} %get-tuple-element.101.refs_3_), channel_id=1, source_target_pairs={{0,8},{8,0},{4,12},{12,4},{1,9},{9,1},{5,13},{13,5},{2,10},{10,2},... | collective-permute-start | bytes 98312 | tf_op jit(solution)/shard_map/ppermute | solution.py:1172
  44.1 5.7 %collective-permute-start.10 = (f32[32,1024]{1,0:T(8,128)S(1)}, f32[32,1024]{1,0:T(8,128)S(1)}, u32[]{:S(2)}, u32[]{:S(2)}) collective-permute-start(f32[32,1024]{1,0:T(8,128)S(1)} %get-tuple-element.112), channel_id=1, source_target_pairs={{0,1},{1,0},{2,3},{3,2},{4,5},{5,4},{6,7},{7,6},{8,9},{9,8},{10,11... | collective-permute-start | bytes 393224 | tf_op jit(solution)/shard_map/ppermute | solution.py:991
  44.1 6.3 %collective-permute-start.11 = (f32[32,1024]{1,0:T(8,128)S(1)}, f32[32,1024]{1,0:T(8,128)S(1)}, u32[]{:S(2)}, u32[]{:S(2)}) collective-permute-start(f32[32,1024]{1,0:T(8,128)S(1)} %get-tuple-element.113), channel_id=1, source_target_pairs={{1,2},{2,1},{5,6},{6,5},{9,10},{10,9},{13,14},{14,13},{17,18},{18,... | collective-permute-start | bytes 393224 | tf_op jit(solution)/shard_map/ppermute | solution.py:992
  46.1 3.7 %collective-permute-start.12 = (f32[8,128]{1,0:T(8,128)S(1)}, f32[8,128]{1,0:T(8,128)S(1)}, u32[]{:S(2)}, u32[]{:S(2)}) collective-permute-start(f32[8,128]{1,0:T(8,128)S(1)} %get-tuple-element.114), channel_id=1, source_target_pairs={{0,16},{16,0},{1,17},{17,1},{2,18},{18,2},{3,19},{19,3},{4,20},{20... | collective-permute-start | bytes 12296 | tf_op jit(solution)/shard_map/ppermute | solution.py:993
  51.5 8.6 %collective-permute-start.13 = (f32[2,8,1024]{2,1,0:T(8,128)S(1)}, f32[2,8,1024]{2,1,0:T(8,128)S(1)}, u32[]{:S(2)}, u32[]{:S(2)}) collective-permute-start(f32[2,8,1024]{2,1,0:T(8,128)S(1)} %get-tuple-element.121.refs_0_), channel_id=1, source_target_pairs={{0,4},{4,0},{8,12},{12,8},{1,5},{5,1},{9,13},{13,9},{2,6},{6,2},{1... | collective-permute-start | bytes 196616 | tf_op jit(solution)/shard_map/ppermute | solution.py:1194
  52.9 5.7 %collective-permute-start.15 = (f32[8,1024]{1,0:T(8,128)S(1)}, f32[8,1024]{1,0:T(8,128)S(1)}, u32[]{:S(2)}, u32[]{:S(2)}) collective-permute-start(f32[8,1024]{1,0:T(8,128)S(1)} %get-tuple-element.122), channel_id=1, source_target_pairs={{0,12},{12,0},{4,8},{8,4},{1,13},{13,1},{5,9},{9,5},{2,14},{14,2},... | collective-permute-start | bytes 98312 | tf_op jit(solution)/shard_map/ppermute | solution.py:1194
  55.2 4.8 %collective-permute-start.14 = (f32[8,1024]{1,0:T(8,128)S(1)}, f32[8,1024]{1,0:T(8,128)S(1)}, u32[]{:S(2)}, u32[]{:S(2)}) collective-permute-start(f32[8,1024]{1,0:T(8,128)S(1)} %get-tuple-element.122), channel_id=1, source_target_pairs={{0,8},{8,0},{4,12},{12,4},{1,9},{9,1},{5,13},{13,5},{2,10},{10,2},... | collective-permute-start | bytes 98312 | tf_op jit(solution)/shard_map/ppermute | solution.py:1194

commit v4 on v3

--- a/solution.py
+++ b/solution.py
@@ -367,31 +367,37 @@
     return tiles
 
 
-def row_sums(g, at, y, depth, items, columns, coefficients, basis, turns, left, right, emit):
+STEP = 16
+
+
+def fill_left(g, at, y, depth, items, columns, coefficients, turns, left, part):
     groups = NX // LANES
     sign = 1.0 - 2.0 * g.astype(F32)
     first_wave = g * (coefficients.shape[0] * LANES)
-    step = 16
-    for part in range(depth // step):
-        rows = pl.ds(part * step * items + y, step, stride=items)
-        shift = columns[pl.ds(at * depth + part * step, step), :]
-        values = twisted(first_wave, shift, coefficients, rows)
-        turned = [
-            times(value, (sign * math.cos(2 * math.pi * p / groups), sign * math.sin(2 * math.pi * p / groups)))
-            if p
-            else (sign * value[0], sign * value[1])
-            for p, value in enumerate(values)
-        ]
-        even, odd = eight_point(values), eight_point(turned)
-        for group in range(groups):
-            value = odd[group // 2] if group % 2 else even[group // 2]
-            if group:
-                value = times(value, (turns[0, group : group + 1], turns[1, group : group + 1]))
-            first = group * depth + part * step
-            for place_of, piece in enumerate(value):
-                for half, bits in enumerate(split(piece)):
-                    target = (2 * half + place_of) * LANES
-                    left[first : first + step, target : target + LANES] = bits
+    rows = pl.ds(part * STEP * items + y, STEP, stride=items)
+    shift = columns[pl.ds(at * depth + part * STEP, STEP), :]
+    values = twisted(first_wave, shift, coefficients, rows)
+    angles = [2 * math.pi * p / groups for p in range(len(values))]
+    turned = [
+        times(value, (sign * math.cos(angle), sign * math.sin(angle)))
+        if angle
+        else (sign * value[0], sign * value[1])
+        for angle, value in zip(angles, values)
+    ]
+    even, odd = eight_point(values), eight_point(turned)
+    for group in range(groups):
+        value = odd[group // 2] if group % 2 else even[group // 2]
+        if group:
+            value = times(value, (turns[0, group : group + 1], turns[1, group : group + 1]))
+        first = group * depth + part * STEP
+        for place_of, piece in enumerate(value):
+            for half, bits in enumerate(split(piece)):
+                target = (2 * half + place_of) * LANES
+                left[first : first + STEP, target : target + LANES] = bits
+
+
+def finish_row(at, depth, basis, left, right, emit):
+    groups = NX // LANES
     spread = jnp.concatenate([left[...], left[:, : 2 * LANES]], axis=1)
     bases = basis[...].reshape(-1, LANES)
     right[...] = jnp.dot(spread, bases, preferred_element_type=F32)
@@ -403,19 +409,40 @@
         emit(pl.ds(at * depth + part * ROWS, ROWS), interleave(tiles))
 
 
-def load_coefficients(spectral, coefficients, arrivals):
-    parts = coefficients.shape[0]
-    copies = [
-        pltpu.make_async_copy(
-            spectral.at[:, :, part * LANES : (part + 1) * LANES],
-            coefficients.at[part],
-            arrivals.at[part],
-        )
-        for part in range(parts)
-    ]
-    for copy in copies:
-        copy.start()
+def load_coefficients(spectral, coefficients, arrivals, items):
+    parts, halves = arrivals.shape
+    copies = []
+    for half in range(halves):
+        rows = slice(half * STEP * items, (half + 1) * STEP * items)
+        copies.append(
+            [
+                pltpu.make_async_copy(
+                    spectral.at[:, rows, part * LANES : (part + 1) * LANES],
+                    coefficients.at[part, :, rows],
+                    arrivals.at[part, half],
+                )
+                for part in range(parts)
+            ]
+        )
+    for half in copies:
+        for copy in half:
+            copy.start()
     return copies
+
+
+def all_rows(g, ys, shifts, shift_copy, copies, columns, coefficients, tables, left, right, emit):
+    items, depth = shifts.shape
+    basis, turns = tables
+    fill_tables(basis, turns)
+    shift_copy.wait()
+    shift_columns(shifts, ys, columns)
+    for half, arriving in enumerate(copies):
+        for copy in arriving:
+            copy.wait()
+        for at, y in enumerate(ys):
+            fill_left(g, at, y, depth, items, columns, coefficients, turns, left.at[at], half)
+    for at in range(len(ys)):
+        finish_row(at, depth, basis, left.at[at], right.at[at], emit)
 
 
 def keep_edges(rows, tiles, edges):
@@ -440,13 +467,11 @@
 
 
 def wide_sums_kernel(ys, shifts, spectral, other, own, kept, *refs):
-    columns, edges, coefficients, arrivals, *tables, left, right = refs
+    local, arrived, columns, edges, coefficients, arrivals, *tables, left, right = refs
     items, depth = shifts.shape
-    copies = load_coefficients(spectral, coefficients, arrivals)
-    fill_tables(*tables)
-    shift_columns(shifts, ys, columns)
-    for copy in copies:
-        copy.wait()
+    copies = load_coefficients(spectral, coefficients, arrivals, items)
+    shift_copy = pltpu.make_async_copy(shifts, local, arrived)
+    shift_copy.start()
     g = lax.axis_index("gx")
 
     def emit(rows, tiles):
@@ -457,22 +482,19 @@
             other[rows, there] = jnp.where(g == 0, high, low)
             own[rows, there] = jnp.where(g == 0, low, high)
 
-    for at, y in enumerate(ys):
-        row_sums(
-            *(g, at, y, depth, items, columns, coefficients, *tables),
-            *(left.at[at % 2], right.at[at % 2], emit),
-        )
+    all_rows(
+        *(g, ys, local, shift_copy, copies, columns, coefficients, tables, left, right, emit)
+    )
     edge_columns(ys, depth, edges, kept)
 
 
-def last_sums_kernel(ys, shifts, outer_kept, inner_kept, p_column, spectral, one, two, own, *refs):
-    columns_own, kept, columns, edges, coefficients, arrivals, *tables, left, right = refs
+def last_sums_kernel(ys, outer_kept, inner_kept, p_column, shifts, spectral, one, two, own, *refs):
+    columns_own, kept, local, arrived, columns, edges, coefficients, *refs = refs
+    arrivals, *tables, left, right = refs
     items, depth = shifts.shape
-    copies = load_coefficients(spectral, coefficients, arrivals)
-    fill_tables(*tables)
-    shift_columns(shifts, ys, columns)
-    for copy in copies:
-        copy.wait()
+    copies = load_coefficients(spectral, coefficients, arrivals, items)
+    shift_copy = pltpu.make_async_copy(shifts, local, arrived)
+    shift_copy.start()
     g = lax.axis_index("gx")
 
     def emit(rows, tiles):
@@ -491,11 +513,9 @@
                 )
             start += count
 
-    for at, y in enumerate(ys):
-        row_sums(
-            *(g, at, y, depth, items, columns, coefficients, *tables),
-            *(left.at[at % 2], right.at[at % 2], emit),
-        )
+    all_rows(
+        *(g, ys, local, shift_copy, copies, columns, coefficients, tables, left, right, emit)
+    )
     edge_columns(ys, depth, edges, kept)
     sides_of = [
         jnp.concatenate(
@@ -1043,14 +1063,16 @@
 
     def scratch(count):
         return [
+            pltpu.VMEM((items, depth), jnp.int32),
+            pltpu.SemaphoreType.DMA,
             pltpu.VMEM((count, LANES), jnp.int32),
             pltpu.VMEM((6, count, LANES), F32),
             pltpu.VMEM((parts, 2, rows, LANES), F32),
-            pltpu.SemaphoreType.DMA((parts,)),
+            pltpu.SemaphoreType.DMA((parts, depth // STEP)),
             pltpu.VMEM((3, 2 * LANES, LANES), jnp.bfloat16),
             pltpu.VMEM((2, groups, LANES), F32),
-            pltpu.VMEM((2, groups * depth, 4 * LANES), jnp.bfloat16),
-            pltpu.VMEM((2, groups * depth, LANES), F32),
+            pltpu.VMEM((count // depth, groups * depth, 4 * LANES), jnp.bfloat16),
+            pltpu.VMEM((count // depth, groups * depth, LANES), F32),
         ]
 
     def wide_types(ys):
@@ -1062,9 +1084,9 @@
         functools.partial(wide_sums_kernel, outer_ys),
         "outer_row_sums",
         wide_types(outer_ys),
-        [shift_rows],
+        [],
         scratch=scratch(2 * depth),
-        far=[coefficients],
+        far=[shift_rows, coefficients],
         mib=SUMS_GRANT,
     )
     outer = lax.ppermute(sums, "gx", PAIR)
@@ -1073,24 +1095,15 @@
         functools.partial(inner_sums_kernel, inner_ys),
         "inner_row_sums",
         wide_types(inner_ys) + [column_type],
-        [shift_rows],
+        [],
         scratch=[pltpu.VMEM((depth, ROWS, LANES), F32), pltpu.SemaphoreType.DMA]
         + scratch(len(inner_ys) * depth),
-        far=[coefficients, pressure],
+        far=[shift_rows, coefficients, pressure],
         mib=20,
     )
     inner = lax.ppermute(sums, "gx", PAIR)
     edge_row, edge_column = shaped(depth, width), shaped(ROWS, LANES)
     edges = [edge_row, edge_row, edge_column]
-    pressure_rows, _ = lax.optimization_barrier((pressure, own_inner))
-    to_near, to_middle = call(
-        functools.partial(outer_field_kernel, depth),
-        "outer_field",
-        [shaped(2 * depth, width)] * 2,
-        [own_outer, outer, pressure_rows],
-        flags,
-    )
-    from_near, from_middle = exchange_edges([to_near, to_middle])
     last_one, last_two, own_last, own_columns = call(
         functools.partial(last_sums_kernel, last_ys),
         "last_row_sums",
@@ -1100,11 +1113,20 @@
             shaped(last_rows, width),
             shaped(6, ROWS, LANES),
         ],
-        [shift_rows, outer_kept, inner_kept, p_column],
+        [outer_kept, inner_kept, p_column],
         scratch=[pltpu.VMEM((6, len(last_ys), LANES), F32)] + scratch(last_rows),
-        far=[coefficients],
+        far=[shift_rows, coefficients],
         mib=20,
     )
+    pressure_rows, _ = lax.optimization_barrier((pressure, own_last))
+    to_near, to_middle = call(
+        functools.partial(outer_field_kernel, depth),
+        "outer_field",
+        [shaped(2 * depth, width)] * 2,
+        [own_outer, outer, pressure_rows],
+        flags,
+    )
+    from_near, from_middle = exchange_edges([to_near, to_middle])
     last_one = lax.ppermute(last_one, "gx", PAIR)
     wide, *around = call(
         functools.partial(wide_field_kernel, depth),

time: 61.3 us -> 60.4 us (0.985)
  the two profiles are of different devices: /device:TPU:6 before, /device:TPU:0 now
where the time goes in v4:
time: 60.4 us; the launch traced here: 60.2 us
  starting transfers between devices  22.7 us (38%)
  waiting for transfers between devices  18.3 us (30%)
  Pallas kernels  17.2 us (28%)
  local copies, waits for them, and re-layouts  1.25 us (2%)
  between operations  0.79 us (1%)
    pallas_call x15, Pallas kernels, call(): pl.pallas_call(body, out_shape=out_shape, in_specs=specs, out_specs=jax.t...  17.2 us
    ppermute x2, starting transfers between devices, join(): return (across, lax.ppermute(across, 'gz', SKIP), kept)  5.86 us
    ppermute x1, waiting for transfers between devices, fast_body(): inner = lax.ppermute(sums, 'gx', PAIR)  5.02 us
    ppermute x3, waiting for transfers between devices, fast_body(): lax.ppermute(planes, 'gz', pairs)  4.59 us
    ppermute x3, starting transfers between devices, fast_body(): lax.ppermute(planes, 'gz', pairs)  3.76 us
    ppermute x1, waiting for transfers between devices, fast_body(): last_one = lax.ppermute(last_one, 'gx', PAIR)  3.21 us
    ppermute x1, starting transfers between devices, fast_body(): outer = lax.ppermute(sums, 'gx', PAIR)  3.03 us
    ppermute x2, waiting for transfers between devices, join(): return (across, lax.ppermute(across, 'gz', SKIP), kept)  2.58 us
  transfers between devices with their start and end apart: 16, of which 8 were waited for; matrix products, arithmetic and copies ran while one was open for 0% of the time, Pallas kernels for 17%

profile of v4, /device:TPU:0, one launch (start us, length us, event | category | flops | bytes accessed | tf_op | source)
XLA Modules:
  0.0 60.2 jit_solution(15329929030770872915)
XLA Ops:
  0.6 4.1 %outer_row_sums.1 = (f32[64,1024]{1,0:T(8,128)}, f32[64,1024]{1,0:T(8,128)}, f32[6,2,128]{2,1,0:T(2,128)}) custom-call(s32[8,32]{1,0:T(8,128)} %bitcast.5, f32[2,256,1024]{2,1,0:T(8,128)} %bitcast.2), custom_call_target="tpu_custom_call" | custom-call | flops 1 | bytes 1 | tf_op jit(solution)/shard_map/outer_row_sums/pallas_call | solution.py:548
  4.8 3.0 %collective-permute-start = (f32[64,1024]{1,0:T(8,128)}, f32[64,1024]{1,0:T(8,128)S(1)}, u32[]{:S(2)}, u32[]{:S(2)}) collective-permute-start(f32[64,1024]{1,0:T(8,128)} %get-tuple-element.65), channel_id=1, source_target_pairs={{0,16},{16,0},{1,17},{17,1},{2,18},{18,2},{3,19},{19,3},{4,20},{20... | collective-permute-start | bytes 786440 | tf_op jit(solution)/shard_map/ppermute | solution.py:1092
  7.8 1.2 %copy-done.1 = f32[32,8,1024]{2,1,0:T(8,128)S(1)} copy-done((f32[32,8,1024]{2,1,0:T(8,128)S(1)}, f32[32,8,1024]{2,1,0:T(8,128)}, u32[]{:S(2)}) %copy-start.1) | copy-done | bytes 1048600
  9.0 2.9 %inner_row_sums.1 = (f32[96,1024]{1,0:T(8,128)S(1)}, f32[96,1024]{1,0:T(8,128)S(1)}, f32[6,3,128]{2,1,0:T(4,128)S(1)}, f32[8,128]{1,0:T(8,128)S(1)}) custom-call(s32[8,32]{1,0:T(8,128)S(1)} %bitcast.6, f32[2,256,1024]{2,1,0:T(8,128)S(1)} %bitcast.3, f32[32,8,1024]{2,1,0:T(8,128)S(1)} %copy-done.1), custom_call_target="tpu_custom_call" | custom-call | flops 1 | bytes 1 | tf_op jit(solution)/shard_map/inner_row_sums/pallas_call | solution.py:548
  12.0 2.7 %last_row_sums.1 = (f32[104,640]{1,0:T(8,128)S(1)}, f32[96,384]{1,0:T(8,128)S(1)}, f32[96,1024]{1,0:T(8,128)S(1)}, f32[6,8,128]{2,1,0:T(8,128)S(1)}) custom-call(f32[6,2,128]{2,1,0:T(2,128)S(1)} %copy-done.7, f32[6,3,128]{2,1,0:T(4,128)S(1)} %get-tuple-element.70.inner_kept, f32[8,128]{1,0:T(8,128)S(1)} %get-tuple-element.71.p_column, s32[8,32]{1,0:T(8,128)S(1)} %bitcast.7, ...), custom_call_target="tpu_custom_call" | custom-call | flops 1 | bytes 1 | tf_op jit(solution)/shard_map/last_row_sums/pallas_call | solution.py:548
  15.2 0.7 %collective-permute-start.3 = (f32[64,1024]{1,0:T(8,128)S(1)}, f32[64,1024]{1,0:T(8,128)S(1)}, u32[]{:S(2)}, u32[]{:S(2)}) collective-permute-start(f32[64,1024]{1,0:T(8,128)S(1)} %get-tuple-element.75.refs_5_), channel_id=1, source_target_pairs={{1,2},{2,1},{5,6},{6,5},{9,10},{10,9},{13,14},{14,13},{17,18},{18,... | collective-permute-start | bytes 786440 | tf_op jit(solution)/shard_map/ppermute | solution.py:1012
  15.9 2.4 %collective-permute-start.4 = (f32[104,640]{1,0:T(8,128)S(1)}, f32[104,640]{1,0:T(8,128)S(1)}, u32[]{:S(2)}, u32[]{:S(2)}) collective-permute-start(f32[104,640]{1,0:T(8,128)S(1)} %get-tuple-element.77), channel_id=1, source_target_pairs={{0,16},{16,0},{1,17},{17,1},{2,18},{18,2},{3,19},{19,3},{4,20},{20... | collective-permute-start | bytes 798728 | tf_op jit(solution)/shard_map/ppermute | solution.py:1130
  18.3 5.0 %collective-permute-done.1.refs_3_ = f32[96,1024]{1,0:T(8,128)S(1)} collective-permute-done((f32[96,1024]{1,0:T(8,128)S(1)}, f32[96,1024]{1,0:T(8,128)S(1)}, u32[]{:S(2)}, u32[]{:S(2)}) %collective-permute-start.1) | collective-permute-done | bytes 393248 | tf_op jit(solution)/shard_map/ppermute | solution.py:1104
  23.4 0.7 %wide_field.1 = (f32[160,1024]{1,0:T(8,128)S(1)}, f32[32,1024]{1,0:T(8,128)S(1)}, f32[32,1024]{1,0:T(8,128)S(1)}, f32[32,8,1024]{2,1,0:T(8,128)S(1)}, f32[32,8,1...) custom-call(f32[64,1024]{1,0:T(8,128)S(1)} %copy-done.4, ...), custom_call_target="tpu_custom_call" | custom-call | flops 1 | bytes 1 | tf_op jit(solution)/shard_map/wide_field/pallas_call | solution.py:548
  24.1 1.8 %collective-permute-start.5 = (f32[96,384]{1,0:T(8,128)S(1)}, f32[96,384]{1,0:T(8,128)S(1)}, u32[]{:S(2)}, u32[]{:S(2)}) collective-permute-start(f32[96,384]{1,0:T(8,128)S(1)} %get-tuple-element.81), channel_id=1, source_target_pairs={{0,16},{16,0},{1,17},{17,1},{2,18},{18,2},{3,19},{19,3},{4,20},{20... | collective-permute-start | bytes 442376 | tf_op jit(solution)/shard_map/ppermute | solution.py:1143
  25.9 3.2 %collective-permute-done.4.refs_2_ = f32[104,640]{1,0:T(8,128)S(1)} collective-permute-done((f32[104,640]{1,0:T(8,128)S(1)}, f32[104,640]{1,0:T(8,128)S(1)}, u32[]{:S(2)}, u32[]{:S(2)}) %collective-permute-start.4) | collective-permute-done | bytes 266272 | tf_op jit(solution)/shard_map/ppermute | solution.py:1130
  29.1 0.5 first_field.1
  29.6 0.9 %first_sweep.2 = (f32[32,8,512]{2,1,0:T(8,128)S(1)}, f32[32,8,512]{2,1,0:T(8,128)S(1)}, f32[8,128]{1,0:T(8,128)S(1)}, f32[32,8,512]{2,1,0:T(8,128)S(1)}, f32[32,...) custom-call(f32[32,8,640]{2,1,0:T(8,128)S(1)} %get-tuple-element.82.refs_0, ...), custom_call_target="tpu_custom_call" | custom-call | flops 1 | bytes 1 | tf_op jit(solution)/shard_map/first_sweep/pallas_call | solution.py:548
  30.6 2.1 %collective-permute-start.6 = (f32[5,8,512]{2,1,0:T(8,128)S(1)}, f32[5,8,512]{2,1,0:T(8,128)S(1)}, u32[]{:S(2)}, u32[]{:S(2)}) collective-permute-start(f32[5,8,512]{2,1,0:T(8,128)S(1)} %get-tuple-element.94.refs_0_), channel_id=1, source_target_pairs={{0,4},{4,0},{8,12},{12,8},{1,5},{5,1},{9,13},{13,9},{2,6},{6,2},{1... | collective-permute-start | bytes 245768 | tf_op jit(solution)/shard_map/ppermute | solution.py:1167
  32.7 0.3 second_field.1
  33.0 0.9 %first_sweep.3 = (f32[32,8,512]{2,1,0:T(8,128)S(1)}, f32[32,8,512]{2,1,0:T(8,128)S(1)}, f32[8,128]{1,0:T(8,128)S(1)}, f32[32,8,512]{2,1,0:T(8,128)S(1)}, f32[32,...) custom-call(f32[32,8,512]{2,1,0:T(8,128)S(1)} %get-tuple-element.97.refs_0, ...), custom_call_target="tpu_custom_call" | custom-call | flops 1 | bytes 1 | tf_op jit(solution)/shard_map/first_sweep/pallas_call | solution.py:548
  33.9 0.8 %collective-permute-start.8 = (f32[5,8,512]{2,1,0:T(8,128)S(1)}, f32[5,8,512]{2,1,0:T(8,128)S(1)}, u32[]{:S(2)}, u32[]{:S(2)}) collective-permute-start(f32[5,8,512]{2,1,0:T(8,128)S(1)} %get-tuple-element.98.refs_2_.refs_0_), channel_id=1, source_target_pairs={{0,4},{4,0},{8,12},{12,8},{1,5},{5,1},{9,13},{13,9},{2,6},{6,2},{1... | collective-permute-start | bytes 245768 | tf_op jit(solution)/shard_map/ppermute | solution.py:1178
  34.7 0.5 collective-permute-done.6.refs_1_
  35.2 3.6 %collective-permute-start.7 = (f32[2,8,512]{2,1,0:T(8,128)S(1)}, f32[2,8,512]{2,1,0:T(8,128)S(1)}, u32[]{:S(2)}, u32[]{:S(2)}) collective-permute-start(f32[2,8,512]{2,1,0:T(8,128)S(1)} %get-tuple-element.99.refs_0_), channel_id=1, source_target_pairs={{0,8},{8,0},{4,12},{12,4},{1,9},{9,1},{5,13},{13,5},{2,10},{10,2},... | collective-permute-start | bytes 98312 | tf_op jit(solution)/shard_map/ppermute | solution.py:1194
  38.8 2.3 %collective-permute-start.9 = (f32[2,8,512]{2,1,0:T(8,128)S(1)}, f32[2,8,512]{2,1,0:T(8,128)S(1)}, u32[]{:S(2)}, u32[]{:S(2)}) collective-permute-start(f32[2,8,512]{2,1,0:T(8,128)S(1)} %get-tuple-element.101.refs_3_), channel_id=1, source_target_pairs={{0,8},{8,0},{4,12},{12,4},{1,9},{9,1},{5,13},{13,5},{2,10},{10,2},... | collective-permute-start | bytes 98312 | tf_op jit(solution)/shard_map/ppermute | solution.py:1194
  41.1 2.6 %collective-permute-done.9.refs_4_ = f32[2,8,512]{2,1,0:T(8,128)S(1)} collective-permute-done((f32[2,8,512]{2,1,0:T(8,128)S(1)}, f32[2,8,512]{2,1,0:T(8,128)S(1)}, u32[]{:S(2)}, u32[]{:S(2)}) %collective-permute-start.9) | collective-permute-done | bytes 32800 | tf_op jit(solution)/shard_map/ppermute | solution.py:1194
  43.7 0.5 half.1
  44.3 0.7 %collective-permute-start.11 = (f32[32,1024]{1,0:T(8,128)S(1)}, f32[32,1024]{1,0:T(8,128)S(1)}, u32[]{:S(2)}, u32[]{:S(2)}) collective-permute-start(f32[32,1024]{1,0:T(8,128)S(1)} %get-tuple-element.113), channel_id=1, source_target_pairs={{1,2},{2,1},{5,6},{6,5},{9,10},{10,9},{13,14},{14,13},{17,18},{18,... | collective-permute-start | bytes 393224 | tf_op jit(solution)/shard_map/ppermute | solution.py:1012
  45.0 1.3 %collective-permute-start.12 = (f32[8,128]{1,0:T(8,128)S(1)}, f32[8,128]{1,0:T(8,128)S(1)}, u32[]{:S(2)}, u32[]{:S(2)}) collective-permute-start(f32[8,128]{1,0:T(8,128)S(1)} %get-tuple-element.114), channel_id=1, source_target_pairs={{0,16},{16,0},{1,17},{17,1},{2,18},{18,2},{3,19},{19,3},{4,20},{20... | collective-permute-start | bytes 12296 | tf_op jit(solution)/shard_map/ppermute | solution.py:1013
  46.3 2.3 %collective-permute-done.12.refs_3_ = f32[8,128]{1,0:T(8,128)S(1)} collective-permute-done((f32[8,128]{1,0:T(8,128)S(1)}, f32[8,128]{1,0:T(8,128)S(1)}, u32[]{:S(2)}, u32[]{:S(2)}) %collective-permute-start.12) | collective-permute-done | bytes 4128 | tf_op jit(solution)/shard_map/ppermute | solution.py:1013
  48.6 1.0 %second_sweep.1 = (f32[32,8,512]{2,1,0:T(8,128)S(1)}, f32[32,8,512]{2,1,0:T(8,128)S(1)}, f32[2,8,1024]{2,1,0:T(8,128)S(1)}, f32[8,1024]{1,0:T(8,128)S(1)}) custom-call(f32[32,8,1024]{2,1,0:T(8,128)S(1)} %get-tuple-element.111.refs_0_.refs_15_, f32[32,1024]{1,0:T(8,128)S(1)} %collective-permute-done.10.refs_1_, ...), custom_call_target="tpu_custom_call" | custom-call | flops 1 | bytes 1 | tf_op jit(solution)/shard_map/second_sweep/pallas_call | solution.py:548
  49.7 1.6 %collective-permute-start.13 = (f32[2,8,1024]{2,1,0:T(8,128)S(1)}, f32[2,8,1024]{2,1,0:T(8,128)S(1)}, u32[]{:S(2)}, u32[]{:S(2)}) collective-permute-start(f32[2,8,1024]{2,1,0:T(8,128)S(1)} %get-tuple-element.121.refs_0_), channel_id=1, source_target_pairs={{0,4},{4,0},{8,12},{12,8},{1,5},{5,1},{9,13},{13,9},{2,6},{6,2},{1... | collective-permute-start | bytes 196616 | tf_op jit(solution)/shard_map/ppermute | solution.py:1216
  51.3 2.1 %collective-permute-start.15 = (f32[8,1024]{1,0:T(8,128)S(1)}, f32[8,1024]{1,0:T(8,128)S(1)}, u32[]{:S(2)}, u32[]{:S(2)}) collective-permute-start(f32[8,1024]{1,0:T(8,128)S(1)} %get-tuple-element.122), channel_id=1, source_target_pairs={{0,12},{12,0},{4,8},{8,4},{1,13},{13,1},{5,9},{9,5},{2,14},{14,2},... | collective-permute-start | bytes 98312 | tf_op jit(solution)/shard_map/ppermute | solution.py:1216
  53.4 1.1 %log_perm.1 = f32[32,8,1024]{2,1,0:T(8,128)} custom-call(f32[32,8,640]{2,1,0:T(8,128)S(1)} %get-tuple-element.79.refs_0_, f32[32,8,384]{2,1,0:T(8,128)S(1)} %get-tuple-element.96.refs_1_, f32[5,8,512]{2,1,0:T(8,128)S(1)} %get-tuple-element.98.refs_2_.refs_0_), custom_call_target="tpu_custom_call" | custom-call | flops 1 | bytes 1 | tf_op jit(solution)/shard_map/log_perm/pallas_call | solution.py:548
  54.5 2.9 %collective-permute-done.15.refs_3_ = f32[8,1024]{1,0:T(8,128)S(1)} collective-permute-done((f32[8,1024]{1,0:T(8,128)S(1)}, f32[8,1024]{1,0:T(8,128)S(1)}, u32[]{:S(2)}, u32[]{:S(2)}) %collective-permute-start.15) | collective-permute-done | bytes 32800 | tf_op jit(solution)/shard_map/ppermute | solution.py:1216
  57.4 1.7 %collective-permute-done.14.refs_2_ = f32[8,1024]{1,0:T(8,128)S(1)} collective-permute-done((f32[8,1024]{1,0:T(8,128)S(1)}, f32[8,1024]{1,0:T(8,128)S(1)}, u32[]{:S(2)}, u32[]{:S(2)}) %collective-permute-start.14) | collective-permute-done | bytes 32800 | tf_op jit(solution)/shard_map/ppermute | solution.py:1216
  59.1 1.1 %smoothed.1 = f32[32,8,1024]{2,1,0:T(8,128)} custom-call(f32[2,8,1024]{2,1,0:T(8,128)S(1)} %get-tuple-element.121.refs_0_, f32[2,8,1024]{2,1,0:T(8,128)S(1)} %collective-permute-done.13.refs_1_, f32[8,1024]{1,0:T(8,128)S(1)} %collective-permute-done.14.refs_2_, f32[8,1024]{1,0:T(8,128)S(1)} %collective-permute-done.15.refs_3_, ...), custom_call_target="tpu_custom_call" | custom-call | flops 1 | bytes 1 | tf_op jit(solution)/shard_map/smoothed/pallas_call | solution.py:548
  (31 shorter events, 0.7 us)
Async XLA Ops:
  0.6 7.2 %copy-start.6 = (s32[32,8]{0,1:T(8,128)S(1)}, s32[32,8]{0,1:T(8,128)}, u32[]{:S(2)}) copy-start(s32[32,8]{0,1:T(8,128)} %param.6) | copy-start | bytes 3076
  0.6 7.2 %copy-start = (f32[2,32,8,1024]{3,2,1,0:T(8,128)S(1)}, f32[2,32,8,1024]{3,2,1,0:T(8,128)}, u32[]{:S(2)}) copy-start(f32[2,32,8,1024]{3,2,1,0:T(8,128)} %param.5) | copy-start | bytes 6291460
  4.8 10.1 %collective-permute-start = (f32[64,1024]{1,0:T(8,128)}, f32[64,1024]{1,0:T(8,128)S(1)}, u32[]{:S(2)}, u32[]{:S(2)}) collective-permute-start(f32[64,1024]{1,0:T(8,128)} %get-tuple-element.65), channel_id=1, source_target_pairs={{0,16},{16,0},{1,17},{17,1},{2,18},{18,2},{3,19},{19,3},{4,20},{20... | collective-permute-start | bytes 786440 | tf_op jit(solution)/shard_map/ppermute | solution.py:1092
  7.8 1.2 %copy-start.1 = (f32[32,8,1024]{2,1,0:T(8,128)S(1)}, f32[32,8,1024]{2,1,0:T(8,128)}, u32[]{:S(2)}) copy-start(f32[32,8,1024]{2,1,0:T(8,128)} %refs_14_.1) | copy-start | bytes 3145732
  9.0 3.0 %copy-start.7 = (f32[6,2,128]{2,1,0:T(2,128)S(1)}, f32[6,2,128]{2,1,0:T(2,128)}, u32[]{:S(2)}) copy-start(f32[6,2,128]{2,1,0:T(2,128)} %get-tuple-element.69.outer_kept) | copy-start | bytes 18436
  9.0 5.8 %copy-start.2 = (f32[32,8,1024]{2,1,0:T(8,128)S(1)}, f32[32,8,1024]{2,1,0:T(8,128)}, u32[]{:S(2)}) copy-start(f32[32,8,1024]{2,1,0:T(8,128)} %refs_14_.1) | copy-start | bytes 3145732
  9.0 5.8 %copy-start.4 = (f32[64,1024]{1,0:T(8,128)S(1)}, f32[64,1024]{1,0:T(8,128)}, u32[]{:S(2)}) copy-start(f32[64,1024]{1,0:T(8,128)} %get-tuple-element.64.refs_0_) | copy-start | bytes 786436
  11.9 11.4 %collective-permute-start.1 = (f32[96,1024]{1,0:T(8,128)S(1)}, f32[96,1024]{1,0:T(8,128)S(1)}, u32[]{:S(2)}, u32[]{:S(2)}) collective-permute-start(f32[96,1024]{1,0:T(8,128)S(1)} %get-tuple-element.68), channel_id=1, source_target_pairs={{0,16},{16,0},{1,17},{17,1},{2,18},{18,2},{3,19},{19,3},{4,20},{20... | collective-permute-start | bytes 1179656 | tf_op jit(solution)/shard_map/ppermute | solution.py:1104
  15.1 8.2 %collective-permute-start.2 = (f32[64,1024]{1,0:T(8,128)S(1)}, f32[64,1024]{1,0:T(8,128)S(1)}, u32[]{:S(2)}, u32[]{:S(2)}) collective-permute-start(f32[64,1024]{1,0:T(8,128)S(1)} %get-tuple-element.74.refs_4_), channel_id=1, source_target_pairs={{0,1},{1,0},{2,3},{3,2},{4,5},{5,4},{6,7},{7,6},{8,9},{9,8},{10,11... | collective-permute-start | bytes 786440 | tf_op jit(solution)/shard_map/ppermute | solution.py:1011
  15.2 8.2 %collective-permute-start.3 = (f32[64,1024]{1,0:T(8,128)S(1)}, f32[64,1024]{1,0:T(8,128)S(1)}, u32[]{:S(2)}, u32[]{:S(2)}) collective-permute-start(f32[64,1024]{1,0:T(8,128)S(1)} %get-tuple-element.75.refs_5_), channel_id=1, source_target_pairs={{1,2},{2,1},{5,6},{6,5},{9,10},{10,9},{13,14},{14,13},{17,18},{18,... | collective-permute-start | bytes 786440 | tf_op jit(solution)/shard_map/ppermute | solution.py:1012
  15.9 13.2 %collective-permute-start.4 = (f32[104,640]{1,0:T(8,128)S(1)}, f32[104,640]{1,0:T(8,128)S(1)}, u32[]{:S(2)}, u32[]{:S(2)}) collective-permute-start(f32[104,640]{1,0:T(8,128)S(1)} %get-tuple-element.77), channel_id=1, source_target_pairs={{0,16},{16,0},{1,17},{17,1},{2,18},{18,2},{3,19},{19,3},{4,20},{20... | collective-permute-start | bytes 798728 | tf_op jit(solution)/shard_map/ppermute | solution.py:1130
  23.4 6.2 %copy-start.3 = (f32[32,8,1024]{2,1,0:T(8,128)S(1)}, f32[32,8,1024]{2,1,0:T(8,128)}, u32[]{:S(2)}) copy-start(f32[32,8,1024]{2,1,0:T(8,128)} %refs_4_.1) | copy-start | bytes 3145732
  24.1 8.6 %collective-permute-start.5 = (f32[96,384]{1,0:T(8,128)S(1)}, f32[96,384]{1,0:T(8,128)S(1)}, u32[]{:S(2)}, u32[]{:S(2)}) collective-permute-start(f32[96,384]{1,0:T(8,128)S(1)} %get-tuple-element.81), channel_id=1, source_target_pairs={{0,16},{16,0},{1,17},{17,1},{2,18},{18,2},{3,19},{19,3},{4,20},{20... | collective-permute-start | bytes 442376 | tf_op jit(solution)/shard_map/ppermute | solution.py:1143
  30.6 4.6 %collective-permute-start.6 = (f32[5,8,512]{2,1,0:T(8,128)S(1)}, f32[5,8,512]{2,1,0:T(8,128)S(1)}, u32[]{:S(2)}, u32[]{:S(2)}) collective-permute-start(f32[5,8,512]{2,1,0:T(8,128)S(1)} %get-tuple-element.94.refs_0_), channel_id=1, source_target_pairs={{0,4},{4,0},{8,12},{12,8},{1,5},{5,1},{9,13},{13,9},{2,6},{6,2},{1... | collective-permute-start | bytes 245768 | tf_op jit(solution)/shard_map/ppermute | solution.py:1167
  33.0 10.7 %copy-start.5 = (s32[8,1024]{1,0:T(8,128)S(1)}, s32[8,1024]{1,0:T(8,128)}, u32[]{:S(2)}) copy-start(s32[8,1024]{1,0:T(8,128)} %refs_16_.1) | copy-start | bytes 98308
  33.9 4.9 %collective-permute-start.8 = (f32[5,8,512]{2,1,0:T(8,128)S(1)}, f32[5,8,512]{2,1,0:T(8,128)S(1)}, u32[]{:S(2)}, u32[]{:S(2)}) collective-permute-start(f32[5,8,512]{2,1,0:T(8,128)S(1)} %get-tuple-element.98.refs_2_.refs_0_), channel_id=1, source_target_pairs={{0,4},{4,0},{8,12},{12,8},{1,5},{5,1},{9,13},{13,9},{2,6},{6,2},{1... | collective-permute-start | bytes 245768 | tf_op jit(solution)/shard_map/ppermute | solution.py:1178
  35.2 5.9 %collective-permute-start.7 = (f32[2,8,512]{2,1,0:T(8,128)S(1)}, f32[2,8,512]{2,1,0:T(8,128)S(1)}, u32[]{:S(2)}, u32[]{:S(2)}) collective-permute-start(f32[2,8,512]{2,1,0:T(8,128)S(1)} %get-tuple-element.99.refs_0_), channel_id=1, source_target_pairs={{0,8},{8,0},{4,12},{12,4},{1,9},{9,1},{5,13},{13,5},{2,10},{10,2},... | collective-permute-start | bytes 98312 | tf_op jit(solution)/shard_map/ppermute | solution.py:1194
  38.8 4.9 %collective-permute-start.9 = (f32[2,8,512]{2,1,0:T(8,128)S(1)}, f32[2,8,512]{2,1,0:T(8,128)S(1)}, u32[]{:S(2)}, u32[]{:S(2)}) collective-permute-start(f32[2,8,512]{2,1,0:T(8,128)S(1)} %get-tuple-element.101.refs_3_), channel_id=1, source_target_pairs={{0,8},{8,0},{4,12},{12,4},{1,9},{9,1},{5,13},{13,5},{2,10},{10,2},... | collective-permute-start | bytes 98312 | tf_op jit(solution)/shard_map/ppermute | solution.py:1194
  44.2 4.4 %collective-permute-start.10 = (f32[32,1024]{1,0:T(8,128)S(1)}, f32[32,1024]{1,0:T(8,128)S(1)}, u32[]{:S(2)}, u32[]{:S(2)}) collective-permute-start(f32[32,1024]{1,0:T(8,128)S(1)} %get-tuple-element.112), channel_id=1, source_target_pairs={{0,1},{1,0},{2,3},{3,2},{4,5},{5,4},{6,7},{7,6},{8,9},{9,8},{10,11... | collective-permute-start | bytes 393224 | tf_op jit(solution)/shard_map/ppermute | solution.py:1011
  44.3 4.4 %collective-permute-start.11 = (f32[32,1024]{1,0:T(8,128)S(1)}, f32[32,1024]{1,0:T(8,128)S(1)}, u32[]{:S(2)}, u32[]{:S(2)}) collective-permute-start(f32[32,1024]{1,0:T(8,128)S(1)} %get-tuple-element.113), channel_id=1, source_target_pairs={{1,2},{2,1},{5,6},{6,5},{9,10},{10,9},{13,14},{14,13},{17,18},{18,... | collective-permute-start | bytes 393224 | tf_op jit(solution)/shard_map/ppermute | solution.py:1012
  45.0 3.7 %collective-permute-start.12 = (f32[8,128]{1,0:T(8,128)S(1)}, f32[8,128]{1,0:T(8,128)S(1)}, u32[]{:S(2)}, u32[]{:S(2)}) collective-permute-start(f32[8,128]{1,0:T(8,128)S(1)} %get-tuple-element.114), channel_id=1, source_target_pairs={{0,16},{16,0},{1,17},{17,1},{2,18},{18,2},{3,19},{19,3},{4,20},{20... | collective-permute-start | bytes 12296 | tf_op jit(solution)/shard_map/ppermute | solution.py:1013
  49.7 9.4 %collective-permute-start.13 = (f32[2,8,1024]{2,1,0:T(8,128)S(1)}, f32[2,8,1024]{2,1,0:T(8,128)S(1)}, u32[]{:S(2)}, u32[]{:S(2)}) collective-permute-start(f32[2,8,1024]{2,1,0:T(8,128)S(1)} %get-tuple-element.121.refs_0_), channel_id=1, source_target_pairs={{0,4},{4,0},{8,12},{12,8},{1,5},{5,1},{9,13},{13,9},{2,6},{6,2},{1... | collective-permute-start | bytes 196616 | tf_op jit(solution)/shard_map/ppermute | solution.py:1216
  51.3 6.1 %collective-permute-start.15 = (f32[8,1024]{1,0:T(8,128)S(1)}, f32[8,1024]{1,0:T(8,128)S(1)}, u32[]{:S(2)}, u32[]{:S(2)}) collective-permute-start(f32[8,1024]{1,0:T(8,128)S(1)} %get-tuple-element.122), channel_id=1, source_target_pairs={{0,12},{12,0},{4,8},{8,4},{1,13},{13,1},{5,9},{9,5},{2,14},{14,2},... | collective-permute-start | bytes 98312 | tf_op jit(solution)/shard_map/ppermute | solution.py:1216
  53.4 5.6 %collective-permute-start.14 = (f32[8,1024]{1,0:T(8,128)S(1)}, f32[8,1024]{1,0:T(8,128)S(1)}, u32[]{:S(2)}, u32[]{:S(2)}) collective-permute-start(f32[8,1024]{1,0:T(8,128)S(1)} %get-tuple-element.122), channel_id=1, source_target_pairs={{0,8},{8,0},{4,12},{12,4},{1,9},{9,1},{5,13},{13,5},{2,10},{10,2},... | collective-permute-start | bytes 98312 | tf_op jit(solution)/shard_map/ppermute | solution.py:1216

commit v5 on v4

--- a/solution.py
+++ b/solution.py
@@ -469,9 +469,9 @@
 def wide_sums_kernel(ys, shifts, spectral, other, own, kept, *refs):
     local, arrived, columns, edges, coefficients, arrivals, *tables, left, right = refs
     items, depth = shifts.shape
-    copies = load_coefficients(spectral, coefficients, arrivals, items)
     shift_copy = pltpu.make_async_copy(shifts, local, arrived)
     shift_copy.start()
+    copies = load_coefficients(spectral, coefficients, arrivals, items)
     g = lax.axis_index("gx")
 
     def emit(rows, tiles):
@@ -492,9 +492,9 @@
     columns_own, kept, local, arrived, columns, edges, coefficients, *refs = refs
     arrivals, *tables, left, right = refs
     items, depth = shifts.shape
-    copies = load_coefficients(spectral, coefficients, arrivals, items)
     shift_copy = pltpu.make_async_copy(shifts, local, arrived)
     shift_copy.start()
+    copies = load_coefficients(spectral, coefficients, arrivals, items)
     g = lax.axis_index("gx")
 
     def emit(rows, tiles):
@@ -1000,7 +1000,7 @@
 
 PAIR = [(0, 1), (1, 0)]
 NEAR = [(0, 1), (1, 0), (2, 3), (3, 2)]
-MIDDLE = [(1, 2), (2, 1)]
+MIDDLE = [(1, 2), (2, 1), (0, 3), (3, 0)]
 SKIP = [(0, 2), (2, 0), (1, 3), (3, 1)]
 CROSS = [(0, 3), (3, 0), (1, 2), (2, 1)]
 

time: 60.4 us -> 60 us (level)
  waiting for transfers between devices: 18.3 us -> 16.7 us
  starting transfers between devices: 22.7 us -> 24.2 us
    ppermute x2, starting transfers between devices: 1.35 us -> 3.66 us  [exchange_edges(): lax.ppermute(to_middle, 'gy', MIDDLE)]
    ppermute x3, waiting for transfers between devices: 4.59 us -> 3.76 us  [fast_body(): lax.ppermute(planes, 'gz', pairs)]
    ppermute x1, waiting for transfers between devices: 3.21 us -> 2.4 us  [fast_body(): last_one = lax.ppermute(last_one, 'gx', PAIR)]
  transfers between devices with their start and end apart: 16 -> 16, of which waited for: 8 -> 10; matrix products, arithmetic and copies ran while one was open for 0% -> 0% of each run, Pallas kernels for 17% -> 17%
where the time goes in v5:
time: 60 us; the launch traced here: 59.8 us
  starting transfers between devices  24.2 us (40%)
  Pallas kernels  16.9 us (28%)
  waiting for transfers between devices  16.7 us (28%)
  local copies, waits for them, and re-layouts  1.25 us (2%)
  between operations  0.77 us (1%)
    pallas_call x15, Pallas kernels, call(): pl.pallas_call(body, out_shape=out_shape, in_specs=specs, out_specs=jax.t...  16.9 us
    ppermute x2, starting transfers between devices, join(): return (across, lax.ppermute(across, 'gz', SKIP), kept)  5.46 us
    ppermute x1, waiting for transfers between devices, fast_body(): inner = lax.ppermute(sums, 'gx', PAIR)  4.84 us
    ppermute x3, starting transfers between devices, fast_body(): lax.ppermute(planes, 'gz', pairs)  3.8 us
    ppermute x3, waiting for transfers between devices, fast_body(): lax.ppermute(planes, 'gz', pairs)  3.76 us
    ppermute x2, starting transfers between devices, exchange_edges(): lax.ppermute(to_middle, 'gy', MIDDLE)  3.66 us
    ppermute x1, starting transfers between devices, fast_body(): outer = lax.ppermute(sums, 'gx', PAIR)  3.03 us
    ppermute x2, waiting for transfers between devices, join(): return (across, lax.ppermute(across, 'gz', SKIP), kept)  2.57 us
  transfers between devices with their start and end apart: 16, of which 10 were waited for; matrix products, arithmetic and copies ran while one was open for 0% of the time, Pallas kernels for 17%

profile of v5, /device:TPU:0, one launch (start us, length us, event | category | flops | bytes accessed | tf_op | source)
XLA Modules:
  0.0 59.8 jit_solution(9987265231921704404)
XLA Ops:
  0.6 3.9 %outer_row_sums.1 = (f32[64,1024]{1,0:T(8,128)}, f32[64,1024]{1,0:T(8,128)}, f32[6,2,128]{2,1,0:T(2,128)}) custom-call(s32[8,32]{1,0:T(8,128)} %bitcast.5, f32[2,256,1024]{2,1,0:T(8,128)} %bitcast.2), custom_call_target="tpu_custom_call" | custom-call | flops 1 | bytes 1 | tf_op jit(solution)/shard_map/outer_row_sums/pallas_call | solution.py:548
  4.5 3.0 %collective-permute-start = (f32[64,1024]{1,0:T(8,128)}, f32[64,1024]{1,0:T(8,128)S(1)}, u32[]{:S(2)}, u32[]{:S(2)}) collective-permute-start(f32[64,1024]{1,0:T(8,128)} %get-tuple-element.65), channel_id=1, source_target_pairs={{0,16},{16,0},{1,17},{17,1},{2,18},{18,2},{3,19},{19,3},{4,20},{20... | collective-permute-start | bytes 786440 | tf_op jit(solution)/shard_map/ppermute | solution.py:1092
  7.6 1.2 %copy-done.1 = f32[32,8,1024]{2,1,0:T(8,128)S(1)} copy-done((f32[32,8,1024]{2,1,0:T(8,128)S(1)}, f32[32,8,1024]{2,1,0:T(8,128)}, u32[]{:S(2)}) %copy-start.1) | copy-done | bytes 1048600
  8.8 2.9 %inner_row_sums.1 = (f32[96,1024]{1,0:T(8,128)S(1)}, f32[96,1024]{1,0:T(8,128)S(1)}, f32[6,3,128]{2,1,0:T(4,128)S(1)}, f32[8,128]{1,0:T(8,128)S(1)}) custom-call(s32[8,32]{1,0:T(8,128)S(1)} %bitcast.6, f32[2,256,1024]{2,1,0:T(8,128)S(1)} %bitcast.3, f32[32,8,1024]{2,1,0:T(8,128)S(1)} %copy-done.1), custom_call_target="tpu_custom_call" | custom-call | flops 1 | bytes 1 | tf_op jit(solution)/shard_map/inner_row_sums/pallas_call | solution.py:548
  11.8 2.7 %last_row_sums.1 = (f32[104,640]{1,0:T(8,128)S(1)}, f32[96,384]{1,0:T(8,128)S(1)}, f32[96,1024]{1,0:T(8,128)S(1)}, f32[6,8,128]{2,1,0:T(8,128)S(1)}) custom-call(f32[6,2,128]{2,1,0:T(2,128)S(1)} %copy-done.7, f32[6,3,128]{2,1,0:T(4,128)S(1)} %get-tuple-element.70.inner_kept, f32[8,128]{1,0:T(8,128)S(1)} %get-tuple-element.71.p_column, s32[8,32]{1,0:T(8,128)S(1)} %bitcast.7, ...), custom_call_target="tpu_custom_call" | custom-call | flops 1 | bytes 1 | tf_op jit(solution)/shard_map/last_row_sums/pallas_call | solution.py:548
  15.0 2.1 %collective-permute-start.3 = (f32[64,1024]{1,0:T(8,128)S(1)}, f32[64,1024]{1,0:T(8,128)S(1)}, u32[]{:S(2)}, u32[]{:S(2)}) collective-permute-start(f32[64,1024]{1,0:T(8,128)S(1)} %get-tuple-element.75.refs_5_), channel_id=1, source_target_pairs={{1,2},{2,1},{0,3},{3,0},{5,6},{6,5},{4,7},{7,4},{9,10},{10,9},{8,1... | collective-permute-start | bytes 786440 | tf_op jit(solution)/shard_map/ppermute | solution.py:1012
  17.0 1.9 %collective-permute-start.4 = (f32[104,640]{1,0:T(8,128)S(1)}, f32[104,640]{1,0:T(8,128)S(1)}, u32[]{:S(2)}, u32[]{:S(2)}) collective-permute-start(f32[104,640]{1,0:T(8,128)S(1)} %get-tuple-element.77), channel_id=1, source_target_pairs={{0,16},{16,0},{1,17},{17,1},{2,18},{18,2},{3,19},{19,3},{4,20},{20... | collective-permute-start | bytes 798728 | tf_op jit(solution)/shard_map/ppermute | solution.py:1130
  19.0 4.8 %collective-permute-done.1.refs_3_ = f32[96,1024]{1,0:T(8,128)S(1)} collective-permute-done((f32[96,1024]{1,0:T(8,128)S(1)}, f32[96,1024]{1,0:T(8,128)S(1)}, u32[]{:S(2)}, u32[]{:S(2)}) %collective-permute-start.1) | collective-permute-done | bytes 393248 | tf_op jit(solution)/shard_map/ppermute | solution.py:1104
  23.8 0.7 %wide_field.1 = (f32[160,1024]{1,0:T(8,128)S(1)}, f32[32,1024]{1,0:T(8,128)S(1)}, f32[32,1024]{1,0:T(8,128)S(1)}, f32[32,8,1024]{2,1,0:T(8,128)S(1)}, f32[32,8,1...) custom-call(f32[64,1024]{1,0:T(8,128)S(1)} %copy-done.4, ...), custom_call_target="tpu_custom_call" | custom-call | flops 1 | bytes 1 | tf_op jit(solution)/shard_map/wide_field/pallas_call | solution.py:548
  24.5 1.7 %collective-permute-start.5 = (f32[96,384]{1,0:T(8,128)S(1)}, f32[96,384]{1,0:T(8,128)S(1)}, u32[]{:S(2)}, u32[]{:S(2)}) collective-permute-start(f32[96,384]{1,0:T(8,128)S(1)} %get-tuple-element.81), channel_id=1, source_target_pairs={{0,16},{16,0},{1,17},{17,1},{2,18},{18,2},{3,19},{19,3},{4,20},{20... | collective-permute-start | bytes 442376 | tf_op jit(solution)/shard_map/ppermute | solution.py:1143
  26.2 2.4 %collective-permute-done.4.refs_2_ = f32[104,640]{1,0:T(8,128)S(1)} collective-permute-done((f32[104,640]{1,0:T(8,128)S(1)}, f32[104,640]{1,0:T(8,128)S(1)}, u32[]{:S(2)}, u32[]{:S(2)}) %collective-permute-start.4) | collective-permute-done | bytes 266272 | tf_op jit(solution)/shard_map/ppermute | solution.py:1130
  28.6 0.5 first_field.1
  29.1 0.9 %first_sweep.2 = (f32[32,8,512]{2,1,0:T(8,128)S(1)}, f32[32,8,512]{2,1,0:T(8,128)S(1)}, f32[8,128]{1,0:T(8,128)S(1)}, f32[32,8,512]{2,1,0:T(8,128)S(1)}, f32[32,...) custom-call(f32[32,8,640]{2,1,0:T(8,128)S(1)} %get-tuple-element.82.refs_0, ...), custom_call_target="tpu_custom_call" | custom-call | flops 1 | bytes 1 | tf_op jit(solution)/shard_map/first_sweep/pallas_call | solution.py:548
  30.1 2.1 %collective-permute-start.6 = (f32[5,8,512]{2,1,0:T(8,128)S(1)}, f32[5,8,512]{2,1,0:T(8,128)S(1)}, u32[]{:S(2)}, u32[]{:S(2)}) collective-permute-start(f32[5,8,512]{2,1,0:T(8,128)S(1)} %get-tuple-element.94.refs_0_), channel_id=1, source_target_pairs={{0,4},{4,0},{8,12},{12,8},{1,5},{5,1},{9,13},{13,9},{2,6},{6,2},{1... | collective-permute-start | bytes 245768 | tf_op jit(solution)/shard_map/ppermute | solution.py:1167
  32.2 0.3 second_field.1
  32.5 0.9 %first_sweep.3 = (f32[32,8,512]{2,1,0:T(8,128)S(1)}, f32[32,8,512]{2,1,0:T(8,128)S(1)}, f32[8,128]{1,0:T(8,128)S(1)}, f32[32,8,512]{2,1,0:T(8,128)S(1)}, f32[32,...) custom-call(f32[32,8,512]{2,1,0:T(8,128)S(1)} %get-tuple-element.97.refs_0, ...), custom_call_target="tpu_custom_call" | custom-call | flops 1 | bytes 1 | tf_op jit(solution)/shard_map/first_sweep/pallas_call | solution.py:548
  33.5 1.0 %collective-permute-start.8 = (f32[5,8,512]{2,1,0:T(8,128)S(1)}, f32[5,8,512]{2,1,0:T(8,128)S(1)}, u32[]{:S(2)}, u32[]{:S(2)}) collective-permute-start(f32[5,8,512]{2,1,0:T(8,128)S(1)} %get-tuple-element.98.refs_2_.refs_0_), channel_id=1, source_target_pairs={{0,4},{4,0},{8,12},{12,8},{1,5},{5,1},{9,13},{13,9},{2,6},{6,2},{1... | collective-permute-start | bytes 245768 | tf_op jit(solution)/shard_map/ppermute | solution.py:1178
  34.6 3.2 %collective-permute-start.7 = (f32[2,8,512]{2,1,0:T(8,128)S(1)}, f32[2,8,512]{2,1,0:T(8,128)S(1)}, u32[]{:S(2)}, u32[]{:S(2)}) collective-permute-start(f32[2,8,512]{2,1,0:T(8,128)S(1)} %get-tuple-element.99.refs_0_), channel_id=1, source_target_pairs={{0,8},{8,0},{4,12},{12,4},{1,9},{9,1},{5,13},{13,5},{2,10},{10,2},... | collective-permute-start | bytes 98312 | tf_op jit(solution)/shard_map/ppermute | solution.py:1194
  37.8 0.5 collective-permute-done.8.refs_1_
  38.3 2.3 %collective-permute-start.9 = (f32[2,8,512]{2,1,0:T(8,128)S(1)}, f32[2,8,512]{2,1,0:T(8,128)S(1)}, u32[]{:S(2)}, u32[]{:S(2)}) collective-permute-start(f32[2,8,512]{2,1,0:T(8,128)S(1)} %get-tuple-element.101.refs_3_), channel_id=1, source_target_pairs={{0,8},{8,0},{4,12},{12,4},{1,9},{9,1},{5,13},{13,5},{2,10},{10,2},... | collective-permute-start | bytes 98312 | tf_op jit(solution)/shard_map/ppermute | solution.py:1194
  40.7 2.6 %collective-permute-done.9.refs_4_ = f32[2,8,512]{2,1,0:T(8,128)S(1)} collective-permute-done((f32[2,8,512]{2,1,0:T(8,128)S(1)}, f32[2,8,512]{2,1,0:T(8,128)S(1)}, u32[]{:S(2)}, u32[]{:S(2)}) %collective-permute-start.9) | collective-permute-done | bytes 32800 | tf_op jit(solution)/shard_map/ppermute | solution.py:1194
  43.2 0.5 half.1
  43.8 1.6 %collective-permute-start.11 = (f32[32,1024]{1,0:T(8,128)S(1)}, f32[32,1024]{1,0:T(8,128)S(1)}, u32[]{:S(2)}, u32[]{:S(2)}) collective-permute-start(f32[32,1024]{1,0:T(8,128)S(1)} %get-tuple-element.113), channel_id=1, source_target_pairs={{1,2},{2,1},{0,3},{3,0},{5,6},{6,5},{4,7},{7,4},{9,10},{10,9},{8,1... | collective-permute-start | bytes 393224 | tf_op jit(solution)/shard_map/ppermute | solution.py:1012
  45.4 1.3 %collective-permute-start.12 = (f32[8,128]{1,0:T(8,128)S(1)}, f32[8,128]{1,0:T(8,128)S(1)}, u32[]{:S(2)}, u32[]{:S(2)}) collective-permute-start(f32[8,128]{1,0:T(8,128)S(1)} %get-tuple-element.114), channel_id=1, source_target_pairs={{0,16},{16,0},{1,17},{17,1},{2,18},{18,2},{3,19},{19,3},{4,20},{20... | collective-permute-start | bytes 12296 | tf_op jit(solution)/shard_map/ppermute | solution.py:1013
  46.7 2.3 %collective-permute-done.12.refs_3_ = f32[8,128]{1,0:T(8,128)S(1)} collective-permute-done((f32[8,128]{1,0:T(8,128)S(1)}, f32[8,128]{1,0:T(8,128)S(1)}, u32[]{:S(2)}, u32[]{:S(2)}) %collective-permute-start.12) | collective-permute-done | bytes 4128 | tf_op jit(solution)/shard_map/ppermute | solution.py:1013
  49.1 1.0 %second_sweep.1 = (f32[32,8,512]{2,1,0:T(8,128)S(1)}, f32[32,8,512]{2,1,0:T(8,128)S(1)}, f32[2,8,1024]{2,1,0:T(8,128)S(1)}, f32[8,1024]{1,0:T(8,128)S(1)}) custom-call(f32[32,8,1024]{2,1,0:T(8,128)S(1)} %get-tuple-element.111.refs_0_.refs_15_, f32[32,1024]{1,0:T(8,128)S(1)} %collective-permute-done.10.refs_1_, ...), custom_call_target="tpu_custom_call" | custom-call | flops 1 | bytes 1 | tf_op jit(solution)/shard_map/second_sweep/pallas_call | solution.py:548
  50.1 1.1 %collective-permute-start.13 = (f32[2,8,1024]{2,1,0:T(8,128)S(1)}, f32[2,8,1024]{2,1,0:T(8,128)S(1)}, u32[]{:S(2)}, u32[]{:S(2)}) collective-permute-start(f32[2,8,1024]{2,1,0:T(8,128)S(1)} %get-tuple-element.121.refs_0_), channel_id=1, source_target_pairs={{0,4},{4,0},{8,12},{12,8},{1,5},{5,1},{9,13},{13,9},{2,6},{6,2},{1... | collective-permute-start | bytes 196616 | tf_op jit(solution)/shard_map/ppermute | solution.py:1216
  51.3 2.6 %collective-permute-start.15 = (f32[8,1024]{1,0:T(8,128)S(1)}, f32[8,1024]{1,0:T(8,128)S(1)}, u32[]{:S(2)}, u32[]{:S(2)}) collective-permute-start(f32[8,1024]{1,0:T(8,128)S(1)} %get-tuple-element.122), channel_id=1, source_target_pairs={{0,12},{12,0},{4,8},{8,4},{1,13},{13,1},{5,9},{9,5},{2,14},{14,2},... | collective-permute-start | bytes 98312 | tf_op jit(solution)/shard_map/ppermute | solution.py:1216
  53.9 1.1 %log_perm.1 = f32[32,8,1024]{2,1,0:T(8,128)} custom-call(f32[32,8,640]{2,1,0:T(8,128)S(1)} %get-tuple-element.79.refs_0_, f32[32,8,384]{2,1,0:T(8,128)S(1)} %get-tuple-element.96.refs_1_, f32[5,8,512]{2,1,0:T(8,128)S(1)} %get-tuple-element.98.refs_2_.refs_0_), custom_call_target="tpu_custom_call" | custom-call | flops 1 | bytes 1 | tf_op jit(solution)/shard_map/log_perm/pallas_call | solution.py:548
  55.0 2.2 %collective-permute-done.15.refs_3_ = f32[8,1024]{1,0:T(8,128)S(1)} collective-permute-done((f32[8,1024]{1,0:T(8,128)S(1)}, f32[8,1024]{1,0:T(8,128)S(1)}, u32[]{:S(2)}, u32[]{:S(2)}) %collective-permute-start.15) | collective-permute-done | bytes 32800 | tf_op jit(solution)/shard_map/ppermute | solution.py:1216
  57.2 1.5 %collective-permute-done.14.refs_2_ = f32[8,1024]{1,0:T(8,128)S(1)} collective-permute-done((f32[8,1024]{1,0:T(8,128)S(1)}, f32[8,1024]{1,0:T(8,128)S(1)}, u32[]{:S(2)}, u32[]{:S(2)}) %collective-permute-start.14) | collective-permute-done | bytes 32800 | tf_op jit(solution)/shard_map/ppermute | solution.py:1216
  58.7 1.1 %smoothed.1 = f32[32,8,1024]{2,1,0:T(8,128)} custom-call(f32[2,8,1024]{2,1,0:T(8,128)S(1)} %get-tuple-element.121.refs_0_, f32[2,8,1024]{2,1,0:T(8,128)S(1)} %collective-permute-done.13.refs_1_, f32[8,1024]{1,0:T(8,128)S(1)} %collective-permute-done.14.refs_2_, f32[8,1024]{1,0:T(8,128)S(1)} %collective-permute-done.15.refs_3_, ...), custom_call_target="tpu_custom_call" | custom-call | flops 1 | bytes 1 | tf_op jit(solution)/shard_map/smoothed/pallas_call | solution.py:548
  (31 shorter events, 0.9 us)
Async XLA Ops:
  0.6 6.9 %copy-start.6 = (s32[32,8]{0,1:T(8,128)S(1)}, s32[32,8]{0,1:T(8,128)}, u32[]{:S(2)}) copy-start(s32[32,8]{0,1:T(8,128)} %param.6) | copy-start | bytes 3076
  0.6 6.9 %copy-start = (f32[2,32,8,1024]{3,2,1,0:T(8,128)S(1)}, f32[2,32,8,1024]{3,2,1,0:T(8,128)}, u32[]{:S(2)}) copy-start(f32[2,32,8,1024]{3,2,1,0:T(8,128)} %param.5) | copy-start | bytes 6291460
  4.5 10.1 %collective-permute-start = (f32[64,1024]{1,0:T(8,128)}, f32[64,1024]{1,0:T(8,128)S(1)}, u32[]{:S(2)}, u32[]{:S(2)}) collective-permute-start(f32[64,1024]{1,0:T(8,128)} %get-tuple-element.65), channel_id=1, source_target_pairs={{0,16},{16,0},{1,17},{17,1},{2,18},{18,2},{3,19},{19,3},{4,20},{20... | collective-permute-start | bytes 786440 | tf_op jit(solution)/shard_map/ppermute | solution.py:1092
  7.6 1.2 %copy-start.1 = (f32[32,8,1024]{2,1,0:T(8,128)S(1)}, f32[32,8,1024]{2,1,0:T(8,128)}, u32[]{:S(2)}) copy-start(f32[32,8,1024]{2,1,0:T(8,128)} %refs_14_.1) | copy-start | bytes 3145732
  8.8 3.0 %copy-start.7 = (f32[6,2,128]{2,1,0:T(2,128)S(1)}, f32[6,2,128]{2,1,0:T(2,128)}, u32[]{:S(2)}) copy-start(f32[6,2,128]{2,1,0:T(2,128)} %get-tuple-element.69.outer_kept) | copy-start | bytes 18436
  8.8 5.8 %copy-start.2 = (f32[32,8,1024]{2,1,0:T(8,128)S(1)}, f32[32,8,1024]{2,1,0:T(8,128)}, u32[]{:S(2)}) copy-start(f32[32,8,1024]{2,1,0:T(8,128)} %refs_14_.1) | copy-start | bytes 3145732
  8.8 5.8 %copy-start.4 = (f32[64,1024]{1,0:T(8,128)S(1)}, f32[64,1024]{1,0:T(8,128)}, u32[]{:S(2)}) copy-start(f32[64,1024]{1,0:T(8,128)} %get-tuple-element.64.refs_0_) | copy-start | bytes 786436
  11.7 12.1 %collective-permute-start.1 = (f32[96,1024]{1,0:T(8,128)S(1)}, f32[96,1024]{1,0:T(8,128)S(1)}, u32[]{:S(2)}, u32[]{:S(2)}) collective-permute-start(f32[96,1024]{1,0:T(8,128)S(1)} %get-tuple-element.68), channel_id=1, source_target_pairs={{0,16},{16,0},{1,17},{17,1},{2,18},{18,2},{3,19},{19,3},{4,20},{20... | collective-permute-start | bytes 1179656 | tf_op jit(solution)/shard_map/ppermute | solution.py:1104
  14.9 8.9 %collective-permute-start.2 = (f32[64,1024]{1,0:T(8,128)S(1)}, f32[64,1024]{1,0:T(8,128)S(1)}, u32[]{:S(2)}, u32[]{:S(2)}) collective-permute-start(f32[64,1024]{1,0:T(8,128)S(1)} %get-tuple-element.74.refs_4_), channel_id=1, source_target_pairs={{0,1},{1,0},{2,3},{3,2},{4,5},{5,4},{6,7},{7,6},{8,9},{9,8},{10,11... | collective-permute-start | bytes 786440 | tf_op jit(solution)/shard_map/ppermute | solution.py:1011
  15.0 8.8 %collective-permute-start.3 = (f32[64,1024]{1,0:T(8,128)S(1)}, f32[64,1024]{1,0:T(8,128)S(1)}, u32[]{:S(2)}, u32[]{:S(2)}) collective-permute-start(f32[64,1024]{1,0:T(8,128)S(1)} %get-tuple-element.75.refs_5_), channel_id=1, source_target_pairs={{1,2},{2,1},{0,3},{3,0},{5,6},{6,5},{4,7},{7,4},{9,10},{10,9},{8,1... | collective-permute-start | bytes 786440 | tf_op jit(solution)/shard_map/ppermute | solution.py:1012
  17.0 11.6 %collective-permute-start.4 = (f32[104,640]{1,0:T(8,128)S(1)}, f32[104,640]{1,0:T(8,128)S(1)}, u32[]{:S(2)}, u32[]{:S(2)}) collective-permute-start(f32[104,640]{1,0:T(8,128)S(1)} %get-tuple-element.77), channel_id=1, source_target_pairs={{0,16},{16,0},{1,17},{17,1},{2,18},{18,2},{3,19},{19,3},{4,20},{20... | collective-permute-start | bytes 798728 | tf_op jit(solution)/shard_map/ppermute | solution.py:1130
  23.8 5.3 %copy-start.3 = (f32[32,8,1024]{2,1,0:T(8,128)S(1)}, f32[32,8,1024]{2,1,0:T(8,128)}, u32[]{:S(2)}) copy-start(f32[32,8,1024]{2,1,0:T(8,128)} %refs_4_.1) | copy-start | bytes 3145732
  24.5 7.7 %collective-permute-start.5 = (f32[96,384]{1,0:T(8,128)S(1)}, f32[96,384]{1,0:T(8,128)S(1)}, u32[]{:S(2)}, u32[]{:S(2)}) collective-permute-start(f32[96,384]{1,0:T(8,128)S(1)} %get-tuple-element.81), channel_id=1, source_target_pairs={{0,16},{16,0},{1,17},{17,1},{2,18},{18,2},{3,19},{19,3},{4,20},{20... | collective-permute-start | bytes 442376 | tf_op jit(solution)/shard_map/ppermute | solution.py:1143
  30.1 4.5 %collective-permute-start.6 = (f32[5,8,512]{2,1,0:T(8,128)S(1)}, f32[5,8,512]{2,1,0:T(8,128)S(1)}, u32[]{:S(2)}, u32[]{:S(2)}) collective-permute-start(f32[5,8,512]{2,1,0:T(8,128)S(1)} %get-tuple-element.94.refs_0_), channel_id=1, source_target_pairs={{0,4},{4,0},{8,12},{12,8},{1,5},{5,1},{9,13},{13,9},{2,6},{6,2},{1... | collective-permute-start | bytes 245768 | tf_op jit(solution)/shard_map/ppermute | solution.py:1167
  32.5 10.7 %copy-start.5 = (s32[8,1024]{1,0:T(8,128)S(1)}, s32[8,1024]{1,0:T(8,128)}, u32[]{:S(2)}) copy-start(s32[8,1024]{1,0:T(8,128)} %refs_16_.1) | copy-start | bytes 98308
  33.5 4.9 %collective-permute-start.8 = (f32[5,8,512]{2,1,0:T(8,128)S(1)}, f32[5,8,512]{2,1,0:T(8,128)S(1)}, u32[]{:S(2)}, u32[]{:S(2)}) collective-permute-start(f32[5,8,512]{2,1,0:T(8,128)S(1)} %get-tuple-element.98.refs_2_.refs_0_), channel_id=1, source_target_pairs={{0,4},{4,0},{8,12},{12,8},{1,5},{5,1},{9,13},{13,9},{2,6},{6,2},{1... | collective-permute-start | bytes 245768 | tf_op jit(solution)/shard_map/ppermute | solution.py:1178
  34.6 6.0 %collective-permute-start.7 = (f32[2,8,512]{2,1,0:T(8,128)S(1)}, f32[2,8,512]{2,1,0:T(8,128)S(1)}, u32[]{:S(2)}, u32[]{:S(2)}) collective-permute-start(f32[2,8,512]{2,1,0:T(8,128)S(1)} %get-tuple-element.99.refs_0_), channel_id=1, source_target_pairs={{0,8},{8,0},{4,12},{12,4},{1,9},{9,1},{5,13},{13,5},{2,10},{10,2},... | collective-permute-start | bytes 98312 | tf_op jit(solution)/shard_map/ppermute | solution.py:1194
  38.3 4.9 %collective-permute-start.9 = (f32[2,8,512]{2,1,0:T(8,128)S(1)}, f32[2,8,512]{2,1,0:T(8,128)S(1)}, u32[]{:S(2)}, u32[]{:S(2)}) collective-permute-start(f32[2,8,512]{2,1,0:T(8,128)S(1)} %get-tuple-element.101.refs_3_), channel_id=1, source_target_pairs={{0,8},{8,0},{4,12},{12,4},{1,9},{9,1},{5,13},{13,5},{2,10},{10,2},... | collective-permute-start | bytes 98312 | tf_op jit(solution)/shard_map/ppermute | solution.py:1194
  43.8 5.3 %collective-permute-start.10 = (f32[32,1024]{1,0:T(8,128)S(1)}, f32[32,1024]{1,0:T(8,128)S(1)}, u32[]{:S(2)}, u32[]{:S(2)}) collective-permute-start(f32[32,1024]{1,0:T(8,128)S(1)} %get-tuple-element.112), channel_id=1, source_target_pairs={{0,1},{1,0},{2,3},{3,2},{4,5},{5,4},{6,7},{7,6},{8,9},{9,8},{10,11... | collective-permute-start | bytes 393224 | tf_op jit(solution)/shard_map/ppermute | solution.py:1011
  43.8 5.3 %collective-permute-start.11 = (f32[32,1024]{1,0:T(8,128)S(1)}, f32[32,1024]{1,0:T(8,128)S(1)}, u32[]{:S(2)}, u32[]{:S(2)}) collective-permute-start(f32[32,1024]{1,0:T(8,128)S(1)} %get-tuple-element.113), channel_id=1, source_target_pairs={{1,2},{2,1},{0,3},{3,0},{5,6},{6,5},{4,7},{7,4},{9,10},{10,9},{8,1... | collective-permute-start | bytes 393224 | tf_op jit(solution)/shard_map/ppermute | solution.py:1012
  45.4 3.6 %collective-permute-start.12 = (f32[8,128]{1,0:T(8,128)S(1)}, f32[8,128]{1,0:T(8,128)S(1)}, u32[]{:S(2)}, u32[]{:S(2)}) collective-permute-start(f32[8,128]{1,0:T(8,128)S(1)} %get-tuple-element.114), channel_id=1, source_target_pairs={{0,16},{16,0},{1,17},{17,1},{2,18},{18,2},{3,19},{19,3},{4,20},{20... | collective-permute-start | bytes 12296 | tf_op jit(solution)/shard_map/ppermute | solution.py:1013
  50.1 8.6 %collective-permute-start.13 = (f32[2,8,1024]{2,1,0:T(8,128)S(1)}, f32[2,8,1024]{2,1,0:T(8,128)S(1)}, u32[]{:S(2)}, u32[]{:S(2)}) collective-permute-start(f32[2,8,1024]{2,1,0:T(8,128)S(1)} %get-tuple-element.121.refs_0_), channel_id=1, source_target_pairs={{0,4},{4,0},{8,12},{12,8},{1,5},{5,1},{9,13},{13,9},{2,6},{6,2},{1... | collective-permute-start | bytes 196616 | tf_op jit(solution)/shard_map/ppermute | solution.py:1216
  51.3 5.9 %collective-permute-start.15 = (f32[8,1024]{1,0:T(8,128)S(1)}, f32[8,1024]{1,0:T(8,128)S(1)}, u32[]{:S(2)}, u32[]{:S(2)}) collective-permute-start(f32[8,1024]{1,0:T(8,128)S(1)} %get-tuple-element.122), channel_id=1, source_target_pairs={{0,12},{12,0},{4,8},{8,4},{1,13},{13,1},{5,9},{9,5},{2,14},{14,2},... | collective-permute-start | bytes 98312 | tf_op jit(solution)/shard_map/ppermute | solution.py:1216
  53.9 4.8 %collective-permute-start.14 = (f32[8,1024]{1,0:T(8,128)S(1)}, f32[8,1024]{1,0:T(8,128)S(1)}, u32[]{:S(2)}, u32[]{:S(2)}) collective-permute-start(f32[8,1024]{1,0:T(8,128)S(1)} %get-tuple-element.122), channel_id=1, source_target_pairs={{0,8},{8,0},{4,12},{12,4},{1,9},{9,1},{5,13},{13,5},{2,10},{10,2},... | collective-permute-start | bytes 98312 | tf_op jit(solution)/shard_map/ppermute | solution.py:1216

commit v6 on v5

--- a/solution.py
+++ b/solution.py
@@ -441,8 +441,8 @@
             copy.wait()
         for at, y in enumerate(ys):
             fill_left(g, at, y, depth, items, columns, coefficients, turns, left.at[at], half)
-    for at in range(len(ys)):
-        finish_row(at, depth, basis, left.at[at], right.at[at], emit)
+            if half == len(copies) - 1:
+                finish_row(at, depth, basis, left.at[at], right.at[at], emit)
 
 
 def keep_edges(rows, tiles, edges):
@@ -1227,7 +1227,7 @@
             *(half, colour),
         ],
         flags,
-        [pltpu.VMEM((depth, items, width), F32), pltpu.SemaphoreType.DMA((4,))],
+        [pltpu.VMEM((depth, items, width), F32), pltpu.SemaphoreType.DMA((8,))],
         out=IN_HBM,
     )
     return (log_perm, smoothed)

time: 60 us -> 60 us (level)
  no operation moved by 1% of the time
where the time goes in v6:
time: 60 us; the launch traced here: 59.9 us
  starting transfers between devices  24.2 us (40%)
  Pallas kernels  16.9 us (28%)
  waiting for transfers between devices  16.7 us (28%)
  local copies, waits for them, and re-layouts  1.25 us (2%)
  between operations  0.77 us (1%)
    pallas_call x15, Pallas kernels, call(): pl.pallas_call(body, out_shape=out_shape, in_specs=specs, out_specs=jax.t...  16.9 us
    ppermute x2, starting transfers between devices, join(): return (across, lax.ppermute(across, 'gz', SKIP), kept)  5.46 us
    ppermute x1, waiting for transfers between devices, fast_body(): inner = lax.ppermute(sums, 'gx', PAIR)  4.84 us
    ppermute x3, starting transfers between devices, fast_body(): lax.ppermute(planes, 'gz', pairs)  3.8 us
    ppermute x3, waiting for transfers between devices, fast_body(): lax.ppermute(planes, 'gz', pairs)  3.76 us
    ppermute x2, starting transfers between devices, exchange_edges(): lax.ppermute(to_middle, 'gy', MIDDLE)  3.66 us
    ppermute x1, starting transfers between devices, fast_body(): outer = lax.ppermute(sums, 'gx', PAIR)  3.03 us
    ppermute x2, waiting for transfers between devices, join(): return (across, lax.ppermute(across, 'gz', SKIP), kept)  2.57 us
  transfers between devices with their start and end apart: 16, of which 10 were waited for; matrix products, arithmetic and copies ran while one was open for 0% of the time, Pallas kernels for 17%

profile of v6, /device:TPU:0, one launch (start us, length us, event | category | flops | bytes accessed | tf_op | source)
XLA Modules:
  0.0 59.9 jit_solution(9192809103364881711)
XLA Ops:
  0.6 3.9 %outer_row_sums.1 = (f32[64,1024]{1,0:T(8,128)}, f32[64,1024]{1,0:T(8,128)}, f32[6,2,128]{2,1,0:T(2,128)}) custom-call(s32[8,32]{1,0:T(8,128)} %bitcast.5, f32[2,256,1024]{2,1,0:T(8,128)} %bitcast.2), custom_call_target="tpu_custom_call" | custom-call | flops 1 | bytes 1 | tf_op jit(solution)/shard_map/outer_row_sums/pallas_call | solution.py:548
  4.5 3.0 %collective-permute-start = (f32[64,1024]{1,0:T(8,128)}, f32[64,1024]{1,0:T(8,128)S(1)}, u32[]{:S(2)}, u32[]{:S(2)}) collective-permute-start(f32[64,1024]{1,0:T(8,128)} %get-tuple-element.65), channel_id=1, source_target_pairs={{0,16},{16,0},{1,17},{17,1},{2,18},{18,2},{3,19},{19,3},{4,20},{20... | collective-permute-start | bytes 786440 | tf_op jit(solution)/shard_map/ppermute | solution.py:1092
  7.6 1.2 %copy-done.1 = f32[32,8,1024]{2,1,0:T(8,128)S(1)} copy-done((f32[32,8,1024]{2,1,0:T(8,128)S(1)}, f32[32,8,1024]{2,1,0:T(8,128)}, u32[]{:S(2)}) %copy-start.1) | copy-done | bytes 1048600
  8.8 2.9 %inner_row_sums.1 = (f32[96,1024]{1,0:T(8,128)S(1)}, f32[96,1024]{1,0:T(8,128)S(1)}, f32[6,3,128]{2,1,0:T(4,128)S(1)}, f32[8,128]{1,0:T(8,128)S(1)}) custom-call(s32[8,32]{1,0:T(8,128)S(1)} %bitcast.6, f32[2,256,1024]{2,1,0:T(8,128)S(1)} %bitcast.3, f32[32,8,1024]{2,1,0:T(8,128)S(1)} %copy-done.1), custom_call_target="tpu_custom_call" | custom-call | flops 1 | bytes 1 | tf_op jit(solution)/shard_map/inner_row_sums/pallas_call | solution.py:548
  11.8 2.7 %last_row_sums.1 = (f32[104,640]{1,0:T(8,128)S(1)}, f32[96,384]{1,0:T(8,128)S(1)}, f32[96,1024]{1,0:T(8,128)S(1)}, f32[6,8,128]{2,1,0:T(8,128)S(1)}) custom-call(f32[6,2,128]{2,1,0:T(2,128)S(1)} %copy-done.7, f32[6,3,128]{2,1,0:T(4,128)S(1)} %get-tuple-element.70.inner_kept, f32[8,128]{1,0:T(8,128)S(1)} %get-tuple-element.71.p_column, s32[8,32]{1,0:T(8,128)S(1)} %bitcast.7, ...), custom_call_target="tpu_custom_call" | custom-call | flops 1 | bytes 1 | tf_op jit(solution)/shard_map/last_row_sums/pallas_call | solution.py:548
  15.0 2.1 %collective-permute-start.3 = (f32[64,1024]{1,0:T(8,128)S(1)}, f32[64,1024]{1,0:T(8,128)S(1)}, u32[]{:S(2)}, u32[]{:S(2)}) collective-permute-start(f32[64,1024]{1,0:T(8,128)S(1)} %get-tuple-element.75.refs_5_), channel_id=1, source_target_pairs={{1,2},{2,1},{0,3},{3,0},{5,6},{6,5},{4,7},{7,4},{9,10},{10,9},{8,1... | collective-permute-start | bytes 786440 | tf_op jit(solution)/shard_map/ppermute | solution.py:1012
  17.0 1.9 %collective-permute-start.4 = (f32[104,640]{1,0:T(8,128)S(1)}, f32[104,640]{1,0:T(8,128)S(1)}, u32[]{:S(2)}, u32[]{:S(2)}) collective-permute-start(f32[104,640]{1,0:T(8,128)S(1)} %get-tuple-element.77), channel_id=1, source_target_pairs={{0,16},{16,0},{1,17},{17,1},{2,18},{18,2},{3,19},{19,3},{4,20},{20... | collective-permute-start | bytes 798728 | tf_op jit(solution)/shard_map/ppermute | solution.py:1130
  19.0 4.8 %collective-permute-done.1.refs_3_ = f32[96,1024]{1,0:T(8,128)S(1)} collective-permute-done((f32[96,1024]{1,0:T(8,128)S(1)}, f32[96,1024]{1,0:T(8,128)S(1)}, u32[]{:S(2)}, u32[]{:S(2)}) %collective-permute-start.1) | collective-permute-done | bytes 393248 | tf_op jit(solution)/shard_map/ppermute | solution.py:1104
  23.8 0.7 %wide_field.1 = (f32[160,1024]{1,0:T(8,128)S(1)}, f32[32,1024]{1,0:T(8,128)S(1)}, f32[32,1024]{1,0:T(8,128)S(1)}, f32[32,8,1024]{2,1,0:T(8,128)S(1)}, f32[32,8,1...) custom-call(f32[64,1024]{1,0:T(8,128)S(1)} %copy-done.4, ...), custom_call_target="tpu_custom_call" | custom-call | flops 1 | bytes 1 | tf_op jit(solution)/shard_map/wide_field/pallas_call | solution.py:548
  24.5 1.7 %collective-permute-start.5 = (f32[96,384]{1,0:T(8,128)S(1)}, f32[96,384]{1,0:T(8,128)S(1)}, u32[]{:S(2)}, u32[]{:S(2)}) collective-permute-start(f32[96,384]{1,0:T(8,128)S(1)} %get-tuple-element.81), channel_id=1, source_target_pairs={{0,16},{16,0},{1,17},{17,1},{2,18},{18,2},{3,19},{19,3},{4,20},{20... | collective-permute-start | bytes 442376 | tf_op jit(solution)/shard_map/ppermute | solution.py:1143
  26.2 2.4 %collective-permute-done.4.refs_2_ = f32[104,640]{1,0:T(8,128)S(1)} collective-permute-done((f32[104,640]{1,0:T(8,128)S(1)}, f32[104,640]{1,0:T(8,128)S(1)}, u32[]{:S(2)}, u32[]{:S(2)}) %collective-permute-start.4) | collective-permute-done | bytes 266272 | tf_op jit(solution)/shard_map/ppermute | solution.py:1130
  28.6 0.5 first_field.1
  29.1 0.9 %first_sweep.2 = (f32[32,8,512]{2,1,0:T(8,128)S(1)}, f32[32,8,512]{2,1,0:T(8,128)S(1)}, f32[8,128]{1,0:T(8,128)S(1)}, f32[32,8,512]{2,1,0:T(8,128)S(1)}, f32[32,...) custom-call(f32[32,8,640]{2,1,0:T(8,128)S(1)} %get-tuple-element.82.refs_0, ...), custom_call_target="tpu_custom_call" | custom-call | flops 1 | bytes 1 | tf_op jit(solution)/shard_map/first_sweep/pallas_call | solution.py:548
  30.1 2.1 %collective-permute-start.6 = (f32[5,8,512]{2,1,0:T(8,128)S(1)}, f32[5,8,512]{2,1,0:T(8,128)S(1)}, u32[]{:S(2)}, u32[]{:S(2)}) collective-permute-start(f32[5,8,512]{2,1,0:T(8,128)S(1)} %get-tuple-element.94.refs_0_), channel_id=1, source_target_pairs={{0,4},{4,0},{8,12},{12,8},{1,5},{5,1},{9,13},{13,9},{2,6},{6,2},{1... | collective-permute-start | bytes 245768 | tf_op jit(solution)/shard_map/ppermute | solution.py:1167
  32.2 0.3 second_field.1
  32.5 0.9 %first_sweep.3 = (f32[32,8,512]{2,1,0:T(8,128)S(1)}, f32[32,8,512]{2,1,0:T(8,128)S(1)}, f32[8,128]{1,0:T(8,128)S(1)}, f32[32,8,512]{2,1,0:T(8,128)S(1)}, f32[32,...) custom-call(f32[32,8,512]{2,1,0:T(8,128)S(1)} %get-tuple-element.97.refs_0, ...), custom_call_target="tpu_custom_call" | custom-call | flops 1 | bytes 1 | tf_op jit(solution)/shard_map/first_sweep/pallas_call | solution.py:548
  33.5 1.0 %collective-permute-start.8 = (f32[5,8,512]{2,1,0:T(8,128)S(1)}, f32[5,8,512]{2,1,0:T(8,128)S(1)}, u32[]{:S(2)}, u32[]{:S(2)}) collective-permute-start(f32[5,8,512]{2,1,0:T(8,128)S(1)} %get-tuple-element.98.refs_2_.refs_0_), channel_id=1, source_target_pairs={{0,4},{4,0},{8,12},{12,8},{1,5},{5,1},{9,13},{13,9},{2,6},{6,2},{1... | collective-permute-start | bytes 245768 | tf_op jit(solution)/shard_map/ppermute | solution.py:1178
  34.6 3.2 %collective-permute-start.7 = (f32[2,8,512]{2,1,0:T(8,128)S(1)}, f32[2,8,512]{2,1,0:T(8,128)S(1)}, u32[]{:S(2)}, u32[]{:S(2)}) collective-permute-start(f32[2,8,512]{2,1,0:T(8,128)S(1)} %get-tuple-element.99.refs_0_), channel_id=1, source_target_pairs={{0,8},{8,0},{4,12},{12,4},{1,9},{9,1},{5,13},{13,5},{2,10},{10,2},... | collective-permute-start | bytes 98312 | tf_op jit(solution)/shard_map/ppermute | solution.py:1194
  37.8 0.5 collective-permute-done.8.refs_1_
  38.3 2.3 %collective-permute-start.9 = (f32[2,8,512]{2,1,0:T(8,128)S(1)}, f32[2,8,512]{2,1,0:T(8,128)S(1)}, u32[]{:S(2)}, u32[]{:S(2)}) collective-permute-start(f32[2,8,512]{2,1,0:T(8,128)S(1)} %get-tuple-element.101.refs_3_), channel_id=1, source_target_pairs={{0,8},{8,0},{4,12},{12,4},{1,9},{9,1},{5,13},{13,5},{2,10},{10,2},... | collective-permute-start | bytes 98312 | tf_op jit(solution)/shard_map/ppermute | solution.py:1194
  40.7 2.6 %collective-permute-done.9.refs_4_ = f32[2,8,512]{2,1,0:T(8,128)S(1)} collective-permute-done((f32[2,8,512]{2,1,0:T(8,128)S(1)}, f32[2,8,512]{2,1,0:T(8,128)S(1)}, u32[]{:S(2)}, u32[]{:S(2)}) %collective-permute-start.9) | collective-permute-done | bytes 32800 | tf_op jit(solution)/shard_map/ppermute | solution.py:1194
  43.2 0.5 half.1
  43.8 1.6 %collective-permute-start.11 = (f32[32,1024]{1,0:T(8,128)S(1)}, f32[32,1024]{1,0:T(8,128)S(1)}, u32[]{:S(2)}, u32[]{:S(2)}) collective-permute-start(f32[32,1024]{1,0:T(8,128)S(1)} %get-tuple-element.113), channel_id=1, source_target_pairs={{1,2},{2,1},{0,3},{3,0},{5,6},{6,5},{4,7},{7,4},{9,10},{10,9},{8,1... | collective-permute-start | bytes 393224 | tf_op jit(solution)/shard_map/ppermute | solution.py:1012
  45.4 1.3 %collective-permute-start.12 = (f32[8,128]{1,0:T(8,128)S(1)}, f32[8,128]{1,0:T(8,128)S(1)}, u32[]{:S(2)}, u32[]{:S(2)}) collective-permute-start(f32[8,128]{1,0:T(8,128)S(1)} %get-tuple-element.114), channel_id=1, source_target_pairs={{0,16},{16,0},{1,17},{17,1},{2,18},{18,2},{3,19},{19,3},{4,20},{20... | collective-permute-start | bytes 12296 | tf_op jit(solution)/shard_map/ppermute | solution.py:1013
  46.7 2.3 %collective-permute-done.12.refs_3_ = f32[8,128]{1,0:T(8,128)S(1)} collective-permute-done((f32[8,128]{1,0:T(8,128)S(1)}, f32[8,128]{1,0:T(8,128)S(1)}, u32[]{:S(2)}, u32[]{:S(2)}) %collective-permute-start.12) | collective-permute-done | bytes 4128 | tf_op jit(solution)/shard_map/ppermute | solution.py:1013
  49.1 1.0 %second_sweep.1 = (f32[32,8,512]{2,1,0:T(8,128)S(1)}, f32[32,8,512]{2,1,0:T(8,128)S(1)}, f32[2,8,1024]{2,1,0:T(8,128)S(1)}, f32[8,1024]{1,0:T(8,128)S(1)}) custom-call(f32[32,8,1024]{2,1,0:T(8,128)S(1)} %get-tuple-element.111.refs_0_.refs_15_, f32[32,1024]{1,0:T(8,128)S(1)} %collective-permute-done.10.refs_1_, ...), custom_call_target="tpu_custom_call" | custom-call | flops 1 | bytes 1 | tf_op jit(solution)/shard_map/second_sweep/pallas_call | solution.py:548
  50.1 1.1 %collective-permute-start.13 = (f32[2,8,1024]{2,1,0:T(8,128)S(1)}, f32[2,8,1024]{2,1,0:T(8,128)S(1)}, u32[]{:S(2)}, u32[]{:S(2)}) collective-permute-start(f32[2,8,1024]{2,1,0:T(8,128)S(1)} %get-tuple-element.121.refs_0_), channel_id=1, source_target_pairs={{0,4},{4,0},{8,12},{12,8},{1,5},{5,1},{9,13},{13,9},{2,6},{6,2},{1... | collective-permute-start | bytes 196616 | tf_op jit(solution)/shard_map/ppermute | solution.py:1216
  51.3 2.6 %collective-permute-start.15 = (f32[8,1024]{1,0:T(8,128)S(1)}, f32[8,1024]{1,0:T(8,128)S(1)}, u32[]{:S(2)}, u32[]{:S(2)}) collective-permute-start(f32[8,1024]{1,0:T(8,128)S(1)} %get-tuple-element.122), channel_id=1, source_target_pairs={{0,12},{12,0},{4,8},{8,4},{1,13},{13,1},{5,9},{9,5},{2,14},{14,2},... | collective-permute-start | bytes 98312 | tf_op jit(solution)/shard_map/ppermute | solution.py:1216
  53.9 1.1 %log_perm.1 = f32[32,8,1024]{2,1,0:T(8,128)} custom-call(f32[32,8,640]{2,1,0:T(8,128)S(1)} %get-tuple-element.79.refs_0_, f32[32,8,384]{2,1,0:T(8,128)S(1)} %get-tuple-element.96.refs_1_, f32[5,8,512]{2,1,0:T(8,128)S(1)} %get-tuple-element.98.refs_2_.refs_0_), custom_call_target="tpu_custom_call" | custom-call | flops 1 | bytes 1 | tf_op jit(solution)/shard_map/log_perm/pallas_call | solution.py:548
  55.0 2.2 %collective-permute-done.15.refs_3_ = f32[8,1024]{1,0:T(8,128)S(1)} collective-permute-done((f32[8,1024]{1,0:T(8,128)S(1)}, f32[8,1024]{1,0:T(8,128)S(1)}, u32[]{:S(2)}, u32[]{:S(2)}) %collective-permute-start.15) | collective-permute-done | bytes 32800 | tf_op jit(solution)/shard_map/ppermute | solution.py:1216
  57.2 1.5 %collective-permute-done.14.refs_2_ = f32[8,1024]{1,0:T(8,128)S(1)} collective-permute-done((f32[8,1024]{1,0:T(8,128)S(1)}, f32[8,1024]{1,0:T(8,128)S(1)}, u32[]{:S(2)}, u32[]{:S(2)}) %collective-permute-start.14) | collective-permute-done | bytes 32800 | tf_op jit(solution)/shard_map/ppermute | solution.py:1216
  58.7 1.1 %smoothed.1 = f32[32,8,1024]{2,1,0:T(8,128)} custom-call(f32[2,8,1024]{2,1,0:T(8,128)S(1)} %get-tuple-element.121.refs_0_, f32[2,8,1024]{2,1,0:T(8,128)S(1)} %collective-permute-done.13.refs_1_, f32[8,1024]{1,0:T(8,128)S(1)} %collective-permute-done.14.refs_2_, f32[8,1024]{1,0:T(8,128)S(1)} %collective-permute-done.15.refs_3_, ...), custom_call_target="tpu_custom_call" | custom-call | flops 1 | bytes 1 | tf_op jit(solution)/shard_map/smoothed/pallas_call | solution.py:548
  (31 shorter events, 0.9 us)
Async XLA Ops:
  0.6 6.9 %copy-start.6 = (s32[32,8]{0,1:T(8,128)S(1)}, s32[32,8]{0,1:T(8,128)}, u32[]{:S(2)}) copy-start(s32[32,8]{0,1:T(8,128)} %param.6) | copy-start | bytes 3076
  0.6 6.9 %copy-start = (f32[2,32,8,1024]{3,2,1,0:T(8,128)S(1)}, f32[2,32,8,1024]{3,2,1,0:T(8,128)}, u32[]{:S(2)}) copy-start(f32[2,32,8,1024]{3,2,1,0:T(8,128)} %param.5) | copy-start | bytes 6291460
  4.5 10.1 %collective-permute-start = (f32[64,1024]{1,0:T(8,128)}, f32[64,1024]{1,0:T(8,128)S(1)}, u32[]{:S(2)}, u32[]{:S(2)}) collective-permute-start(f32[64,1024]{1,0:T(8,128)} %get-tuple-element.65), channel_id=1, source_target_pairs={{0,16},{16,0},{1,17},{17,1},{2,18},{18,2},{3,19},{19,3},{4,20},{20... | collective-permute-start | bytes 786440 | tf_op jit(solution)/shard_map/ppermute | solution.py:1092
  7.6 1.2 %copy-start.1 = (f32[32,8,1024]{2,1,0:T(8,128)S(1)}, f32[32,8,1024]{2,1,0:T(8,128)}, u32[]{:S(2)}) copy-start(f32[32,8,1024]{2,1,0:T(8,128)} %refs_14_.1) | copy-start | bytes 3145732
  8.8 3.0 %copy-start.7 = (f32[6,2,128]{2,1,0:T(2,128)S(1)}, f32[6,2,128]{2,1,0:T(2,128)}, u32[]{:S(2)}) copy-start(f32[6,2,128]{2,1,0:T(2,128)} %get-tuple-element.69.outer_kept) | copy-start | bytes 18436
  8.8 5.8 %copy-start.2 = (f32[32,8,1024]{2,1,0:T(8,128)S(1)}, f32[32,8,1024]{2,1,0:T(8,128)}, u32[]{:S(2)}) copy-start(f32[32,8,1024]{2,1,0:T(8,128)} %refs_14_.1) | copy-start | bytes 3145732
  8.8 5.8 %copy-start.4 = (f32[64,1024]{1,0:T(8,128)S(1)}, f32[64,1024]{1,0:T(8,128)}, u32[]{:S(2)}) copy-start(f32[64,1024]{1,0:T(8,128)} %get-tuple-element.64.refs_0_) | copy-start | bytes 786436
  11.7 12.1 %collective-permute-start.1 = (f32[96,1024]{1,0:T(8,128)S(1)}, f32[96,1024]{1,0:T(8,128)S(1)}, u32[]{:S(2)}, u32[]{:S(2)}) collective-permute-start(f32[96,1024]{1,0:T(8,128)S(1)} %get-tuple-element.68), channel_id=1, source_target_pairs={{0,16},{16,0},{1,17},{17,1},{2,18},{18,2},{3,19},{19,3},{4,20},{20... | collective-permute-start | bytes 1179656 | tf_op jit(solution)/shard_map/ppermute | solution.py:1104
  14.9 8.9 %collective-permute-start.2 = (f32[64,1024]{1,0:T(8,128)S(1)}, f32[64,1024]{1,0:T(8,128)S(1)}, u32[]{:S(2)}, u32[]{:S(2)}) collective-permute-start(f32[64,1024]{1,0:T(8,128)S(1)} %get-tuple-element.74.refs_4_), channel_id=1, source_target_pairs={{0,1},{1,0},{2,3},{3,2},{4,5},{5,4},{6,7},{7,6},{8,9},{9,8},{10,11... | collective-permute-start | bytes 786440 | tf_op jit(solution)/shard_map/ppermute | solution.py:1011
  15.0 8.8 %collective-permute-start.3 = (f32[64,1024]{1,0:T(8,128)S(1)}, f32[64,1024]{1,0:T(8,128)S(1)}, u32[]{:S(2)}, u32[]{:S(2)}) collective-permute-start(f32[64,1024]{1,0:T(8,128)S(1)} %get-tuple-element.75.refs_5_), channel_id=1, source_target_pairs={{1,2},{2,1},{0,3},{3,0},{5,6},{6,5},{4,7},{7,4},{9,10},{10,9},{8,1... | collective-permute-start | bytes 786440 | tf_op jit(solution)/shard_map/ppermute | solution.py:1012
  17.0 11.6 %collective-permute-start.4 = (f32[104,640]{1,0:T(8,128)S(1)}, f32[104,640]{1,0:T(8,128)S(1)}, u32[]{:S(2)}, u32[]{:S(2)}) collective-permute-start(f32[104,640]{1,0:T(8,128)S(1)} %get-tuple-element.77), channel_id=1, source_target_pairs={{0,16},{16,0},{1,17},{17,1},{2,18},{18,2},{3,19},{19,3},{4,20},{20... | collective-permute-start | bytes 798728 | tf_op jit(solution)/shard_map/ppermute | solution.py:1130
  23.8 5.3 %copy-start.3 = (f32[32,8,1024]{2,1,0:T(8,128)S(1)}, f32[32,8,1024]{2,1,0:T(8,128)}, u32[]{:S(2)}) copy-start(f32[32,8,1024]{2,1,0:T(8,128)} %refs_4_.1) | copy-start | bytes 3145732
  24.5 7.7 %collective-permute-start.5 = (f32[96,384]{1,0:T(8,128)S(1)}, f32[96,384]{1,0:T(8,128)S(1)}, u32[]{:S(2)}, u32[]{:S(2)}) collective-permute-start(f32[96,384]{1,0:T(8,128)S(1)} %get-tuple-element.81), channel_id=1, source_target_pairs={{0,16},{16,0},{1,17},{17,1},{2,18},{18,2},{3,19},{19,3},{4,20},{20... | collective-permute-start | bytes 442376 | tf_op jit(solution)/shard_map/ppermute | solution.py:1143
  30.1 4.5 %collective-permute-start.6 = (f32[5,8,512]{2,1,0:T(8,128)S(1)}, f32[5,8,512]{2,1,0:T(8,128)S(1)}, u32[]{:S(2)}, u32[]{:S(2)}) collective-permute-start(f32[5,8,512]{2,1,0:T(8,128)S(1)} %get-tuple-element.94.refs_0_), channel_id=1, source_target_pairs={{0,4},{4,0},{8,12},{12,8},{1,5},{5,1},{9,13},{13,9},{2,6},{6,2},{1... | collective-permute-start | bytes 245768 | tf_op jit(solution)/shard_map/ppermute | solution.py:1167
  32.5 10.7 %copy-start.5 = (s32[8,1024]{1,0:T(8,128)S(1)}, s32[8,1024]{1,0:T(8,128)}, u32[]{:S(2)}) copy-start(s32[8,1024]{1,0:T(8,128)} %refs_16_.1) | copy-start | bytes 98308
  33.5 4.9 %collective-permute-start.8 = (f32[5,8,512]{2,1,0:T(8,128)S(1)}, f32[5,8,512]{2,1,0:T(8,128)S(1)}, u32[]{:S(2)}, u32[]{:S(2)}) collective-permute-start(f32[5,8,512]{2,1,0:T(8,128)S(1)} %get-tuple-element.98.refs_2_.refs_0_), channel_id=1, source_target_pairs={{0,4},{4,0},{8,12},{12,8},{1,5},{5,1},{9,13},{13,9},{2,6},{6,2},{1... | collective-permute-start | bytes 245768 | tf_op jit(solution)/shard_map/ppermute | solution.py:1178
  34.6 6.0 %collective-permute-start.7 = (f32[2,8,512]{2,1,0:T(8,128)S(1)}, f32[2,8,512]{2,1,0:T(8,128)S(1)}, u32[]{:S(2)}, u32[]{:S(2)}) collective-permute-start(f32[2,8,512]{2,1,0:T(8,128)S(1)} %get-tuple-element.99.refs_0_), channel_id=1, source_target_pairs={{0,8},{8,0},{4,12},{12,4},{1,9},{9,1},{5,13},{13,5},{2,10},{10,2},... | collective-permute-start | bytes 98312 | tf_op jit(solution)/shard_map/ppermute | solution.py:1194
  38.3 4.9 %collective-permute-start.9 = (f32[2,8,512]{2,1,0:T(8,128)S(1)}, f32[2,8,512]{2,1,0:T(8,128)S(1)}, u32[]{:S(2)}, u32[]{:S(2)}) collective-permute-start(f32[2,8,512]{2,1,0:T(8,128)S(1)} %get-tuple-element.101.refs_3_), channel_id=1, source_target_pairs={{0,8},{8,0},{4,12},{12,4},{1,9},{9,1},{5,13},{13,5},{2,10},{10,2},... | collective-permute-start | bytes 98312 | tf_op jit(solution)/shard_map/ppermute | solution.py:1194
  43.8 5.3 %collective-permute-start.10 = (f32[32,1024]{1,0:T(8,128)S(1)}, f32[32,1024]{1,0:T(8,128)S(1)}, u32[]{:S(2)}, u32[]{:S(2)}) collective-permute-start(f32[32,1024]{1,0:T(8,128)S(1)} %get-tuple-element.112), channel_id=1, source_target_pairs={{0,1},{1,0},{2,3},{3,2},{4,5},{5,4},{6,7},{7,6},{8,9},{9,8},{10,11... | collective-permute-start | bytes 393224 | tf_op jit(solution)/shard_map/ppermute | solution.py:1011
  43.8 5.3 %collective-permute-start.11 = (f32[32,1024]{1,0:T(8,128)S(1)}, f32[32,1024]{1,0:T(8,128)S(1)}, u32[]{:S(2)}, u32[]{:S(2)}) collective-permute-start(f32[32,1024]{1,0:T(8,128)S(1)} %get-tuple-element.113), channel_id=1, source_target_pairs={{1,2},{2,1},{0,3},{3,0},{5,6},{6,5},{4,7},{7,4},{9,10},{10,9},{8,1... | collective-permute-start | bytes 393224 | tf_op jit(solution)/shard_map/ppermute | solution.py:1012
  45.4 3.6 %collective-permute-start.12 = (f32[8,128]{1,0:T(8,128)S(1)}, f32[8,128]{1,0:T(8,128)S(1)}, u32[]{:S(2)}, u32[]{:S(2)}) collective-permute-start(f32[8,128]{1,0:T(8,128)S(1)} %get-tuple-element.114), channel_id=1, source_target_pairs={{0,16},{16,0},{1,17},{17,1},{2,18},{18,2},{3,19},{19,3},{4,20},{20... | collective-permute-start | bytes 12296 | tf_op jit(solution)/shard_map/ppermute | solution.py:1013
  50.1 8.6 %collective-permute-start.13 = (f32[2,8,1024]{2,1,0:T(8,128)S(1)}, f32[2,8,1024]{2,1,0:T(8,128)S(1)}, u32[]{:S(2)}, u32[]{:S(2)}) collective-permute-start(f32[2,8,1024]{2,1,0:T(8,128)S(1)} %get-tuple-element.121.refs_0_), channel_id=1, source_target_pairs={{0,4},{4,0},{8,12},{12,8},{1,5},{5,1},{9,13},{13,9},{2,6},{6,2},{1... | collective-permute-start | bytes 196616 | tf_op jit(solution)/shard_map/ppermute | solution.py:1216
  51.3 5.9 %collective-permute-start.15 = (f32[8,1024]{1,0:T(8,128)S(1)}, f32[8,1024]{1,0:T(8,128)S(1)}, u32[]{:S(2)}, u32[]{:S(2)}) collective-permute-start(f32[8,1024]{1,0:T(8,128)S(1)} %get-tuple-element.122), channel_id=1, source_target_pairs={{0,12},{12,0},{4,8},{8,4},{1,13},{13,1},{5,9},{9,5},{2,14},{14,2},... | collective-permute-start | bytes 98312 | tf_op jit(solution)/shard_map/ppermute | solution.py:1216
  53.9 4.8 %collective-permute-start.14 = (f32[8,1024]{1,0:T(8,128)S(1)}, f32[8,1024]{1,0:T(8,128)S(1)}, u32[]{:S(2)}, u32[]{:S(2)}) collective-permute-start(f32[8,1024]{1,0:T(8,128)S(1)} %get-tuple-element.122), channel_id=1, source_target_pairs={{0,8},{8,0},{4,12},{12,4},{1,9},{9,1},{5,13},{13,5},{2,10},{10,2},... | collective-permute-start | bytes 98312 | tf_op jit(solution)/shard_map/ppermute | solution.py:1216

commit v7 on v6

--- a/solution.py
+++ b/solution.py
@@ -424,9 +424,8 @@
                 for part in range(parts)
             ]
         )
-    for half in copies:
-        for copy in half:
-            copy.start()
+    for copy in copies[0]:
+        copy.start()
     return copies
 
 
@@ -434,6 +433,9 @@
     items, depth = shifts.shape
     basis, turns = tables
     fill_tables(basis, turns)
+    for half in copies[1:]:
+        for copy in half:
+            copy.start()
     shift_copy.wait()
     shift_columns(shifts, ys, columns)
     for half, arriving in enumerate(copies):

time: 60 us -> 60 us (level)
  no operation moved by 1% of the time
where the time goes in v7:
time: 60 us; the launch traced here: 59.8 us
  starting transfers between devices  24.2 us (40%)
  Pallas kernels  16.9 us (28%)
  waiting for transfers between devices  16.7 us (28%)
  local copies, waits for them, and re-layouts  1.25 us (2%)
  between operations  0.77 us (1%)
    pallas_call x15, Pallas kernels, call(): pl.pallas_call(body, out_shape=out_shape, in_specs=specs, out_specs=jax.t...  16.9 us
    ppermute x2, starting transfers between devices, join(): return (across, lax.ppermute(across, 'gz', SKIP), kept)  5.46 us
    ppermute x1, waiting for transfers between devices, fast_body(): inner = lax.ppermute(sums, 'gx', PAIR)  4.84 us
    ppermute x3, starting transfers between devices, fast_body(): lax.ppermute(planes, 'gz', pairs)  3.8 us
    ppermute x3, waiting for transfers between devices, fast_body(): lax.ppermute(planes, 'gz', pairs)  3.76 us
    ppermute x2, starting transfers between devices, exchange_edges(): lax.ppermute(to_middle, 'gy', MIDDLE)  3.65 us
    ppermute x1, starting transfers between devices, fast_body(): outer = lax.ppermute(sums, 'gx', PAIR)  3.03 us
    ppermute x2, waiting for transfers between devices, join(): return (across, lax.ppermute(across, 'gz', SKIP), kept)  2.57 us
  transfers between devices with their start and end apart: 16, of which 10 were waited for; matrix products, arithmetic and copies ran while one was open for 0% of the time, Pallas kernels for 17%

profile of v7, /device:TPU:0, one launch (start us, length us, event | category | flops | bytes accessed | tf_op | source)
XLA Modules:
  0.0 59.8 jit_solution(5872100669705926384)
XLA Ops:
  0.6 3.9 %outer_row_sums.1 = (f32[64,1024]{1,0:T(8,128)}, f32[64,1024]{1,0:T(8,128)}, f32[6,2,128]{2,1,0:T(2,128)}) custom-call(s32[8,32]{1,0:T(8,128)} %bitcast.5, f32[2,256,1024]{2,1,0:T(8,128)} %bitcast.2), custom_call_target="tpu_custom_call" | custom-call | flops 1 | bytes 1 | tf_op jit(solution)/shard_map/outer_row_sums/pallas_call | solution.py:550
  4.5 3.0 %collective-permute-start = (f32[64,1024]{1,0:T(8,128)}, f32[64,1024]{1,0:T(8,128)S(1)}, u32[]{:S(2)}, u32[]{:S(2)}) collective-permute-start(f32[64,1024]{1,0:T(8,128)} %get-tuple-element.65), channel_id=1, source_target_pairs={{0,16},{16,0},{1,17},{17,1},{2,18},{18,2},{3,19},{19,3},{4,20},{20... | collective-permute-start | bytes 786440 | tf_op jit(solution)/shard_map/ppermute | solution.py:1094
  7.6 1.2 %copy-done.1 = f32[32,8,1024]{2,1,0:T(8,128)S(1)} copy-done((f32[32,8,1024]{2,1,0:T(8,128)S(1)}, f32[32,8,1024]{2,1,0:T(8,128)}, u32[]{:S(2)}) %copy-start.1) | copy-done | bytes 1048600
  8.8 2.9 %inner_row_sums.1 = (f32[96,1024]{1,0:T(8,128)S(1)}, f32[96,1024]{1,0:T(8,128)S(1)}, f32[6,3,128]{2,1,0:T(4,128)S(1)}, f32[8,128]{1,0:T(8,128)S(1)}) custom-call(s32[8,32]{1,0:T(8,128)S(1)} %bitcast.6, f32[2,256,1024]{2,1,0:T(8,128)S(1)} %bitcast.3, f32[32,8,1024]{2,1,0:T(8,128)S(1)} %copy-done.1), custom_call_target="tpu_custom_call" | custom-call | flops 1 | bytes 1 | tf_op jit(solution)/shard_map/inner_row_sums/pallas_call | solution.py:550
  11.8 2.7 %last_row_sums.1 = (f32[104,640]{1,0:T(8,128)S(1)}, f32[96,384]{1,0:T(8,128)S(1)}, f32[96,1024]{1,0:T(8,128)S(1)}, f32[6,8,128]{2,1,0:T(8,128)S(1)}) custom-call(f32[6,2,128]{2,1,0:T(2,128)S(1)} %copy-done.7, f32[6,3,128]{2,1,0:T(4,128)S(1)} %get-tuple-element.70.inner_kept, f32[8,128]{1,0:T(8,128)S(1)} %get-tuple-element.71.p_column, s32[8,32]{1,0:T(8,128)S(1)} %bitcast.7, ...), custom_call_target="tpu_custom_call" | custom-call | flops 1 | bytes 1 | tf_op jit(solution)/shard_map/last_row_sums/pallas_call | solution.py:550
  15.0 2.0 %collective-permute-start.3 = (f32[64,1024]{1,0:T(8,128)S(1)}, f32[64,1024]{1,0:T(8,128)S(1)}, u32[]{:S(2)}, u32[]{:S(2)}) collective-permute-start(f32[64,1024]{1,0:T(8,128)S(1)} %get-tuple-element.75.refs_5_), channel_id=1, source_target_pairs={{1,2},{2,1},{0,3},{3,0},{5,6},{6,5},{4,7},{7,4},{9,10},{10,9},{8,1... | collective-permute-start | bytes 786440 | tf_op jit(solution)/shard_map/ppermute | solution.py:1014
  17.0 1.9 %collective-permute-start.4 = (f32[104,640]{1,0:T(8,128)S(1)}, f32[104,640]{1,0:T(8,128)S(1)}, u32[]{:S(2)}, u32[]{:S(2)}) collective-permute-start(f32[104,640]{1,0:T(8,128)S(1)} %get-tuple-element.77), channel_id=1, source_target_pairs={{0,16},{16,0},{1,17},{17,1},{2,18},{18,2},{3,19},{19,3},{4,20},{20... | collective-permute-start | bytes 798728 | tf_op jit(solution)/shard_map/ppermute | solution.py:1132
  19.0 4.8 %collective-permute-done.1.refs_3_ = f32[96,1024]{1,0:T(8,128)S(1)} collective-permute-done((f32[96,1024]{1,0:T(8,128)S(1)}, f32[96,1024]{1,0:T(8,128)S(1)}, u32[]{:S(2)}, u32[]{:S(2)}) %collective-permute-start.1) | collective-permute-done | bytes 393248 | tf_op jit(solution)/shard_map/ppermute | solution.py:1106
  23.8 0.7 %wide_field.1 = (f32[160,1024]{1,0:T(8,128)S(1)}, f32[32,1024]{1,0:T(8,128)S(1)}, f32[32,1024]{1,0:T(8,128)S(1)}, f32[32,8,1024]{2,1,0:T(8,128)S(1)}, f32[32,8,1...) custom-call(f32[64,1024]{1,0:T(8,128)S(1)} %copy-done.4, ...), custom_call_target="tpu_custom_call" | custom-call | flops 1 | bytes 1 | tf_op jit(solution)/shard_map/wide_field/pallas_call | solution.py:550
  24.5 1.7 %collective-permute-start.5 = (f32[96,384]{1,0:T(8,128)S(1)}, f32[96,384]{1,0:T(8,128)S(1)}, u32[]{:S(2)}, u32[]{:S(2)}) collective-permute-start(f32[96,384]{1,0:T(8,128)S(1)} %get-tuple-element.81), channel_id=1, source_target_pairs={{0,16},{16,0},{1,17},{17,1},{2,18},{18,2},{3,19},{19,3},{4,20},{20... | collective-permute-start | bytes 442376 | tf_op jit(solution)/shard_map/ppermute | solution.py:1145
  26.2 2.4 %collective-permute-done.4.refs_2_ = f32[104,640]{1,0:T(8,128)S(1)} collective-permute-done((f32[104,640]{1,0:T(8,128)S(1)}, f32[104,640]{1,0:T(8,128)S(1)}, u32[]{:S(2)}, u32[]{:S(2)}) %collective-permute-start.4) | collective-permute-done | bytes 266272 | tf_op jit(solution)/shard_map/ppermute | solution.py:1132
  28.6 0.5 first_field.1
  29.1 0.9 %first_sweep.2 = (f32[32,8,512]{2,1,0:T(8,128)S(1)}, f32[32,8,512]{2,1,0:T(8,128)S(1)}, f32[8,128]{1,0:T(8,128)S(1)}, f32[32,8,512]{2,1,0:T(8,128)S(1)}, f32[32,...) custom-call(f32[32,8,640]{2,1,0:T(8,128)S(1)} %get-tuple-element.82.refs_0, ...), custom_call_target="tpu_custom_call" | custom-call | flops 1 | bytes 1 | tf_op jit(solution)/shard_map/first_sweep/pallas_call | solution.py:550
  30.1 2.1 %collective-permute-start.6 = (f32[5,8,512]{2,1,0:T(8,128)S(1)}, f32[5,8,512]{2,1,0:T(8,128)S(1)}, u32[]{:S(2)}, u32[]{:S(2)}) collective-permute-start(f32[5,8,512]{2,1,0:T(8,128)S(1)} %get-tuple-element.94.refs_0_), channel_id=1, source_target_pairs={{0,4},{4,0},{8,12},{12,8},{1,5},{5,1},{9,13},{13,9},{2,6},{6,2},{1... | collective-permute-start | bytes 245768 | tf_op jit(solution)/shard_map/ppermute | solution.py:1169
  32.2 0.3 second_field.1
  32.5 0.9 %first_sweep.3 = (f32[32,8,512]{2,1,0:T(8,128)S(1)}, f32[32,8,512]{2,1,0:T(8,128)S(1)}, f32[8,128]{1,0:T(8,128)S(1)}, f32[32,8,512]{2,1,0:T(8,128)S(1)}, f32[32,...) custom-call(f32[32,8,512]{2,1,0:T(8,128)S(1)} %get-tuple-element.97.refs_0, ...), custom_call_target="tpu_custom_call" | custom-call | flops 1 | bytes 1 | tf_op jit(solution)/shard_map/first_sweep/pallas_call | solution.py:550
  33.5 1.0 %collective-permute-start.8 = (f32[5,8,512]{2,1,0:T(8,128)S(1)}, f32[5,8,512]{2,1,0:T(8,128)S(1)}, u32[]{:S(2)}, u32[]{:S(2)}) collective-permute-start(f32[5,8,512]{2,1,0:T(8,128)S(1)} %get-tuple-element.98.refs_2_.refs_0_), channel_id=1, source_target_pairs={{0,4},{4,0},{8,12},{12,8},{1,5},{5,1},{9,13},{13,9},{2,6},{6,2},{1... | collective-permute-start | bytes 245768 | tf_op jit(solution)/shard_map/ppermute | solution.py:1180
  34.6 3.2 %collective-permute-start.7 = (f32[2,8,512]{2,1,0:T(8,128)S(1)}, f32[2,8,512]{2,1,0:T(8,128)S(1)}, u32[]{:S(2)}, u32[]{:S(2)}) collective-permute-start(f32[2,8,512]{2,1,0:T(8,128)S(1)} %get-tuple-element.99.refs_0_), channel_id=1, source_target_pairs={{0,8},{8,0},{4,12},{12,4},{1,9},{9,1},{5,13},{13,5},{2,10},{10,2},... | collective-permute-start | bytes 98312 | tf_op jit(solution)/shard_map/ppermute | solution.py:1196
  37.8 0.5 collective-permute-done.8.refs_1_
  38.3 2.3 %collective-permute-start.9 = (f32[2,8,512]{2,1,0:T(8,128)S(1)}, f32[2,8,512]{2,1,0:T(8,128)S(1)}, u32[]{:S(2)}, u32[]{:S(2)}) collective-permute-start(f32[2,8,512]{2,1,0:T(8,128)S(1)} %get-tuple-element.101.refs_3_), channel_id=1, source_target_pairs={{0,8},{8,0},{4,12},{12,4},{1,9},{9,1},{5,13},{13,5},{2,10},{10,2},... | collective-permute-start | bytes 98312 | tf_op jit(solution)/shard_map/ppermute | solution.py:1196
  40.7 2.6 %collective-permute-done.9.refs_4_ = f32[2,8,512]{2,1,0:T(8,128)S(1)} collective-permute-done((f32[2,8,512]{2,1,0:T(8,128)S(1)}, f32[2,8,512]{2,1,0:T(8,128)S(1)}, u32[]{:S(2)}, u32[]{:S(2)}) %collective-permute-start.9) | collective-permute-done | bytes 32800 | tf_op jit(solution)/shard_map/ppermute | solution.py:1196
  43.2 0.5 half.1
  43.8 1.6 %collective-permute-start.11 = (f32[32,1024]{1,0:T(8,128)S(1)}, f32[32,1024]{1,0:T(8,128)S(1)}, u32[]{:S(2)}, u32[]{:S(2)}) collective-permute-start(f32[32,1024]{1,0:T(8,128)S(1)} %get-tuple-element.113), channel_id=1, source_target_pairs={{1,2},{2,1},{0,3},{3,0},{5,6},{6,5},{4,7},{7,4},{9,10},{10,9},{8,1... | collective-permute-start | bytes 393224 | tf_op jit(solution)/shard_map/ppermute | solution.py:1014
  45.4 1.3 %collective-permute-start.12 = (f32[8,128]{1,0:T(8,128)S(1)}, f32[8,128]{1,0:T(8,128)S(1)}, u32[]{:S(2)}, u32[]{:S(2)}) collective-permute-start(f32[8,128]{1,0:T(8,128)S(1)} %get-tuple-element.114), channel_id=1, source_target_pairs={{0,16},{16,0},{1,17},{17,1},{2,18},{18,2},{3,19},{19,3},{4,20},{20... | collective-permute-start | bytes 12296 | tf_op jit(solution)/shard_map/ppermute | solution.py:1015
  46.7 2.3 %collective-permute-done.12.refs_3_ = f32[8,128]{1,0:T(8,128)S(1)} collective-permute-done((f32[8,128]{1,0:T(8,128)S(1)}, f32[8,128]{1,0:T(8,128)S(1)}, u32[]{:S(2)}, u32[]{:S(2)}) %collective-permute-start.12) | collective-permute-done | bytes 4128 | tf_op jit(solution)/shard_map/ppermute | solution.py:1015
  49.1 1.0 %second_sweep.1 = (f32[32,8,512]{2,1,0:T(8,128)S(1)}, f32[32,8,512]{2,1,0:T(8,128)S(1)}, f32[2,8,1024]{2,1,0:T(8,128)S(1)}, f32[8,1024]{1,0:T(8,128)S(1)}) custom-call(f32[32,8,1024]{2,1,0:T(8,128)S(1)} %get-tuple-element.111.refs_0_.refs_15_, f32[32,1024]{1,0:T(8,128)S(1)} %collective-permute-done.10.refs_1_, ...), custom_call_target="tpu_custom_call" | custom-call | flops 1 | bytes 1 | tf_op jit(solution)/shard_map/second_sweep/pallas_call | solution.py:550
  50.1 1.1 %collective-permute-start.13 = (f32[2,8,1024]{2,1,0:T(8,128)S(1)}, f32[2,8,1024]{2,1,0:T(8,128)S(1)}, u32[]{:S(2)}, u32[]{:S(2)}) collective-permute-start(f32[2,8,1024]{2,1,0:T(8,128)S(1)} %get-tuple-element.121.refs_0_), channel_id=1, source_target_pairs={{0,4},{4,0},{8,12},{12,8},{1,5},{5,1},{9,13},{13,9},{2,6},{6,2},{1... | collective-permute-start | bytes 196616 | tf_op jit(solution)/shard_map/ppermute | solution.py:1218
  51.3 2.6 %collective-permute-start.15 = (f32[8,1024]{1,0:T(8,128)S(1)}, f32[8,1024]{1,0:T(8,128)S(1)}, u32[]{:S(2)}, u32[]{:S(2)}) collective-permute-start(f32[8,1024]{1,0:T(8,128)S(1)} %get-tuple-element.122), channel_id=1, source_target_pairs={{0,12},{12,0},{4,8},{8,4},{1,13},{13,1},{5,9},{9,5},{2,14},{14,2},... | collective-permute-start | bytes 98312 | tf_op jit(solution)/shard_map/ppermute | solution.py:1218
  53.9 1.1 %log_perm.1 = f32[32,8,1024]{2,1,0:T(8,128)} custom-call(f32[32,8,640]{2,1,0:T(8,128)S(1)} %get-tuple-element.79.refs_0_, f32[32,8,384]{2,1,0:T(8,128)S(1)} %get-tuple-element.96.refs_1_, f32[5,8,512]{2,1,0:T(8,128)S(1)} %get-tuple-element.98.refs_2_.refs_0_), custom_call_target="tpu_custom_call" | custom-call | flops 1 | bytes 1 | tf_op jit(solution)/shard_map/log_perm/pallas_call | solution.py:550
  55.0 2.2 %collective-permute-done.15.refs_3_ = f32[8,1024]{1,0:T(8,128)S(1)} collective-permute-done((f32[8,1024]{1,0:T(8,128)S(1)}, f32[8,1024]{1,0:T(8,128)S(1)}, u32[]{:S(2)}, u32[]{:S(2)}) %collective-permute-start.15) | collective-permute-done | bytes 32800 | tf_op jit(solution)/shard_map/ppermute | solution.py:1218
  57.2 1.5 %collective-permute-done.14.refs_2_ = f32[8,1024]{1,0:T(8,128)S(1)} collective-permute-done((f32[8,1024]{1,0:T(8,128)S(1)}, f32[8,1024]{1,0:T(8,128)S(1)}, u32[]{:S(2)}, u32[]{:S(2)}) %collective-permute-start.14) | collective-permute-done | bytes 32800 | tf_op jit(solution)/shard_map/ppermute | solution.py:1218
  58.7 1.1 %smoothed.1 = f32[32,8,1024]{2,1,0:T(8,128)} custom-call(f32[2,8,1024]{2,1,0:T(8,128)S(1)} %get-tuple-element.121.refs_0_, f32[2,8,1024]{2,1,0:T(8,128)S(1)} %collective-permute-done.13.refs_1_, f32[8,1024]{1,0:T(8,128)S(1)} %collective-permute-done.14.refs_2_, f32[8,1024]{1,0:T(8,128)S(1)} %collective-permute-done.15.refs_3_, ...), custom_call_target="tpu_custom_call" | custom-call | flops 1 | bytes 1 | tf_op jit(solution)/shard_map/smoothed/pallas_call | solution.py:550
  (31 shorter events, 0.9 us)
Async XLA Ops:
  0.6 6.9 %copy-start.6 = (s32[32,8]{0,1:T(8,128)S(1)}, s32[32,8]{0,1:T(8,128)}, u32[]{:S(2)}) copy-start(s32[32,8]{0,1:T(8,128)} %param.6) | copy-start | bytes 3076
  0.6 6.9 %copy-start = (f32[2,32,8,1024]{3,2,1,0:T(8,128)S(1)}, f32[2,32,8,1024]{3,2,1,0:T(8,128)}, u32[]{:S(2)}) copy-start(f32[2,32,8,1024]{3,2,1,0:T(8,128)} %param.5) | copy-start | bytes 6291460
  4.5 10.1 %collective-permute-start = (f32[64,1024]{1,0:T(8,128)}, f32[64,1024]{1,0:T(8,128)S(1)}, u32[]{:S(2)}, u32[]{:S(2)}) collective-permute-start(f32[64,1024]{1,0:T(8,128)} %get-tuple-element.65), channel_id=1, source_target_pairs={{0,16},{16,0},{1,17},{17,1},{2,18},{18,2},{3,19},{19,3},{4,20},{20... | collective-permute-start | bytes 786440 | tf_op jit(solution)/shard_map/ppermute | solution.py:1094
  7.6 1.2 %copy-start.1 = (f32[32,8,1024]{2,1,0:T(8,128)S(1)}, f32[32,8,1024]{2,1,0:T(8,128)}, u32[]{:S(2)}) copy-start(f32[32,8,1024]{2,1,0:T(8,128)} %refs_14_.1) | copy-start | bytes 3145732
  8.8 3.0 %copy-start.7 = (f32[6,2,128]{2,1,0:T(2,128)S(1)}, f32[6,2,128]{2,1,0:T(2,128)}, u32[]{:S(2)}) copy-start(f32[6,2,128]{2,1,0:T(2,128)} %get-tuple-element.69.outer_kept) | copy-start | bytes 18436
  8.8 5.8 %copy-start.2 = (f32[32,8,1024]{2,1,0:T(8,128)S(1)}, f32[32,8,1024]{2,1,0:T(8,128)}, u32[]{:S(2)}) copy-start(f32[32,8,1024]{2,1,0:T(8,128)} %refs_14_.1) | copy-start | bytes 3145732
  8.8 5.8 %copy-start.4 = (f32[64,1024]{1,0:T(8,128)S(1)}, f32[64,1024]{1,0:T(8,128)}, u32[]{:S(2)}) copy-start(f32[64,1024]{1,0:T(8,128)} %get-tuple-element.64.refs_0_) | copy-start | bytes 786436
  11.7 12.1 %collective-permute-start.1 = (f32[96,1024]{1,0:T(8,128)S(1)}, f32[96,1024]{1,0:T(8,128)S(1)}, u32[]{:S(2)}, u32[]{:S(2)}) collective-permute-start(f32[96,1024]{1,0:T(8,128)S(1)} %get-tuple-element.68), channel_id=1, source_target_pairs={{0,16},{16,0},{1,17},{17,1},{2,18},{18,2},{3,19},{19,3},{4,20},{20... | collective-permute-start | bytes 1179656 | tf_op jit(solution)/shard_map/ppermute | solution.py:1106
  14.9 8.9 %collective-permute-start.2 = (f32[64,1024]{1,0:T(8,128)S(1)}, f32[64,1024]{1,0:T(8,128)S(1)}, u32[]{:S(2)}, u32[]{:S(2)}) collective-permute-start(f32[64,1024]{1,0:T(8,128)S(1)} %get-tuple-element.74.refs_4_), channel_id=1, source_target_pairs={{0,1},{1,0},{2,3},{3,2},{4,5},{5,4},{6,7},{7,6},{8,9},{9,8},{10,11... | collective-permute-start | bytes 786440 | tf_op jit(solution)/shard_map/ppermute | solution.py:1013
  15.0 8.8 %collective-permute-start.3 = (f32[64,1024]{1,0:T(8,128)S(1)}, f32[64,1024]{1,0:T(8,128)S(1)}, u32[]{:S(2)}, u32[]{:S(2)}) collective-permute-start(f32[64,1024]{1,0:T(8,128)S(1)} %get-tuple-element.75.refs_5_), channel_id=1, source_target_pairs={{1,2},{2,1},{0,3},{3,0},{5,6},{6,5},{4,7},{7,4},{9,10},{10,9},{8,1... | collective-permute-start | bytes 786440 | tf_op jit(solution)/shard_map/ppermute | solution.py:1014
  17.0 11.6 %collective-permute-start.4 = (f32[104,640]{1,0:T(8,128)S(1)}, f32[104,640]{1,0:T(8,128)S(1)}, u32[]{:S(2)}, u32[]{:S(2)}) collective-permute-start(f32[104,640]{1,0:T(8,128)S(1)} %get-tuple-element.77), channel_id=1, source_target_pairs={{0,16},{16,0},{1,17},{17,1},{2,18},{18,2},{3,19},{19,3},{4,20},{20... | collective-permute-start | bytes 798728 | tf_op jit(solution)/shard_map/ppermute | solution.py:1132
  23.8 5.3 %copy-start.3 = (f32[32,8,1024]{2,1,0:T(8,128)S(1)}, f32[32,8,1024]{2,1,0:T(8,128)}, u32[]{:S(2)}) copy-start(f32[32,8,1024]{2,1,0:T(8,128)} %refs_4_.1) | copy-start | bytes 3145732
  24.5 7.7 %collective-permute-start.5 = (f32[96,384]{1,0:T(8,128)S(1)}, f32[96,384]{1,0:T(8,128)S(1)}, u32[]{:S(2)}, u32[]{:S(2)}) collective-permute-start(f32[96,384]{1,0:T(8,128)S(1)} %get-tuple-element.81), channel_id=1, source_target_pairs={{0,16},{16,0},{1,17},{17,1},{2,18},{18,2},{3,19},{19,3},{4,20},{20... | collective-permute-start | bytes 442376 | tf_op jit(solution)/shard_map/ppermute | solution.py:1145
  30.1 4.5 %collective-permute-start.6 = (f32[5,8,512]{2,1,0:T(8,128)S(1)}, f32[5,8,512]{2,1,0:T(8,128)S(1)}, u32[]{:S(2)}, u32[]{:S(2)}) collective-permute-start(f32[5,8,512]{2,1,0:T(8,128)S(1)} %get-tuple-element.94.refs_0_), channel_id=1, source_target_pairs={{0,4},{4,0},{8,12},{12,8},{1,5},{5,1},{9,13},{13,9},{2,6},{6,2},{1... | collective-permute-start | bytes 245768 | tf_op jit(solution)/shard_map/ppermute | solution.py:1169
  32.5 10.7 %copy-start.5 = (s32[8,1024]{1,0:T(8,128)S(1)}, s32[8,1024]{1,0:T(8,128)}, u32[]{:S(2)}) copy-start(s32[8,1024]{1,0:T(8,128)} %refs_16_.1) | copy-start | bytes 98308
  33.5 4.9 %collective-permute-start.8 = (f32[5,8,512]{2,1,0:T(8,128)S(1)}, f32[5,8,512]{2,1,0:T(8,128)S(1)}, u32[]{:S(2)}, u32[]{:S(2)}) collective-permute-start(f32[5,8,512]{2,1,0:T(8,128)S(1)} %get-tuple-element.98.refs_2_.refs_0_), channel_id=1, source_target_pairs={{0,4},{4,0},{8,12},{12,8},{1,5},{5,1},{9,13},{13,9},{2,6},{6,2},{1... | collective-permute-start | bytes 245768 | tf_op jit(solution)/shard_map/ppermute | solution.py:1180
  34.6 6.0 %collective-permute-start.7 = (f32[2,8,512]{2,1,0:T(8,128)S(1)}, f32[2,8,512]{2,1,0:T(8,128)S(1)}, u32[]{:S(2)}, u32[]{:S(2)}) collective-permute-start(f32[2,8,512]{2,1,0:T(8,128)S(1)} %get-tuple-element.99.refs_0_), channel_id=1, source_target_pairs={{0,8},{8,0},{4,12},{12,4},{1,9},{9,1},{5,13},{13,5},{2,10},{10,2},... | collective-permute-start | bytes 98312 | tf_op jit(solution)/shard_map/ppermute | solution.py:1196
  38.3 4.9 %collective-permute-start.9 = (f32[2,8,512]{2,1,0:T(8,128)S(1)}, f32[2,8,512]{2,1,0:T(8,128)S(1)}, u32[]{:S(2)}, u32[]{:S(2)}) collective-permute-start(f32[2,8,512]{2,1,0:T(8,128)S(1)} %get-tuple-element.101.refs_3_), channel_id=1, source_target_pairs={{0,8},{8,0},{4,12},{12,4},{1,9},{9,1},{5,13},{13,5},{2,10},{10,2},... | collective-permute-start | bytes 98312 | tf_op jit(solution)/shard_map/ppermute | solution.py:1196
  43.8 5.3 %collective-permute-start.10 = (f32[32,1024]{1,0:T(8,128)S(1)}, f32[32,1024]{1,0:T(8,128)S(1)}, u32[]{:S(2)}, u32[]{:S(2)}) collective-permute-start(f32[32,1024]{1,0:T(8,128)S(1)} %get-tuple-element.112), channel_id=1, source_target_pairs={{0,1},{1,0},{2,3},{3,2},{4,5},{5,4},{6,7},{7,6},{8,9},{9,8},{10,11... | collective-permute-start | bytes 393224 | tf_op jit(solution)/shard_map/ppermute | solution.py:1013
  43.8 5.3 %collective-permute-start.11 = (f32[32,1024]{1,0:T(8,128)S(1)}, f32[32,1024]{1,0:T(8,128)S(1)}, u32[]{:S(2)}, u32[]{:S(2)}) collective-permute-start(f32[32,1024]{1,0:T(8,128)S(1)} %get-tuple-element.113), channel_id=1, source_target_pairs={{1,2},{2,1},{0,3},{3,0},{5,6},{6,5},{4,7},{7,4},{9,10},{10,9},{8,1... | collective-permute-start | bytes 393224 | tf_op jit(solution)/shard_map/ppermute | solution.py:1014
  45.4 3.6 %collective-permute-start.12 = (f32[8,128]{1,0:T(8,128)S(1)}, f32[8,128]{1,0:T(8,128)S(1)}, u32[]{:S(2)}, u32[]{:S(2)}) collective-permute-start(f32[8,128]{1,0:T(8,128)S(1)} %get-tuple-element.114), channel_id=1, source_target_pairs={{0,16},{16,0},{1,17},{17,1},{2,18},{18,2},{3,19},{19,3},{4,20},{20... | collective-permute-start | bytes 12296 | tf_op jit(solution)/shard_map/ppermute | solution.py:1015
  50.1 8.6 %collective-permute-start.13 = (f32[2,8,1024]{2,1,0:T(8,128)S(1)}, f32[2,8,1024]{2,1,0:T(8,128)S(1)}, u32[]{:S(2)}, u32[]{:S(2)}) collective-permute-start(f32[2,8,1024]{2,1,0:T(8,128)S(1)} %get-tuple-element.121.refs_0_), channel_id=1, source_target_pairs={{0,4},{4,0},{8,12},{12,8},{1,5},{5,1},{9,13},{13,9},{2,6},{6,2},{1... | collective-permute-start | bytes 196616 | tf_op jit(solution)/shard_map/ppermute | solution.py:1218
  51.3 5.9 %collective-permute-start.15 = (f32[8,1024]{1,0:T(8,128)S(1)}, f32[8,1024]{1,0:T(8,128)S(1)}, u32[]{:S(2)}, u32[]{:S(2)}) collective-permute-start(f32[8,1024]{1,0:T(8,128)S(1)} %get-tuple-element.122), channel_id=1, source_target_pairs={{0,12},{12,0},{4,8},{8,4},{1,13},{13,1},{5,9},{9,5},{2,14},{14,2},... | collective-permute-start | bytes 98312 | tf_op jit(solution)/shard_map/ppermute | solution.py:1218
  53.9 4.8 %collective-permute-start.14 = (f32[8,1024]{1,0:T(8,128)S(1)}, f32[8,1024]{1,0:T(8,128)S(1)}, u32[]{:S(2)}, u32[]{:S(2)}) collective-permute-start(f32[8,1024]{1,0:T(8,128)S(1)} %get-tuple-element.122), channel_id=1, source_target_pairs={{0,8},{8,0},{4,12},{12,4},{1,9},{9,1},{5,13},{13,5},{2,10},{10,2},... | collective-permute-start | bytes 98312 | tf_op jit(solution)/shard_map/ppermute | solution.py:1218
